TPU v7x, 512 devices: a whole 4x4x16 slice. The times are simulated.
512 devices in a mesh: dp: 64 (over y, z_hi, x), fsdp: 2 (over core), tensor: 4 (over z_lo).
Axes of the slice: x: 4, y: 4, z: 16 (z_hi: 4, z_lo: 4; z = z_hi * 4 + z_lo), core: 2. Of those that a mesh axis runs over, the one named last changes fastest.
Arguments:
- x_heads: bfloat16 [32768, 2560], P(('dp', 'fsdp'), 'tensor'), may hold values from -24 to 24
- proj_weight: bfloat16 [2560, 2560], P('tensor', 'fsdp'), may hold values from -0.125 to 0.125
- out_grad: bfloat16 [32768, 2560], P(('dp', 'fsdp', 'tensor')), may hold values from -6 to 6
- proj_basis: bfloat16 [2560, 512], P('dp'), may hold values from -0.125 to 0.125
- first_moment: float32 [4, 640, 512], P('tensor', 'dp'), as said below
- second_moment: float32 [4, 640, 512], P('tensor', 'dp'), may hold values from 32 to 328, as said below
Outputs:
- mixed_out: bfloat16 [32768, 2560], P(('dp', 'fsdp', 'tensor'))
- head_grad: bfloat16 [32768, 2560], P(('dp', 'fsdp'), 'tensor')
- update: bfloat16 [2560, 2560], P('tensor', 'fsdp')
Inputs may be any that keep to these rules, and one draw needn't show every extreme that they name: `first_moment`: entries within plus or minus 0.4 times the square root of 32768. `second_moment`: positive, between 32768 / 1000 and 32768 / 100.
All inputs are finite; a program needn't handle non-finite values.
Results may differ from a plain program's by a relative error of at most 0.0056.
Values may be sent and summed in bfloat16 or wider, within the bound.
No kernel may reach another device: no remote copies, remote signals or barrier semaphores. Data moves between devices by JAX's collectives and lax.ppermute only.
A program may use at most 64 MiB of HBM per device.

v0:
```python
import jax
import jax.numpy as jnp
from jax import lax
from jax.sharding import PartitionSpec as P

ADAM_STEP = 10


def core_sum(values):
    return lax.psum(values, "fsdp")


def owner_sum(values):
    return lax.psum_scatter(values, "dp", scatter_dimension=0, tiled=True)


def shards(x_heads, proj_weight, out_grad, proj_basis, first_moment, second_moment):
    weight_full = lax.all_gather(proj_weight, "fsdp", axis=1, tiled=True)
    rows_in = x_heads
    mixed_out = lax.psum_scatter(
        jnp.dot(rows_in, weight_full, preferred_element_type=jnp.float32),
        "tensor",
        scatter_dimension=0,
        tiled=True,
    ).astype(jnp.bfloat16)
    basis_full = lax.all_gather(proj_basis, "dp", axis=0, tiled=True)
    grad_block = lax.all_gather(out_grad, "tensor", axis=0, tiled=True)
    head_rows = lax.dot_general(
        grad_block, weight_full, (((1,), (1,)), ((), ())), preferred_element_type=jnp.float32
    ).astype(jnp.bfloat16)
    reduced = jnp.dot(grad_block, basis_full, preferred_element_type=jnp.float32).astype(
        jnp.bfloat16
    )
    rows_in = x_heads
    low_acc = lax.dot_general(
        rows_in, reduced, (((0,), (0,)), ((), ())), preferred_element_type=jnp.float32
    )
    owned = owner_sum(core_sum(low_acc))
    m_new = 0.9 * first_moment[0] + 0.1 * owned
    v_new = 0.999 * second_moment[0] + 0.001 * owned * owned
    corr_one = 1.0 - 0.9**ADAM_STEP
    corr_two = 1.0 - 0.999**ADAM_STEP
    direction = (m_new / corr_one / (jnp.sqrt(v_new / corr_two) + 1e-08)).astype(jnp.bfloat16)
    half_cols = proj_weight.shape[1]
    basis_half = lax.dynamic_slice_in_dim(
        basis_full, lax.axis_index("fsdp") * half_cols, half_cols, 0
    )
    own_update = lax.dot_general(
        direction, basis_half, (((1,), (1,)), ((), ())), preferred_element_type=jnp.float32
    ).astype(jnp.bfloat16)
    update = lax.all_gather(own_update, "dp", axis=0, tiled=True)
    return (mixed_out, head_rows, update)


def solution(mesh):
    return jax.shard_map(
        shards,
        mesh=mesh,
        in_specs=(
            P(("dp", "fsdp"), "tensor"),
            P("tensor", "fsdp"),
            P(("dp", "fsdp", "tensor"), None),
            P("dp", None),
            P("tensor", "dp", None),
            P("tensor", "dp", None),
        ),
        out_specs=(
            P(("dp", "fsdp", "tensor"), None),
            P(("dp", "fsdp"), "tensor"),
            P("tensor", "fsdp"),
        ),
        check_vma=False,
    )
```

profile of v0, /device:TPU:1, one launch (start us, length us, event | category | flops | bytes accessed | tf_op | source)
XLA Modules:
  0.0 1227.5 jit_solution(17186253349428420610)
XLA Ops:
  7.2 0.0 copy-start
  7.2 0.0 all-gather.8.cloned.1.call-start
  7.2 0.7 all-gather.8.cloned.1.call-update
  7.9 0.0 all-gather.10.cloned.1.call-start
  8.0 0.7 all-gather.10.cloned.1.call-update
  8.7 0.0 all-gather.6.cloned.1.call-start
  8.7 0.7 all-gather.6.cloned.1.call-update
  9.4 0.0 all-reduce.3.cloned.1.call-start
  9.4 48.5 %all-gather.8.cloned.1.call-done = bf16[256,2560]{1,0:T(8,128)(2,1)} async-done(((bf16[64,2560]{1,0:T(8,128)(2,1)}), bf16[256,2560]{1,0:T(8,128)(2,1)}) %all-gather.8.cloned.1.call-update) | async-done | bytes 1310736 | tf_op jit(solution)/shard_map/all_gather | solution.py:27
  58.0 123.3 %all-gather.10.cloned.1.call-done = bf16[2560,512]{1,0:T(8,128)(2,1)} async-done(((bf16[40,512]{1,0:T(8,128)(2,1)}), bf16[2560,512]{1,0:T(8,128)(2,1)}) %all-gather.10.cloned.1.call-update) | async-done | bytes 2621456 | tf_op jit(solution)/shard_map/all_gather | solution.py:26
  181.3 4.5 convolution_bitcast_fusion
  185.8 0.0 all-reduce.3.cloned.1.call-update
  185.8 0.0 reduce-scatter.3.cloned.1.call-start
  185.9 15.5 %all-gather.6.cloned.1.call-done = bf16[640,2560]{1,0:T(8,128)(2,1)} async-done(((bf16[640,1280]{1,0:T(8,128)(2,1)}), bf16[640,2560]{1,0:T(8,128)(2,1)}) %all-gather.6.cloned.1.call-update) | async-done | bytes 3276816 | tf_op jit(solution)/shard_map/all_gather | solution.py:18
  201.4 4.6 fusion.25
  206.0 0.0 reduce-scatter.3.cloned.1.call-update
  206.1 0.0 all-gather.12.cloned.1.call-start
  206.1 1.4 dynamic-slice
  208.2 786.8 %all-reduce.3.cloned.1.call-done = f32[640,512]{0,1:T(8,128)} async-done(((f32[640,512]{0,1:T(8,128)}), f32[640,512]{0,1:T(8,128)}) %all-reduce.3.cloned.1.call-update) | async-done | bytes 1310736
  995.0 1.2 constant_dynamic-slice_fusion
  996.2 0.1 copy.16
  996.3 44.1 %psum.8 = f32[10,512]{1,0:T(8,128)S(1)} all-reduce(f32[10,512]{1,0:T(8,128)S(1)} %copy.16), channel_id=1, replica_groups=mesh['dp'=64,'fsdp'=2,'tensor'=4] {'fsdp'}, use_global_device_ids=true, to_apply=%region_1.0 | all-reduce | flops 5120 | bytes 40960 | tf_op jit(solution)/shard_map/psum | solution.py:10
  1040.4 0.0 copy-done.1
  1040.5 0.0 copy-done.2
  1040.5 0.0 copy-done.3
  1040.5 1.1 fusion
  1041.6 0.0 all-gather.12.cloned.1.call-update
  1041.6 4.3 convolution_convert_fusion.1
  1045.8 45.8 %reduce-scatter.3.cloned.1.call-done = f32[64,2560]{1,0:T(8,128)} async-done(((f32[256,2560]{1,0:T(8,128)}), f32[64,2560]{1,0:T(8,128)}) %reduce-scatter.3.cloned.1.call-update) | async-done | bytes 655376 | tf_op jit(solution)/shard_map/reduce_scatter | solution.py:20
  1091.6 1.8 convert_element_type.15
  1093.5 123.2 %all-gather.12.cloned.1.call-done = bf16[64,10,1280]{2,1,0:T(8,128)(2,1)} async-done(((bf16[1,10,1280]{2,1,0:T(8,128)(2,1)}), bf16[64,10,1280]{2,1,0:T(8,128)(2,1)}) %all-gather.12.cloned.1.call-update) | async-done | bytes 1638416 | tf_op jit(solution)/shard_map/all_gather | solution.py:51
  1216.7 4.0 reshape.11
  (4 shorter events, 0.0 us)
Async XLA Ops:
  7.2 174.1 %copy-start = (bf16[256,640]{1,0:T(8,128)(2,1)S(1)}, bf16[256,640]{1,0:T(8,128)(2,1)}, u32[]{:S(2)}) copy-start(bf16[256,640]{1,0:T(8,128)(2,1)} %param.6) | copy-start | bytes 983044
  7.2 50.8 %all-gather.8.cloned.1.call-start = ((), (), s32[]{:S(2)}) async-start(), calls=%async_computation.3 | async-start | bytes 1638400 | tf_op jit(solution)/shard_map/all_gather | solution.py:27
  7.9 173.4 %all-gather.10.cloned.1.call-start = ((), (), s32[]{:S(2)}) async-start(), calls=%async_computation.4 | async-start | bytes 2662400 | tf_op jit(solution)/shard_map/all_gather | solution.py:26
  8.7 192.7 %all-gather.6.cloned.1.call-start = ((), (), s32[]{:S(2)}) async-start(), calls=%async_computation.1 | async-start | bytes 4915200 | tf_op jit(solution)/shard_map/all_gather | solution.py:18
  9.4 985.6 %all-reduce.3.cloned.1.call-start = ((), (), s32[]{:S(2)}) async-start(), calls=%async_computation.6 | async-start | bytes 2621440
  185.8 905.8 %reduce-scatter.3.cloned.1.call-start = ((), (), s32[]{:S(2)}) async-start(), calls=%async_computation.2 | async-start | bytes 3276800 | tf_op jit(solution)/shard_map/reduce_scatter | solution.py:20
  206.0 834.4 %copy-start.1 = (bf16[2560,512]{1,0:T(8,128)(2,1)S(1)}, bf16[2560,512]{1,0:T(8,128)(2,1)}, u32[]{:S(2)}) copy-start(bf16[2560,512]{1,0:T(8,128)(2,1)} %all-gather.10.cloned.1.call-done) | copy-start | bytes 7864324
  206.0 834.4 %copy-start.2 = (f32[1,10,512]{2,0,1:T(1,128)S(1)}, f32[1,10,512]{2,0,1:T(1,128)}, u32[]{:S(2)}) copy-start(f32[1,10,512]{2,0,1:T(1,128)} %param.11) | copy-start | bytes 61444
  206.0 834.4 %copy-start.3 = (f32[1,10,512]{2,0,1:T(1,128)S(1)}, f32[1,10,512]{2,0,1:T(1,128)}, u32[]{:S(2)}) copy-start(f32[1,10,512]{2,0,1:T(1,128)} %param.10) | copy-start | bytes 61444
  206.1 1010.6 %all-gather.12.cloned.1.call-start = ((), (), s32[]{:S(2)}) async-start(), calls=%async_computation.5 | async-start | bytes 2662400 | tf_op jit(solution)/shard_map/all_gather | solution.py:51
Sparse Core Ops, SparseCore 0:
  10.1 47.8 all-gather.7
  62.1 119.1 all-gather.9
  183.4 17.9 all-gather.5
  204.7 790.2 all-reduce.2
  998.0 93.6 reduce-scatter.2
  1097.0 119.6 all-gather.11
where the time goes:
time: 1230 us
  waiting for transfers between devices  1150 us (93%)
  blocking collectives  44.1 us (4%)
  between operations  14.8 us (1%)
  matrix products  14.5 us (1%)
    unnamed x7, waiting for transfers between devices  789 us
    all_gather x1, waiting for transfers between devices, shards(): basis_full = lax.all_gather(proj_basis, 'dp', axis=0, tiled=True)  123 us
    all_gather x1, waiting for transfers between devices, shards(): update = lax.all_gather(own_update, 'dp', axis=0, tiled=True)  123 us
    all_gather x1, waiting for transfers between devices, shards(): grad_block = lax.all_gather(out_grad, 'tensor', axis=0, tiled=True)  48.5 us
    reduce_scatter x1, waiting for transfers between devices, shards(): lax.psum_scatter(jnp.dot(rows_in, weight_full, preferred_element_type=jnp...  45.8 us
    psum x1, blocking collectives, core_sum(): return lax.psum(values, 'fsdp')  44.1 us
  transfers between devices with their start and end apart: 6, of which 6 were waited for; matrix products, arithmetic and copies ran while one was open for 2% of the time, Pallas kernels for 0%

commit v1 on v0

v1 whole, which is shorter than its diff:
```python
import jax
import jax.numpy as jnp
from jax import lax
from jax.sharding import Mesh, PartitionSpec as P

ADAM_STEP = 10
BF16 = jnp.bfloat16
F32 = jnp.float32
AXES = ("y", "zh", "x", "core", "zl")
SIZES = (4, 4, 4, 2, 4)
CORE_SWAP = [(0, 1), (1, 0)]
PAIR = [(0, 1), (1, 0), (2, 3), (3, 2)]
MIRROR = [(0, 3), (3, 0), (1, 2), (2, 1)]
TURN = [(a * 4 + b, b * 4 + a) for a in range(4) for b in range(4)]


def spread(values, axes, count):
    copies = jnp.broadcast_to(values[None], (count,) + values.shape)
    return lax.all_to_all(copies, axes, 0, 0, tiled=True)


def gather_zh(values, beside):
    zh = lax.axis_index("zh")
    got = lax.ppermute(values, "zh", PAIR)
    odd = zh % 2 == 1
    pair = jnp.concatenate([jnp.where(odd, got, values), jnp.where(odd, values, got)], 0)
    got = lax.ppermute(pair, "zh", MIRROR)
    got, beside = lax.optimization_barrier((got, beside))
    high = zh >= 2
    both = jnp.stack([jnp.where(high, got, pair), jnp.where(high, pair, got)])
    return both.reshape(4, *values.shape), beside


def sum_zh(values, beside):
    sent = values.astype(BF16)
    got = lax.ppermute(sent, "zh", PAIR)
    got, beside = lax.optimization_barrier((got, beside))
    sent = (sent.astype(F32) + got.astype(F32)).astype(BF16)
    got = lax.ppermute(sent, "zh", MIRROR)
    return sent.astype(F32) + got.astype(F32), beside


def shards(x_heads, proj_weight, out_grad, proj_basis, first_moment, second_moment):
    core = lax.axis_index("core")
    zl = lax.axis_index("zl")
    half = proj_weight.shape[1]

    grad_block = lax.all_gather(out_grad, "zl", axis=0, tiled=True)

    def own_columns(moment):
        cols = lax.dynamic_slice_in_dim(moment[0], core * 256, 256, 1).astype(BF16)
        return [cols[:, :128], cols[:, 128:]]

    moments = jnp.concatenate(own_columns(first_moment) + own_columns(second_moment), 0)
    moments = lax.ppermute(moments, ("zh", "x"), TURN)

    weight_other = lax.ppermute(proj_weight, "core", CORE_SWAP)
    weight_full = jnp.zeros((proj_weight.shape[0], 2 * half), BF16)
    weight_full = lax.dynamic_update_slice(weight_full, proj_weight, (0, core * half))
    weight_full = lax.dynamic_update_slice(weight_full, weight_other, (0, (1 - core) * half))

    mixed_part = jnp.dot(x_heads, weight_full, preferred_element_type=F32).astype(BF16)

    basis_own = lax.dynamic_slice_in_dim(proj_basis, zl * 128, 128, 1)
    by_zh, mixed_part = gather_zh(jnp.concatenate([basis_own, moments], 0), mixed_part)
    basis_zh = by_zh[:, :40]
    moment_zh = by_zh[:, 40:].reshape(4, 2, 2, 10, 128)
    m_old = moment_zh[:, 0].transpose(0, 2, 1, 3).reshape(40, 256).astype(F32)
    v_old = moment_zh[:, 1].transpose(0, 2, 1, 3).reshape(40, 256).astype(F32)
    by_yx = spread(basis_zh.reshape(160, 128), ("y", "x"), 16)
    basis_cols = (
        by_yx.reshape(4, 4, 4, 40, 128).transpose(0, 2, 1, 3, 4).reshape(2560, 128)
    )

    mixed_out = lax.psum_scatter(mixed_part, "zl", scatter_dimension=0, tiled=True)

    basis_half = lax.all_gather(
        lax.dynamic_slice_in_dim(basis_cols, core * half, half, 0), "zl", axis=0, tiled=False
    )

    reduced_part = jnp.dot(grad_block, basis_cols, preferred_element_type=F32).astype(BF16)
    reduced = spread(reduced_part, "zl", 4)

    def low_columns(which):
        cols = lax.dynamic_slice_in_dim(reduced, 2 * which, 2, 0)
        cols = cols.transpose(1, 0, 2).reshape(256, 256)
        return lax.dot_general(x_heads, cols, (((0,), (0,)), ((), ())), preferred_element_type=F32)

    low_sent = low_columns(1 - core).astype(BF16)
    low_got = lax.ppermute(low_sent, "core", CORE_SWAP)
    low_chip = (low_columns(core) + low_got.astype(F32)).astype(BF16)

    low_yx = lax.all_to_all(low_chip.reshape(16, 40, 256), ("y", "x"), 0, 0, tiled=True)
    head_rows = lax.dot_general(
        grad_block, weight_full, (((1,), (1,)), ((), ())), preferred_element_type=F32
    ).astype(BF16)
    low, head_rows = sum_zh(jnp.sum(low_yx.astype(F32), 0), head_rows)

    m_new = 0.9 * m_old + 0.1 * low
    v_new = 0.999 * v_old + 0.001 * low * low
    corr_one = 1.0 - 0.9**ADAM_STEP
    corr_two = 1.0 - 0.999**ADAM_STEP
    direction = (m_new / corr_one / (jnp.sqrt(v_new / corr_two) + 1e-08)).astype(BF16)

    rows = spread(direction, ("y", "x"), 16).reshape(640, 256)
    rows_other = lax.ppermute(rows, "core", CORE_SWAP)

    def half_update(columns, which):
        cols = lax.dynamic_slice_in_dim(basis_half, 2 * which, 2, 0)
        cols = cols.transpose(1, 0, 2).reshape(half, 256)
        return lax.dot_general(columns, cols, (((1,), (1,)), ((), ())), preferred_element_type=F32)

    update = (half_update(rows, core) + half_update(rows_other, 1 - core)).astype(BF16)
    return (mixed_out, head_rows, update)


def solution(mesh):
    fine = Mesh(mesh.devices.reshape(SIZES), AXES)
    dp = ("y", "zh", "x")
    return jax.shard_map(
        shards,
        mesh=fine,
        in_specs=(
            P(dp + ("core",), "zl"),
            P("zl", "core"),
            P(dp + ("core", "zl"), None),
            P(dp, None),
            P("zl", dp, None),
            P("zl", dp, None),
        ),
        out_specs=(
            P(dp + ("core", "zl"), None),
            P(dp + ("core",), "zl"),
            P("zl", "core"),
        ),
        check_vma=False,
    )
```

time: 1230 us -> 163 us (0.13)
  waiting for transfers between devices: 1150 us -> 35.1 us
  starting transfers between devices: 0.24 us -> 71.7 us
  blocking collectives: 44.1 us -> 15.2 us
    unnamed x7 -> x4, waiting for transfers between devices: 789 us -> 10.2 us
    all_gather x4 -> x2, waiting for transfers between devices: 311 us -> 0.04 us  [the longest x1 0.02 us: shards(): lax.all_gather(lax.dynamic_slice_in_dim(basis_cols, core * half, half, 0)...]
    ppermute x0 -> x8, starting transfers between devices: none -> 59.3 us  [the longest x1 15.1 us: gather_zh(): got = lax.ppermute(pair, 'zh', MIRROR)]
    reduce_scatter x1 -> x0, waiting for transfers between devices: 45.8 us -> none  [shards(): lax.psum_scatter(jnp.dot(rows_in, weight_full, preferred_element_type=jnp...]
    psum x1 -> x0, blocking collectives: 44.1 us -> none  [core_sum(): return lax.psum(values, 'fsdp')]
    all_to_all x0 -> x3, waiting for transfers between devices: none -> 19.8 us  [the longest x2 12.6 us: spread(): return lax.all_to_all(copies, axes, 0, 0, tiled=True)]
    all_to_all x0 -> x1, blocking collectives: none -> 15.2 us  [spread(): return lax.all_to_all(copies, axes, 0, 0, tiled=True)]
  transfers between devices with their start and end apart: 6 -> 14, of which waited for: 6 -> 7; matrix products, arithmetic and copies ran while one was open for 2% -> 16% of each run, Pallas kernels for 0% -> 0%
where the time goes in v1:
time: 163 us; the launch traced here: 162 us
  starting transfers between devices  71.7 us (44%)
  waiting for transfers between devices  35.1 us (22%)
  local copies, waits for them, and re-layouts  15.2 us (9%)
  blocking collectives  15.2 us (9%)
  between operations  14.1 us (9%)
  matrix products  10.9 us (7%)
    all_to_all x1, blocking collectives, spread(): return lax.all_to_all(copies, axes, 0, 0, tiled=True)  15.2 us
    ppermute x1, starting transfers between devices, gather_zh(): got = lax.ppermute(pair, 'zh', MIRROR)  15.1 us
    all_to_all x2, waiting for transfers between devices, spread(): return lax.all_to_all(copies, axes, 0, 0, tiled=True)  12.6 us
    ppermute x1, starting transfers between devices, gather_zh(): got = lax.ppermute(values, 'zh', PAIR)  11.2 us
    unnamed x4, waiting for transfers between devices  10.2 us
    ppermute x1, starting transfers between devices, shards(): weight_other = lax.ppermute(proj_weight, 'core', CORE_SWAP)  8.92 us
    all_to_all x2, starting transfers between devices, spread(): return lax.all_to_all(copies, axes, 0, 0, tiled=True)  8.62 us
    all_to_all x1, waiting for transfers between devices, shards(): lax.all_to_all(low_chip.reshape(16, 40, 256), ('y', 'x'), 0, 0, tiled=True)  7.25 us
  transfers between devices with their start and end apart: 14, of which 7 were waited for; matrix products, arithmetic and copies ran while one was open for 16% of the time, Pallas kernels for 0%

profile of v1, /device:TPU:1, one launch (start us, length us, event | category | flops | bytes accessed | tf_op | source)
XLA Modules:
  0.0 162.4 jit_solution(16678644846788522560)
XLA Ops:
  7.2 8.9 %collective-permute-start.3 = (bf16[640,1280]{1,0:T(8,128)(2,1)}, bf16[640,1280]{1,0:T(8,128)(2,1)}, u32[]{:S(2)}, u32[]{:S(2)}) collective-permute-start(bf16[640,1280]{1,0:T(8,128)(2,1)} %param.7), channel_id=1, source_target_pairs={{0,4},{4,0},{1,5},{5,1},{2,6},{6,2},{3,7},{7,3},{8,12},{12,8},{9,1... | collective-permute-start | bytes 4915208 | tf_op jit(solution)/shard_map/ppermute | solution.py:57
  16.2 0.7 dynamic-slice_convert_fusion
  18.4 11.2 %collective-permute-start.1 = (bf16[80,128]{1,0:T(8,128)(2,1)S(1)}, bf16[80,128]{1,0:T(8,128)(2,1)S(1)}, u32[]{:S(2)}, u32[]{:S(2)}) collective-permute-start(bf16[80,128]{1,0:T(8,128)(2,1)S(1)} %pad_maximum_fusion.2), channel_id=1, source_target_pairs={{0,32},{32,0},{64,96},{96,64},{1,33},{33,1},{65,97},{97,65},{2,34}... | collective-permute-start | bytes 61448 | tf_op jit(solution)/shard_map/ppermute | solution.py:24
  29.6 1.9 %broadcast_in_dim.10 = bf16[640,2560]{1,0:T(8,128)(2,1)} broadcast(bf16[]{:T(256)} %constant.51.clone.1), dimensions={} | broadcast | bytes 3276802 | tf_op jit(solution)/shard_map/broadcast_in_dim | solution.py:58
  31.5 1.3 constant_dynamic-update-slice_fusion.1
  32.9 15.1 %collective-permute-start.2 = (bf16[160,128]{1,0:T(8,128)(2,1)S(1)}, bf16[160,128]{1,0:T(8,128)(2,1)S(1)}, u32[]{:S(2)}, u32[]{:S(2)}) collective-permute-start(bf16[160,128]{1,0:T(8,128)(2,1)S(1)} %pad_maximum_fusion.1), channel_id=1, source_target_pairs={{0,96},{96,0},{32,64},{64,32},{1,97},{97,1},{33,65},{65,33},{2,98}... | collective-permute-start | bytes 122888 | tf_op jit(solution)/shard_map/ppermute | solution.py:27
  48.1 2.8 %constant_dynamic-update-slice_fusion = bf16[640,2560]{1,0:T(8,128)(2,1)} fusion(bf16[640,2560]{1,0:T(8,128)(2,1)} %constant_dynamic-update-slice_fusion.1, bf16[640,1280]{1,0:T(8,128)(2,1)} %collective-permute-done.3, s32[]{:T(128)S(6)} %select_n.60), kind=kLoop, calls=%fused_computation.41 | loop fusion | bytes 3276804 | tf_op jit(solution)/shard_map/dynamic_update_slice | solution.py:60
  50.8 3.2 %fusion = bf16[256,2560]{0,1:T(8,128)(2,1)S(1)} fusion(bf16[640,2560]{1,0:T(8,128)(2,1)} %constant_dynamic-update-slice_fusion, bf16[256,640]{1,0:T(8,128)(2,1)S(1)} %copy-done), kind=kOutput, calls=%fused_computation.2 | convolution fusion | flops 839516160 | bytes 4915200 | tf_op jit(solution)/shard_map/dot_general | solution.py:62
  54.2 15.2 %all_to_all.20 = bf16[16,160,128]{2,1,0:T(8,128)(2,1)S(1)} all-to-all(bf16[16,160,128]{2,1,0:T(8,128)(2,1)S(1)} %broadcast_in_dim.24), channel_id=1, replica_groups=mesh['y'=4,'zh'=4,'x'=4,'core'=2,'zl'=4] {'y','x'}, dimensions={0} | all-to-all | bytes 1310720 | tf_op jit(solution)/shard_map/all_to_all | solution.py:19
  69.5 0.7 constant_dynamic-slice_fusion.2
  70.2 1.9 %fusion.4 = bf16[256,128]{0,1:T(8,128)(2,1)S(1)} fusion(bf16[2560,128]{1,0:T(8,128)(2,1)S(1)} %bitcast.82, bf16[256,2560]{1,0:T(8,128)(2,1)} %all-gather.4.cloned.1.call-done), kind=kOutput, calls=%fused_computation.10 | convolution fusion | flops 167804928 | bytes 2031616 | tf_op jit(solution)/shard_map/dot_general | solution.py:81
  72.9 5.1 %all-to-all-start.1 = ((bf16[4,256,128]{1,2,0:T(8,128)(2,1)}), bf16[4,256,128]{1,2,0:T(8,128)(2,1)S(1)}, u32[]{:S(2)}, u32[]{:S(2)}) async-start(bf16[4,256,128]{1,2,0:T(8,128)(2,1)} %broadcast_in_dim.25), calls=%async_computation.1 | async-start | bytes 524288 | tf_op jit(solution)/shard_map/all_to_all | solution.py:19
  77.9 5.6 %all-to-all-done.1 = bf16[4,256,128]{1,2,0:T(8,128)(2,1)S(1)} async-done(((bf16[4,256,128]{1,2,0:T(8,128)(2,1)}), bf16[4,256,128]{1,2,0:T(8,128)(2,1)S(1)}, u32[]{:S(2)}, u32[]{:S(2)}) %all-to-all-start.1) | async-done | bytes 262176 | tf_op jit(solution)/shard_map/all_to_all | solution.py:19
  83.9 6.4 %collective-permute-start.4 = (bf16[640,256]{0,1:T(8,128)(2,1)S(1)}, bf16[640,256]{0,1:T(8,128)(2,1)S(1)}, u32[]{:S(2)}, u32[]{:S(2)}) collective-permute-start(bf16[640,256]{0,1:T(8,128)(2,1)S(1)} %fusion.2), channel_id=1, source_target_pairs={{0,4},{4,0},{1,5},{5,1},{2,6},{6,2},{3,7},{7,3},{8,12},{12,8},{9,1... | collective-permute-start | bytes 983048 | tf_op jit(solution)/shard_map/ppermute | solution.py:90
  90.3 1.2 collective-permute-done.4
  91.8 0.9 copy.34
  92.7 3.7 %all-to-all-start.2 = ((bf16[16,40,256]{2,1,0:T(8,128)(2,1)}), bf16[16,40,256]{2,1,0:T(8,128)(2,1)S(1)}, u32[]{:S(2)}, u32[]{:S(2)}) async-start(bf16[16,40,256]{2,1,0:T(8,128)(2,1)} %bitcast.16), calls=%async_computation.2 | async-start | bytes 655360 | tf_op jit(solution)/shard_map/all_to_all | solution.py:93
  96.4 1.6 copy.42
  98.0 7.3 %all-to-all-done.2 = bf16[16,40,256]{2,1,0:T(8,128)(2,1)S(1)} async-done(((bf16[16,40,256]{2,1,0:T(8,128)(2,1)}), bf16[16,40,256]{2,1,0:T(8,128)(2,1)S(1)}, u32[]{:S(2)}, u32[]{:S(2)}) %all-to-all-start.2) | async-done | bytes 327712 | tf_op jit(solution)/shard_map/all_to_all | solution.py:93
  105.3 4.7 %collective-permute-start.5 = (bf16[40,256]{1,0:T(8,128)(2,1)S(1)}, bf16[40,256]{1,0:T(8,128)(2,1)S(1)}, u32[]{:S(2)}, u32[]{:S(2)}) collective-permute-start(bf16[40,256]{1,0:T(8,128)(2,1)S(1)} %reduce_sum.12), channel_id=1, source_target_pairs={{0,32},{32,0},{64,96},{96,64},{1,33},{33,1},{65,97},{97,65},{2,34}... | collective-permute-start | bytes 61448 | tf_op jit(solution)/shard_map/ppermute | solution.py:36
  110.1 3.0 %fusion.3 = bf16[256,640]{0,1:T(8,128)(2,1)S(1)} fusion(bf16[640,2560]{1,0:T(8,128)(2,1)} %constant_dynamic-update-slice_fusion, bf16[256,2560]{1,0:T(8,128)(2,1)S(1)} %copy-done.2), kind=kOutput, calls=%fused_computation.8 | convolution fusion | flops 839024640 | bytes 4915200 | tf_op jit(solution)/shard_map/dot_general | solution.py:94
  113.0 0.8 collective-permute-done.5
  113.8 5.4 %collective-permute-start.6 = (bf16[40,256]{1,0:T(8,128)(2,1)S(1)}, bf16[40,256]{1,0:T(8,128)(2,1)S(1)}, u32[]{:S(2)}, u32[]{:S(2)}) collective-permute-start(bf16[40,256]{1,0:T(8,128)(2,1)S(1)} %add_convert_fusion.1), channel_id=1, source_target_pairs={{0,96},{96,0},{32,64},{64,32},{1,97},{97,1},{33,65},{65,33},{2,98}... | collective-permute-start | bytes 61448 | tf_op jit(solution)/shard_map/ppermute | solution.py:39
  119.3 2.9 %collective-permute-done.6 = bf16[40,256]{1,0:T(8,128)(2,1)S(1)} collective-permute-done((bf16[40,256]{1,0:T(8,128)(2,1)S(1)}, bf16[40,256]{1,0:T(8,128)(2,1)S(1)}, u32[]{:S(2)}, u32[]{:S(2)}) %collective-permute-start.6) | collective-permute-done | bytes 20512 | tf_op jit(solution)/shard_map/ppermute | solution.py:39
  122.3 0.7 broadcast_in_dim.26
  123.0 3.5 %all-to-all-start.3 = ((bf16[16,40,256]{2,1,0:T(8,128)(2,1)}), bf16[16,40,256]{2,1,0:T(8,128)(2,1)S(1)}, u32[]{:S(2)}, u32[]{:S(2)}) async-start(bf16[16,40,256]{2,1,0:T(8,128)(2,1)} %broadcast_in_dim.26), calls=%async_computation.3 | async-start | bytes 655360 | tf_op jit(solution)/shard_map/all_to_all | solution.py:19
  126.6 0.9 copy.41
  127.5 7.0 %all-to-all-done.3 = bf16[16,40,256]{2,1,0:T(8,128)(2,1)S(1)} async-done(((bf16[16,40,256]{2,1,0:T(8,128)(2,1)}), bf16[16,40,256]{2,1,0:T(8,128)(2,1)S(1)}, u32[]{:S(2)}, u32[]{:S(2)}) %all-to-all-start.3) | async-done | bytes 327712 | tf_op jit(solution)/shard_map/all_to_all | solution.py:19
  134.4 6.9 %collective-permute-start.7 = (bf16[640,256]{1,0:T(8,128)(2,1)S(1)}, bf16[640,256]{1,0:T(8,128)(2,1)S(1)}, u32[]{:S(2)}, u32[]{:S(2)}) collective-permute-start(bf16[640,256]{1,0:T(8,128)(2,1)S(1)} %bitcast.86), channel_id=1, source_target_pairs={{0,4},{4,0},{1,5},{5,1},{2,6},{6,2},{3,7},{7,3},{8,12},{12,8},{9,1... | collective-permute-start | bytes 983048 | tf_op jit(solution)/shard_map/ppermute | solution.py:106
  141.4 1.4 constant_dynamic-slice_fusion
  143.9 1.8 %fusion.1 = bf16[640,1280]{1,0:T(8,128)(2,1)} fusion(f32[640,1280]{1,0:T(8,128)S(1)} %fusion.16, bf16[640,256]{1,0:T(8,128)(2,1)S(1)} %collective-permute-done.7, bf16[1280,256]{0,1:T(8,128)(2,1)S(1)} %bitcast.84), kind=kOutput, calls=%fused_computation.3 | convolution fusion | flops 421068800 | bytes 5898240 | tf_op jit(solution)/shard_map/dot_general | solution.py:111
  145.7 10.2 %reduce-scatter.4.cloned.1.call-done = bf16[64,2560]{1,0:T(8,128)(2,1)} async-done(((bf16[256,2560]{1,0:T(8,128)(2,1)}), bf16[64,2560]{1,0:T(8,128)(2,1)}) %reduce-scatter.4.cloned.1.call-update) | async-done | bytes 327696
  (48 shorter events, 4.4 us)
Async XLA Ops:
  7.2 43.7 %copy-start = (bf16[256,640]{1,0:T(8,128)(2,1)S(1)}, bf16[256,640]{1,0:T(8,128)(2,1)}, u32[]{:S(2)}) copy-start(bf16[256,640]{1,0:T(8,128)(2,1)} %param.6) | copy-start | bytes 983044
  7.2 24.4 %copy-start.1 = (bf16[640,1280]{1,0:T(8,128)(2,1)S(1)}, bf16[640,1280]{1,0:T(8,128)(2,1)}, u32[]{:S(2)}) copy-start(bf16[640,1280]{1,0:T(8,128)(2,1)} %param.7) | copy-start | bytes 4915204
  7.2 63.0 %all-gather.4.cloned.1.call-start = ((), (), s32[]{:S(2)}) async-start(), calls=%async_computation.5 | async-start | bytes 1638400 | tf_op jit(solution)/shard_map/all_gather | solution.py:48
  7.2 40.8 %collective-permute-start.3 = (bf16[640,1280]{1,0:T(8,128)(2,1)}, bf16[640,1280]{1,0:T(8,128)(2,1)}, u32[]{:S(2)}, u32[]{:S(2)}) collective-permute-start(bf16[640,1280]{1,0:T(8,128)(2,1)} %param.7), channel_id=1, source_target_pairs={{0,4},{4,0},{1,5},{5,1},{2,6},{6,2},{3,7},{7,3},{8,12},{12,8},{9,1... | collective-permute-start | bytes 4915208 | tf_op jit(solution)/shard_map/ppermute | solution.py:57
  17.0 1.5 collective-permute-start
  17.7 123.7 %all-gather.6.cloned.1.call-start = ((), (), s32[]{:S(2)}) async-start(), calls=%async_computation.6 | async-start | bytes 1638400 | tf_op jit(solution)/shard_map/all_gather | solution.py:77
  18.4 14.4 %collective-permute-start.1 = (bf16[80,128]{1,0:T(8,128)(2,1)S(1)}, bf16[80,128]{1,0:T(8,128)(2,1)S(1)}, u32[]{:S(2)}, u32[]{:S(2)}) collective-permute-start(bf16[80,128]{1,0:T(8,128)(2,1)S(1)} %pad_maximum_fusion.2), channel_id=1, source_target_pairs={{0,32},{32,0},{64,96},{96,64},{1,33},{33,1},{65,97},{97,65},{2,34}... | collective-permute-start | bytes 61448 | tf_op jit(solution)/shard_map/ppermute | solution.py:24
  32.9 21.1 %collective-permute-start.2 = (bf16[160,128]{1,0:T(8,128)(2,1)S(1)}, bf16[160,128]{1,0:T(8,128)(2,1)S(1)}, u32[]{:S(2)}, u32[]{:S(2)}) collective-permute-start(bf16[160,128]{1,0:T(8,128)(2,1)S(1)} %pad_maximum_fusion.1), channel_id=1, source_target_pairs={{0,96},{96,0},{32,64},{64,32},{1,97},{97,1},{33,65},{65,33},{2,98}... | collective-permute-start | bytes 122888 | tf_op jit(solution)/shard_map/ppermute | solution.py:27
  72.9 10.7 %all-to-all-start.1 = ((bf16[4,256,128]{1,2,0:T(8,128)(2,1)}), bf16[4,256,128]{1,2,0:T(8,128)(2,1)S(1)}, u32[]{:S(2)}, u32[]{:S(2)}) async-start(bf16[4,256,128]{1,2,0:T(8,128)(2,1)} %broadcast_in_dim.25), calls=%async_computation.1 | async-start | bytes 524288 | tf_op jit(solution)/shard_map/all_to_all | solution.py:19
  83.9 7.6 %collective-permute-start.4 = (bf16[640,256]{0,1:T(8,128)(2,1)S(1)}, bf16[640,256]{0,1:T(8,128)(2,1)S(1)}, u32[]{:S(2)}, u32[]{:S(2)}) collective-permute-start(bf16[640,256]{0,1:T(8,128)(2,1)S(1)} %fusion.2), channel_id=1, source_target_pairs={{0,4},{4,0},{1,5},{5,1},{2,6},{6,2},{3,7},{7,3},{8,12},{12,8},{9,1... | collective-permute-start | bytes 983048 | tf_op jit(solution)/shard_map/ppermute | solution.py:90
  92.7 17.4 %copy-start.2 = (bf16[256,2560]{1,0:T(8,128)(2,1)S(1)}, bf16[256,2560]{1,0:T(8,128)(2,1)}, u32[]{:S(2)}) copy-start(bf16[256,2560]{1,0:T(8,128)(2,1)} %all-gather.4.cloned.1.call-done) | copy-start | bytes 3932164
  92.7 12.6 %all-to-all-start.2 = ((bf16[16,40,256]{2,1,0:T(8,128)(2,1)}), bf16[16,40,256]{2,1,0:T(8,128)(2,1)S(1)}, u32[]{:S(2)}, u32[]{:S(2)}) async-start(bf16[16,40,256]{2,1,0:T(8,128)(2,1)} %bitcast.16), calls=%async_computation.2 | async-start | bytes 655360 | tf_op jit(solution)/shard_map/all_to_all | solution.py:93
  96.4 59.5 %reduce-scatter.4.cloned.1.call-start = ((), (), s32[]{:S(2)}) async-start(), calls=%async_computation.7 | async-start | bytes 1638400
  105.3 8.5 %collective-permute-start.5 = (bf16[40,256]{1,0:T(8,128)(2,1)S(1)}, bf16[40,256]{1,0:T(8,128)(2,1)S(1)}, u32[]{:S(2)}, u32[]{:S(2)}) collective-permute-start(bf16[40,256]{1,0:T(8,128)(2,1)S(1)} %reduce_sum.12), channel_id=1, source_target_pairs={{0,32},{32,0},{64,96},{96,64},{1,33},{33,1},{65,97},{97,65},{2,34}... | collective-permute-start | bytes 61448 | tf_op jit(solution)/shard_map/ppermute | solution.py:36
  113.8 8.4 %collective-permute-start.6 = (bf16[40,256]{1,0:T(8,128)(2,1)S(1)}, bf16[40,256]{1,0:T(8,128)(2,1)S(1)}, u32[]{:S(2)}, u32[]{:S(2)}) collective-permute-start(bf16[40,256]{1,0:T(8,128)(2,1)S(1)} %add_convert_fusion.1), channel_id=1, source_target_pairs={{0,96},{96,0},{32,64},{64,32},{1,97},{97,1},{33,65},{65,33},{2,98}... | collective-permute-start | bytes 61448 | tf_op jit(solution)/shard_map/ppermute | solution.py:39
  123.0 11.4 %all-to-all-start.3 = ((bf16[16,40,256]{2,1,0:T(8,128)(2,1)}), bf16[16,40,256]{2,1,0:T(8,128)(2,1)S(1)}, u32[]{:S(2)}, u32[]{:S(2)}) async-start(bf16[16,40,256]{2,1,0:T(8,128)(2,1)} %broadcast_in_dim.26), calls=%async_computation.3 | async-start | bytes 655360 | tf_op jit(solution)/shard_map/all_to_all | solution.py:19
  134.4 9.5 %collective-permute-start.7 = (bf16[640,256]{1,0:T(8,128)(2,1)S(1)}, bf16[640,256]{1,0:T(8,128)(2,1)S(1)}, u32[]{:S(2)}, u32[]{:S(2)}) collective-permute-start(bf16[640,256]{1,0:T(8,128)(2,1)S(1)} %bitcast.86), channel_id=1, source_target_pairs={{0,4},{4,0},{1,5},{5,1},{2,6},{6,2},{3,7},{7,3},{8,12},{12,8},{9,1... | collective-permute-start | bytes 983048 | tf_op jit(solution)/shard_map/ppermute | solution.py:106
Sparse Core Ops, SparseCore 0:
  17.8 48.1 all-gather.3
  70.3 40.4 all-gather.5
  114.3 41.5 reduce-scatter.3

commit v2 on v1

v2 whole, which is shorter than its diff:
```python
import jax
import jax.numpy as jnp
from jax import lax
from jax.experimental import pallas as pl
from jax.experimental.pallas import tpu as pltpu
from jax.sharding import Mesh, PartitionSpec as P

ADAM_STEP = 10
BF16 = jnp.bfloat16
F32 = jnp.float32
AXES = ("y", "zh", "x", "core", "zl")
SIZES = (4, 4, 4, 2, 4)
CORE_SWAP = [(0, 1), (1, 0)]
PAIR = [(0, 1), (1, 0), (2, 3), (3, 2)]
MIRROR = [(0, 3), (3, 0), (1, 2), (2, 1)]
TURN = [(a * 4 + b, b * 4 + a) for a in range(4) for b in range(4)]


def spread(values, axes, count):
    copies = jnp.broadcast_to(values[None], (count,) + values.shape)
    return lax.all_to_all(copies, axes, 0, 0, tiled=True)


def gather_zh(values):
    zh = lax.axis_index("zh")
    got = lax.ppermute(values, "zh", PAIR)
    odd = zh % 2 == 1
    pair = jnp.concatenate([jnp.where(odd, got, values), jnp.where(odd, values, got)], 0)
    got = lax.ppermute(pair, "zh", MIRROR)
    high = zh >= 2
    both = jnp.stack([jnp.where(high, got, pair), jnp.where(high, pair, got)])
    return both.reshape(4, *values.shape)


def sum_zh(values):
    for partners in (PAIR, MIRROR):
        sent = values.astype(BF16)
        values = sent.astype(F32) + lax.ppermute(sent, "zh", partners).astype(F32)
    return values


VMEM = pl.BlockSpec(memory_space=pltpu.VMEM)
SMEM = pl.BlockSpec(memory_space=pltpu.SMEM)
ROOM = pltpu.CompilerParams(vmem_limit_bytes=40 * 2**20)


def cost(flops, moved):
    return pl.CostEstimate(flops=flops, bytes_accessed=moved, transcendentals=0)


def columns_of(which, half):
    return pl.ds(pl.multiple_of(which * half, 128), half)


def mixed_kernel(core_ref, x_ref, own_ref, other_ref, out_ref):
    core = core_ref[0]
    half = own_ref.shape[1]
    for which, weight in ((core, own_ref), (1 - core, other_ref)):
        part = jnp.dot(x_ref[...], weight[...], preferred_element_type=F32)
        out_ref[:, columns_of(which, half)] = part.astype(BF16)


def mixed_matmul(core, x_heads, own, other):
    return pl.pallas_call(
        mixed_kernel,
        out_shape=jax.ShapeDtypeStruct((256, 2560), BF16),
        in_specs=[SMEM, VMEM, VMEM, VMEM],
        out_specs=VMEM,
        compiler_params=ROOM,
        cost_estimate=cost(2 * 256 * 640 * 2560, 5_000_000),
    )(core, x_heads, own, other)


def head_kernel(core_ref, grad_ref, own_ref, other_ref, out_ref):
    core = core_ref[0]
    half = own_ref.shape[1]
    total = None
    for which, weight in ((core, own_ref), (1 - core, other_ref)):
        part = lax.dot_general(
            grad_ref[:, columns_of(which, half)],
            weight[...],
            (((1,), (1,)), ((), ())),
            preferred_element_type=F32,
        )
        total = part if total is None else total + part
    out_ref[...] = total.astype(BF16)


def head_matmul(core, grads, own, other):
    return pl.pallas_call(
        head_kernel,
        out_shape=jax.ShapeDtypeStruct((256, 640), BF16),
        in_specs=[SMEM, VMEM, VMEM, VMEM],
        out_specs=VMEM,
        compiler_params=ROOM,
        cost_estimate=cost(2 * 256 * 640 * 2560, 5_000_000),
    )(core, grads, own, other)


def low_kernel(basis_ref, x_ref, grad_ref, *refs):
    out_ref = refs[-1]
    reduced = jnp.dot(grad_ref[...], basis_ref[...], preferred_element_type=F32).astype(BF16)
    low = lax.dot_general(
        x_ref[...], reduced, (((0,), (0,)), ((), ())), preferred_element_type=F32
    )
    if len(refs) == 2:
        low = refs[0][...] + low
    out_ref[...] = low.astype(out_ref.dtype)


def low_matmul(basis, rows, grads, *before):
    return pl.pallas_call(
        low_kernel,
        out_shape=jax.ShapeDtypeStruct((640, 256), BF16 if before else F32),
        in_specs=[VMEM] * (3 + len(before)),
        out_specs=VMEM,
        compiler_params=ROOM,
        cost_estimate=cost(2 * 256 * 256 * (2560 + 640), 3_500_000),
    )(basis, rows, grads, *before)


def shards(x_heads, proj_weight, out_grad, proj_basis, first_moment, second_moment):
    core = lax.axis_index("core")
    half = proj_weight.shape[1]

    scalar = core.reshape(1).astype(jnp.int32)

    grad_block = lax.all_gather(out_grad, "zl", axis=0, tiled=True)

    def own_columns(values):
        return lax.dynamic_slice_in_dim(values, core * 256, 256, 1)

    moments = jnp.concatenate([own_columns(first_moment[0]), own_columns(second_moment[0])], 0)
    moments = lax.ppermute(moments.astype(BF16), ("zh", "x"), TURN)

    weight_other = lax.ppermute(proj_weight, "core", CORE_SWAP)
    x_other = lax.ppermute(x_heads, "core", CORE_SWAP)
    by_zh = gather_zh(jnp.concatenate([own_columns(proj_basis), moments], 0))
    by_zh, weight_other = lax.optimization_barrier((by_zh, weight_other))
    m_old = by_zh[:, 40:50].reshape(40, 256)
    v_old = by_zh[:, 50:].reshape(40, 256)
    by_yx = spread(by_zh[:, :40].reshape(160, 256), ("y", "x"), 16)
    mixed_part = mixed_matmul(scalar, x_heads, proj_weight, weight_other)
    by_yx, mixed_part, grad_block, x_other = lax.optimization_barrier(
        (by_yx, mixed_part, grad_block, x_other)
    )
    grad_other = lax.ppermute(grad_block, "core", CORE_SWAP)
    basis_cols = by_yx.reshape(4, 4, 4, 40, 256).transpose(0, 2, 1, 3, 4).reshape(2560, 256)

    mixed_out = lax.psum_scatter(mixed_part, "zl", scatter_dimension=0, tiled=True)

    low_own = low_matmul(basis_cols, x_heads, grad_block)
    low_chip = low_matmul(basis_cols, x_other, grad_other, low_own)

    low_yx = lax.all_to_all(low_chip.reshape(16, 40, 256), ("y", "x"), 0, 0, tiled=True)
    basis_cols, low_chip = lax.optimization_barrier((basis_cols, low_chip))
    basis_own = lax.dynamic_slice_in_dim(basis_cols, core * half, half, 0)
    basis_other = lax.ppermute(
        lax.dynamic_slice_in_dim(basis_cols, (1 - core) * half, half, 0), "core", CORE_SWAP
    )
    low_yx, basis_other = lax.optimization_barrier((low_yx, basis_other))
    low = sum_zh(jnp.sum(low_yx.astype(F32), 0))

    m_new = 0.9 * m_old.astype(F32) + 0.1 * low
    v_new = 0.999 * v_old.astype(F32) + 0.001 * low * low
    corr_one = 1.0 - 0.9**ADAM_STEP
    corr_two = 1.0 - 0.999**ADAM_STEP
    direction = (m_new / corr_one / (jnp.sqrt(v_new / corr_two) + 1e-08)).astype(BF16)

    rows = spread(direction, ("y", "x"), 16).reshape(640, 256)
    head_rows = head_matmul(scalar, grad_block, proj_weight, weight_other)
    rows, head_rows, mixed_out = lax.optimization_barrier((rows, head_rows, mixed_out))
    rows_other = lax.ppermute(rows, "core", CORE_SWAP)

    def half_update(columns, basis):
        return lax.dot_general(columns, basis, (((1,), (1,)), ((), ())), preferred_element_type=F32)

    update = (half_update(rows, basis_own) + half_update(rows_other, basis_other)).astype(BF16)
    return (mixed_out, head_rows, update)


def solution(mesh):
    fine = Mesh(mesh.devices.reshape(SIZES), AXES)
    dp = ("y", "zh", "x")
    return jax.shard_map(
        shards,
        mesh=fine,
        in_specs=(
            P(dp + ("core",), "zl"),
            P("zl", "core"),
            P(dp + ("core", "zl"), None),
            P(dp, None),
            P("zl", dp, None),
            P("zl", dp, None),
        ),
        out_specs=(
            P(dp + ("core", "zl"), None),
            P(dp + ("core",), "zl"),
            P("zl", "core"),
        ),
        check_vma=False,
    )
```

time: 163 us -> 152 us (0.933)
  waiting for transfers between devices: 35.1 us -> 19.4 us
  starting transfers between devices: 71.7 us -> 81.8 us
  matrix products: 10.9 us -> 3.52 us
  Pallas kernels: 0 us -> 7.3 us
  local copies, waits for them, and re-layouts: 15.2 us -> 11 us
  blocking collectives: 15.2 us -> 13.5 us
    ppermute x4 -> x6, starting transfers between devices: 17.2 us -> 28 us  [the longest x2 14.4 us: sum_zh(): values = sent.astype(F32) + lax.ppermute(sent, 'zh', partners).astype(F32)]
    unnamed x4 -> x2, waiting for transfers between devices: 10.2 us -> 0.03 us
    all_to_all x2, waiting for transfers between devices: 12.6 us -> 3.18 us  [spread(): return lax.all_to_all(copies, axes, 0, 0, tiled=True)]
    all_gather x1, waiting for transfers between devices: 0.02 us -> 9.18 us  [shards(): grad_block = lax.all_gather(out_grad, 'zl', axis=0, tiled=True)]
    dot_general x7 -> x2, matrix products: 10.9 us -> 3.52 us  [half_update(): lax.dot_general(columns, basis, (((1,), (1,)), ((), ())), preferred_eleme...]
    pallas_call x0 -> x4, Pallas kernels: none -> 7.3 us  [the longest x2 3.12 us: low_matmul(): pl.pallas_call(low_kernel, out_shape=jax.ShapeDtypeStruct((640, 256), BF1...]
    all_to_all x1 -> x0, waiting for transfers between devices: 7.25 us -> none  [shards(): lax.all_to_all(low_chip.reshape(16, 40, 256), ('y', 'x'), 0, 0, tiled=True)]
    dynamic_update_slice x2 -> x0, local copies, waits for them, and re-layouts: 4.1 us -> none  [the longest x1 2.77 us: shards(): lax.dynamic_update_slice(weight_full, weight_other, (0, (1 - core) * half))]
  transfers between devices with their start and end apart: 14 -> 14, of which waited for: 7 -> 7; matrix products, arithmetic and copies ran while one was open for 16% -> 3% of each run, Pallas kernels for 0% -> 5%
where the time goes in v2:
time: 152 us; the launch traced here: 151 us
  starting transfers between devices  81.8 us (54%)
  waiting for transfers between devices  19.4 us (13%)
  between operations  14.4 us (9%)
  blocking collectives  13.5 us (9%)
  local copies, waits for them, and re-layouts  11 us (7%)
  Pallas kernels  7.3 us (5%)
  matrix products  3.52 us (2%)
    ppermute x1, starting transfers between devices, gather_zh(): got = lax.ppermute(pair, 'zh', MIRROR)  15.1 us
    ppermute x2, starting transfers between devices, sum_zh(): values = sent.astype(F32) + lax.ppermute(sent, 'zh', partners).astype(F32)  14.4 us
    all_to_all x1, blocking collectives, shards(): lax.all_to_all(low_chip.reshape(16, 40, 256), ('y', 'x'), 0, 0, tiled=True)  13.5 us
    ppermute x1, starting transfers between devices, gather_zh(): got = lax.ppermute(values, 'zh', PAIR)  12 us
    all_to_all x2, starting transfers between devices, spread(): return lax.all_to_all(copies, axes, 0, 0, tiled=True)  11 us
    all_gather x1, waiting for transfers between devices, shards(): grad_block = lax.all_gather(out_grad, 'zl', axis=0, tiled=True)  9.18 us
    ppermute x1, starting transfers between devices, shards(): weight_other = lax.ppermute(proj_weight, 'core', CORE_SWAP)  8.79 us
    ppermute x1, starting transfers between devices, shards(): rows_other = lax.ppermute(rows, 'core', CORE_SWAP)  6.87 us
  transfers between devices with their start and end apart: 14, of which 7 were waited for; matrix products, arithmetic and copies ran while one was open for 3% of the time, Pallas kernels for 5%

profile of v2, /device:TPU:1, one launch (start us, length us, event | category | flops | bytes accessed | tf_op | source)
XLA Modules:
  0.0 151.1 jit_solution(14797178790081667849)
XLA Ops:
  7.2 8.8 %collective-permute-start.3 = (bf16[640,1280]{1,0:T(8,128)(2,1)}, bf16[640,1280]{1,0:T(8,128)(2,1)S(1)}, u32[]{:S(2)}, u32[]{:S(2)}) collective-permute-start(bf16[640,1280]{1,0:T(8,128)(2,1)} %own_ref.3), channel_id=1, source_target_pairs={{0,4},{4,0},{1,5},{5,1},{2,6},{6,2},{3,7},{7,3},{8,12},{12,8},{9,1... | collective-permute-start | bytes 4915208 | tf_op jit(solution)/shard_map/ppermute | solution.py:136
  16.0 0.7 dynamic-slice_convert_fusion
  17.5 12.0 %collective-permute-start.1 = (bf16[60,256]{1,0:T(8,128)(2,1)S(1)}, bf16[60,256]{1,0:T(8,128)(2,1)S(1)}, u32[]{:S(2)}, u32[]{:S(2)}) collective-permute-start(bf16[60,256]{1,0:T(8,128)(2,1)S(1)} %pad_maximum_fusion.2), channel_id=1, source_target_pairs={{0,32},{32,0},{64,96},{96,64},{1,33},{33,1},{65,97},{97,65},{2,34}... | collective-permute-start | bytes 92168 | tf_op jit(solution)/shard_map/ppermute | solution.py:26
  29.5 1.3 collective-permute-done.1
  30.8 15.1 %collective-permute-start.2 = (bf16[120,256]{1,0:T(8,128)(2,1)S(1)}, bf16[120,256]{1,0:T(8,128)(2,1)S(1)}, u32[]{:S(2)}, u32[]{:S(2)}) collective-permute-start(bf16[120,256]{1,0:T(8,128)(2,1)S(1)} %pad_maximum_fusion.1), channel_id=1, source_target_pairs={{0,96},{96,0},{32,64},{64,32},{1,97},{97,1},{33,65},{65,33},{2,98}... | collective-permute-start | bytes 184328 | tf_op jit(solution)/shard_map/ppermute | solution.py:29
  46.0 1.9 %collective-permute-done.2 = bf16[120,256]{1,0:T(8,128)(2,1)S(1)} collective-permute-done((bf16[120,256]{1,0:T(8,128)(2,1)S(1)}, bf16[120,256]{1,0:T(8,128)(2,1)S(1)}, u32[]{:S(2)}, u32[]{:S(2)}) %collective-permute-start.2) | collective-permute-done | bytes 61472 | tf_op jit(solution)/shard_map/ppermute | solution.py:29
  48.0 1.2 copy-done.2
  49.2 1.2 broadcast_in_dim.14
  50.4 7.5 %all-to-all-start = ((bf16[16,160,256]{2,1,0:T(8,128)(2,1)}), bf16[16,160,256]{2,1,0:T(8,128)(2,1)}, u32[]{:S(2)}, u32[]{:S(2)}) async-start(bf16[16,160,256]{2,1,0:T(8,128)(2,1)} %broadcast_in_dim.14), calls=%async_computation | async-start | bytes 2621440 | tf_op jit(solution)/shard_map/all_to_all | solution.py:21
  57.9 6.7 %collective-permute-start.4 = (bf16[256,640]{1,0:T(8,128)(2,1)S(1)}, bf16[256,640]{1,0:T(8,128)(2,1)S(1)}, u32[]{:S(2)}, u32[]{:S(2)}) collective-permute-start(bf16[256,640]{1,0:T(8,128)(2,1)S(1)} %copy-done.7), channel_id=1, source_target_pairs={{0,4},{4,0},{1,5},{5,1},{2,6},{6,2},{3,7},{7,3},{8,12},{12,8},{9,1... | collective-permute-start | bytes 983048 | tf_op jit(solution)/shard_map/ppermute | solution.py:137
  64.6 1.4 copy-done.3
  66.0 2.2 %shard_map.85 = bf16[256,2560]{1,0:T(8,128)(2,1)} custom-call(s32[1]{0:T(128)} %bitcast.4.core_ref, bf16[256,640]{1,0:T(8,128)(2,1)S(1)} %copy-done.7, bf16[640,1280]{1,0:T(8,128)(2,1)S(1)} %copy-done.1, bf16[640,1280]{1,0:T(8,128)(2,1)S(1)} %copy-done.3), custom_call_target="tpu_custom_call" | custom-call | flops 838860800 | bytes 5000000 | tf_op jit(solution)/shard_map/pallas_call | solution.py:64
  68.3 9.2 %all-gather.2.cloned.1.call-done.grad_ref = bf16[256,2560]{1,0:T(8,128)(2,1)} async-done(((bf16[64,2560]{1,0:T(8,128)(2,1)}), bf16[256,2560]{1,0:T(8,128)(2,1)}) %all-gather.2.cloned.1.call-update) | async-done | bytes 1310736 | tf_op jit(solution)/shard_map/all_gather | solution.py:128
  77.5 4.3 %collective-permute-start.5 = (bf16[256,2560]{1,0:T(8,128)(2,1)}, bf16[256,2560]{1,0:T(8,128)(2,1)}, u32[]{:S(2)}, u32[]{:S(2)}) collective-permute-start(bf16[256,2560]{1,0:T(8,128)(2,1)} %all-gather.2.cloned.1.call-done.grad_ref), channel_id=1, source_target_pairs={{0,4},{4,0},{1,5},{5,1},{2,6},{6,2},{3,7},{7,3},{8,12},{12,8},{9,1... | collective-permute-start | bytes 3932168 | tf_op jit(solution)/shard_map/ppermute | solution.py:147
  81.8 1.4 copy.11
  83.3 1.3 copy-done.5
  84.6 0.9 shard_map.86.refs_0_
  85.6 2.2 %shard_map.87 = bf16[640,256]{1,0:T(8,128)(2,1)S(1)} custom-call(bf16[2560,256]{1,0:T(8,128)(2,1)S(1)} %bitcast.22, bf16[256,640]{1,0:T(8,128)(2,1)S(1)} %copy-done.9, bf16[256,2560]{1,0:T(8,128)(2,1)} %collective-permute-done.5.grad_ref, f32[640,256]{1,0:T(8,128)S(1)} %shard_map.86.refs_0_), custom_call_target="tpu_custom_call" | custom-call | flops 419430400 | bytes 3500000 | tf_op jit(solution)/shard_map/pallas_call | solution.py:112
  87.8 1.9 %collective-permute-start.6 = (bf16[1280,256]{1,0:T(8,128)(2,1)S(1)}, bf16[1280,256]{1,0:T(8,128)(2,1)}, u32[]{:S(2)}, u32[]{:S(2)}) collective-permute-start(bf16[1280,256]{1,0:T(8,128)(2,1)S(1)} %constant_dynamic-slice_fusion), channel_id=1, source_target_pairs={{0,4},{4,0},{1,5},{5,1},{2,6},{6,2},{3,7},{7,3},{8,12},{12,8},{9,1... | collective-permute-start | bytes 1966088 | tf_op jit(solution)/shard_map/ppermute | solution.py:158
  89.8 13.5 %all_to_all.15 = bf16[16,40,256]{2,1,0:T(8,128)(2,1)S(1)} all-to-all(bf16[16,40,256]{2,1,0:T(8,128)(2,1)S(1)} %bitcast.25), channel_id=1, replica_groups=mesh['y'=4,'zh'=4,'x'=4,'core'=2,'zl'=4] {'y','x'}, dimensions={0} | all-to-all | bytes 655360 | tf_op jit(solution)/shard_map/all_to_all | solution.py:155
  103.3 7.4 %collective-permute-start.7 = (bf16[40,256]{1,0:T(8,128)(2,1)S(1)}, bf16[40,256]{1,0:T(8,128)(2,1)S(1)}, u32[]{:S(2)}, u32[]{:S(2)}) collective-permute-start(bf16[40,256]{1,0:T(8,128)(2,1)S(1)} %reduce_sum.12), channel_id=1, source_target_pairs={{0,32},{32,0},{64,96},{96,64},{1,33},{33,1},{65,97},{97,65},{2,34}... | collective-permute-start | bytes 61448 | tf_op jit(solution)/shard_map/ppermute | solution.py:38
  110.7 1.3 collective-permute-done.7
  112.0 7.1 %collective-permute-start.8 = (bf16[40,256]{1,0:T(8,128)(2,1)S(1)}, bf16[40,256]{1,0:T(8,128)(2,1)S(1)}, u32[]{:S(2)}, u32[]{:S(2)}) collective-permute-start(bf16[40,256]{1,0:T(8,128)(2,1)S(1)} %add_convert_fusion), channel_id=1, source_target_pairs={{0,96},{96,0},{32,64},{64,32},{1,97},{97,1},{33,65},{65,33},{2,98}... | collective-permute-start | bytes 61448 | tf_op jit(solution)/shard_map/ppermute | solution.py:38
  119.2 1.9 %collective-permute-done.8 = bf16[40,256]{1,0:T(8,128)(2,1)S(1)} collective-permute-done((bf16[40,256]{1,0:T(8,128)(2,1)S(1)}, bf16[40,256]{1,0:T(8,128)(2,1)S(1)}, u32[]{:S(2)}, u32[]{:S(2)}) %collective-permute-start.8) | collective-permute-done | bytes 20512 | tf_op jit(solution)/shard_map/ppermute | solution.py:38
  121.1 0.7 broadcast_in_dim.15
  121.9 3.5 %all-to-all-start.2 = ((bf16[16,40,256]{2,1,0:T(8,128)(2,1)}), bf16[16,40,256]{2,1,0:T(8,128)(2,1)S(1)}, u32[]{:S(2)}, u32[]{:S(2)}) async-start(bf16[16,40,256]{2,1,0:T(8,128)(2,1)} %broadcast_in_dim.15), calls=%async_computation.2 | async-start | bytes 655360 | tf_op jit(solution)/shard_map/all_to_all | solution.py:21
  125.4 1.4 copy-done.4
  126.9 1.3 copy-done.6
  128.2 1.9 %shard_map.88 = bf16[256,640]{1,0:T(8,128)(2,1)} custom-call(s32[1]{0:T(128)} %bitcast.4.core_ref, bf16[256,2560]{1,0:T(8,128)(2,1)S(1)} %copy-done.6, bf16[640,1280]{1,0:T(8,128)(2,1)S(1)} %copy-done.1, bf16[640,1280]{1,0:T(8,128)(2,1)S(1)} %copy-done.4), custom_call_target="tpu_custom_call" | custom-call | flops 838860800 | bytes 5000000 | tf_op jit(solution)/shard_map/pallas_call | solution.py:90
  130.1 3.2 %all-to-all-done.2 = bf16[16,40,256]{2,1,0:T(8,128)(2,1)S(1)} async-done(((bf16[16,40,256]{2,1,0:T(8,128)(2,1)}), bf16[16,40,256]{2,1,0:T(8,128)(2,1)S(1)}, u32[]{:S(2)}, u32[]{:S(2)}) %all-to-all-start.2) | async-done | bytes 327712 | tf_op jit(solution)/shard_map/all_to_all | solution.py:21
  133.3 6.9 %collective-permute-start.9 = (bf16[640,256]{1,0:T(8,128)(2,1)S(1)}, bf16[640,256]{1,0:T(8,128)(2,1)S(1)}, u32[]{:S(2)}, u32[]{:S(2)}) collective-permute-start(bf16[640,256]{1,0:T(8,128)(2,1)S(1)} %bitcast.26), channel_id=1, source_target_pairs={{0,4},{4,0},{1,5},{5,1},{2,6},{6,2},{3,7},{7,3},{8,12},{12,8},{9,1... | collective-permute-start | bytes 983048 | tf_op jit(solution)/shard_map/ppermute | solution.py:173
  141.4 2.9 %fusion = bf16[640,1280]{1,0:T(8,128)(2,1)} fusion(f32[640,1280]{1,0:T(8,128)S(1)} %fusion.1, bf16[640,256]{1,0:T(8,128)(2,1)S(1)} %collective-permute-done.9, bf16[1280,256]{1,0:T(8,128)(2,1)} %collective-permute-done.6), kind=kOutput, calls=%fused_computation.1 | convolution fusion | flops 421068800 | bytes 5898240 | tf_op jit(solution)/shard_map/dot_general | solution.py:176
  (47 shorter events, 2.4 us)
Async XLA Ops:
  7.2 10.3 %copy-start = (bf16[40,512]{1,0:T(8,128)(2,1)S(1)}, bf16[40,512]{1,0:T(8,128)(2,1)}, u32[]{:S(2)}) copy-start(bf16[40,512]{1,0:T(8,128)(2,1)} %param.9) | copy-start | bytes 122884
  7.2 70.3 %all-gather.2.cloned.1.call-start = ((), (), s32[]{:S(2)}) async-start(), calls=%async_computation.4 | async-start | bytes 1638400 | tf_op jit(solution)/shard_map/all_gather | solution.py:128
  7.2 40.8 %collective-permute-start.3 = (bf16[640,1280]{1,0:T(8,128)(2,1)}, bf16[640,1280]{1,0:T(8,128)(2,1)S(1)}, u32[]{:S(2)}, u32[]{:S(2)}) collective-permute-start(bf16[640,1280]{1,0:T(8,128)(2,1)} %own_ref.3), channel_id=1, source_target_pairs={{0,4},{4,0},{1,5},{5,1},{2,6},{6,2},{3,7},{7,3},{8,12},{12,8},{9,1... | collective-permute-start | bytes 4915208 | tf_op jit(solution)/shard_map/ppermute | solution.py:136
  16.8 0.7 collective-permute-start
  17.5 13.3 %collective-permute-start.1 = (bf16[60,256]{1,0:T(8,128)(2,1)S(1)}, bf16[60,256]{1,0:T(8,128)(2,1)S(1)}, u32[]{:S(2)}, u32[]{:S(2)}) collective-permute-start(bf16[60,256]{1,0:T(8,128)(2,1)S(1)} %pad_maximum_fusion.2), channel_id=1, source_target_pairs={{0,32},{32,0},{64,96},{96,64},{1,33},{33,1},{65,97},{97,65},{2,34}... | collective-permute-start | bytes 92168 | tf_op jit(solution)/shard_map/ppermute | solution.py:26
  30.8 17.1 %collective-permute-start.2 = (bf16[120,256]{1,0:T(8,128)(2,1)S(1)}, bf16[120,256]{1,0:T(8,128)(2,1)S(1)}, u32[]{:S(2)}, u32[]{:S(2)}) collective-permute-start(bf16[120,256]{1,0:T(8,128)(2,1)S(1)} %pad_maximum_fusion.1), channel_id=1, source_target_pairs={{0,96},{96,0},{32,64},{64,32},{1,97},{97,1},{33,65},{65,33},{2,98}... | collective-permute-start | bytes 184328 | tf_op jit(solution)/shard_map/ppermute | solution.py:29
  48.0 1.2 copy-start.2
  50.4 7.5 %copy-start.7 = (bf16[256,640]{1,0:T(8,128)(2,1)S(1)}, bf16[256,640]{1,0:T(8,128)(2,1)}, u32[]{:S(2)}) copy-start(bf16[256,640]{1,0:T(8,128)(2,1)} %x_ref.3) | copy-start | bytes 983044
  50.4 14.2 %copy-start.1 = (bf16[640,1280]{1,0:T(8,128)(2,1)S(1)}, bf16[640,1280]{1,0:T(8,128)(2,1)}, u32[]{:S(2)}) copy-start(bf16[640,1280]{1,0:T(8,128)(2,1)} %own_ref.3) | copy-start | bytes 4915204
  50.4 27.1 %all-to-all-start = ((bf16[16,160,256]{2,1,0:T(8,128)(2,1)}), bf16[16,160,256]{2,1,0:T(8,128)(2,1)}, u32[]{:S(2)}, u32[]{:S(2)}) async-start(bf16[16,160,256]{2,1,0:T(8,128)(2,1)} %broadcast_in_dim.14), calls=%async_computation | async-start | bytes 2621440 | tf_op jit(solution)/shard_map/all_to_all | solution.py:21
  57.9 75.4 %reduce-scatter.2.cloned.1.call-start = ((), (), s32[]{:S(2)}) async-start(), calls=%async_computation.5 | async-start | bytes 1638400 | tf_op jit(solution)/shard_map/reduce_scatter | solution.py:150
  57.9 10.4 %collective-permute-start.4 = (bf16[256,640]{1,0:T(8,128)(2,1)S(1)}, bf16[256,640]{1,0:T(8,128)(2,1)S(1)}, u32[]{:S(2)}, u32[]{:S(2)}) collective-permute-start(bf16[256,640]{1,0:T(8,128)(2,1)S(1)} %copy-done.7), channel_id=1, source_target_pairs={{0,4},{4,0},{1,5},{5,1},{2,6},{6,2},{3,7},{7,3},{8,12},{12,8},{9,1... | collective-permute-start | bytes 983048 | tf_op jit(solution)/shard_map/ppermute | solution.py:137
  64.6 1.4 copy-start.3
  68.3 13.5 %copy-start.8 = (bf16[256,640]{1,0:T(8,128)(2,1)}, bf16[256,640]{1,0:T(8,128)(2,1)S(1)}, u32[]{:S(2)}) copy-start(bf16[256,640]{1,0:T(8,128)(2,1)S(1)} %collective-permute-done.4.x_ref) | copy-start | bytes 983044
  77.5 8.0 %collective-permute-start.5 = (bf16[256,2560]{1,0:T(8,128)(2,1)}, bf16[256,2560]{1,0:T(8,128)(2,1)}, u32[]{:S(2)}, u32[]{:S(2)}) collective-permute-start(bf16[256,2560]{1,0:T(8,128)(2,1)} %all-gather.2.cloned.1.call-done.grad_ref), channel_id=1, source_target_pairs={{0,4},{4,0},{1,5},{5,1},{2,6},{6,2},{3,7},{7,3},{8,12},{12,8},{9,1... | collective-permute-start | bytes 3932168 | tf_op jit(solution)/shard_map/ppermute | solution.py:147
  83.3 1.3 copy-start.5
  84.6 1.0 copy-start.9
  87.8 15.4 %collective-permute-start.6 = (bf16[1280,256]{1,0:T(8,128)(2,1)S(1)}, bf16[1280,256]{1,0:T(8,128)(2,1)}, u32[]{:S(2)}, u32[]{:S(2)}) collective-permute-start(bf16[1280,256]{1,0:T(8,128)(2,1)S(1)} %constant_dynamic-slice_fusion), channel_id=1, source_target_pairs={{0,4},{4,0},{1,5},{5,1},{2,6},{6,2},{3,7},{7,3},{8,12},{12,8},{9,1... | collective-permute-start | bytes 1966088 | tf_op jit(solution)/shard_map/ppermute | solution.py:158
  103.3 8.7 %collective-permute-start.7 = (bf16[40,256]{1,0:T(8,128)(2,1)S(1)}, bf16[40,256]{1,0:T(8,128)(2,1)S(1)}, u32[]{:S(2)}, u32[]{:S(2)}) collective-permute-start(bf16[40,256]{1,0:T(8,128)(2,1)S(1)} %reduce_sum.12), channel_id=1, source_target_pairs={{0,32},{32,0},{64,96},{96,64},{1,33},{33,1},{65,97},{97,65},{2,34}... | collective-permute-start | bytes 61448 | tf_op jit(solution)/shard_map/ppermute | solution.py:38
  112.0 9.0 %collective-permute-start.8 = (bf16[40,256]{1,0:T(8,128)(2,1)S(1)}, bf16[40,256]{1,0:T(8,128)(2,1)S(1)}, u32[]{:S(2)}, u32[]{:S(2)}) collective-permute-start(bf16[40,256]{1,0:T(8,128)(2,1)S(1)} %add_convert_fusion), channel_id=1, source_target_pairs={{0,96},{96,0},{32,64},{64,32},{1,97},{97,1},{33,65},{65,33},{2,98}... | collective-permute-start | bytes 61448 | tf_op jit(solution)/shard_map/ppermute | solution.py:38
  121.9 11.4 %all-to-all-start.2 = ((bf16[16,40,256]{2,1,0:T(8,128)(2,1)}), bf16[16,40,256]{2,1,0:T(8,128)(2,1)S(1)}, u32[]{:S(2)}, u32[]{:S(2)}) async-start(bf16[16,40,256]{2,1,0:T(8,128)(2,1)} %broadcast_in_dim.15), calls=%async_computation.2 | async-start | bytes 655360 | tf_op jit(solution)/shard_map/all_to_all | solution.py:21
  125.4 1.4 copy-start.4
  126.9 1.3 copy-start.6
  133.3 8.1 %collective-permute-start.9 = (bf16[640,256]{1,0:T(8,128)(2,1)S(1)}, bf16[640,256]{1,0:T(8,128)(2,1)S(1)}, u32[]{:S(2)}, u32[]{:S(2)}) collective-permute-start(bf16[640,256]{1,0:T(8,128)(2,1)S(1)} %bitcast.26), channel_id=1, source_target_pairs={{0,4},{4,0},{1,5},{5,1},{2,6},{6,2},{3,7},{7,3},{8,12},{12,8},{9,1... | collective-permute-start | bytes 983048 | tf_op jit(solution)/shard_map/ppermute | solution.py:173
Sparse Core Ops, SparseCore 0:
  29.6 47.7 all-gather.1
  81.9 41.2 reduce-scatter.1

commit v3 on v2

--- a/solution.py
+++ b/solution.py
@@ -97,68 +97,89 @@
     )(core, grads, own, other)
 
 
-def low_kernel(basis_ref, x_ref, grad_ref, *refs):
-    out_ref = refs[-1]
-    reduced = jnp.dot(grad_ref[...], basis_ref[...], preferred_element_type=F32).astype(BF16)
-    low = lax.dot_general(
-        x_ref[...], reduced, (((0,), (0,)), ((), ())), preferred_element_type=F32
-    )
-    if len(refs) == 2:
-        low = refs[0][...] + low
-    out_ref[...] = low.astype(out_ref.dtype)
-
-
-def low_matmul(basis, rows, grads, *before):
+def reduced_kernel(basis_ref, own_ref, other_ref, out_ref):
+    for which, grads in ((0, own_ref), (1, other_ref)):
+        part = jnp.dot(grads[...], basis_ref[...], preferred_element_type=F32).astype(BF16)
+        for target in range(out_ref.shape[0]):
+            out_ref[target, which] = part
+
+
+def reduced_matmul(basis, grads, grads_other):
+    return pl.pallas_call(
+        reduced_kernel,
+        out_shape=jax.ShapeDtypeStruct((4, 2, 64, 256), BF16),
+        in_specs=[VMEM] * 3,
+        out_specs=VMEM,
+        compiler_params=ROOM,
+        cost_estimate=cost(2 * 128 * 256 * 2560, 2_500_000),
+    )(basis, grads, grads_other)
+
+
+def low_kernel(reduced_ref, own_ref, other_ref, out_ref):
+    total = None
+    for which, rows in ((0, own_ref), (1, other_ref)):
+        reduced = reduced_ref[:, which].reshape(256, 256)
+        part = lax.dot_general(
+            rows[...], reduced, (((0,), (0,)), ((), ())), preferred_element_type=F32
+        )
+        total = part if total is None else total + part
+    out_ref[...] = total.astype(BF16)
+
+
+def low_matmul(reduced, rows, rows_other):
     return pl.pallas_call(
         low_kernel,
-        out_shape=jax.ShapeDtypeStruct((640, 256), BF16 if before else F32),
-        in_specs=[VMEM] * (3 + len(before)),
-        out_specs=VMEM,
-        compiler_params=ROOM,
-        cost_estimate=cost(2 * 256 * 256 * (2560 + 640), 3_500_000),
-    )(basis, rows, grads, *before)
+        out_shape=jax.ShapeDtypeStruct((640, 256), BF16),
+        in_specs=[VMEM] * 3,
+        out_specs=VMEM,
+        compiler_params=ROOM,
+        cost_estimate=cost(2 * 512 * 256 * 640, 1_500_000),
+    )(reduced, rows, rows_other)
 
 
 def shards(x_heads, proj_weight, out_grad, proj_basis, first_moment, second_moment):
     core = lax.axis_index("core")
     half = proj_weight.shape[1]
-
     scalar = core.reshape(1).astype(jnp.int32)
-
-    grad_block = lax.all_gather(out_grad, "zl", axis=0, tiled=True)
 
     def own_columns(values):
         return lax.dynamic_slice_in_dim(values, core * 256, 256, 1)
 
-    moments = jnp.concatenate([own_columns(first_moment[0]), own_columns(second_moment[0])], 0)
-    moments = lax.ppermute(moments.astype(BF16), ("zh", "x"), TURN)
-
+    grad_block = lax.all_gather(out_grad, "zl", axis=0, tiled=True)
     weight_other = lax.ppermute(proj_weight, "core", CORE_SWAP)
+    grad_other = lax.ppermute(out_grad, "core", CORE_SWAP)
     x_other = lax.ppermute(x_heads, "core", CORE_SWAP)
-    by_zh = gather_zh(jnp.concatenate([own_columns(proj_basis), moments], 0))
-    by_zh, weight_other = lax.optimization_barrier((by_zh, weight_other))
-    m_old = by_zh[:, 40:50].reshape(40, 256)
-    v_old = by_zh[:, 50:].reshape(40, 256)
-    by_yx = spread(by_zh[:, :40].reshape(160, 256), ("y", "x"), 16)
+
+    by_zh = gather_zh(own_columns(proj_basis)).reshape(160, 256)
+    moments = [own_columns(first_moment[0]), own_columns(second_moment[0])]
+    by_yx = spread(jnp.concatenate([by_zh] + [m.astype(BF16) for m in moments], 0), ("y", "x"), 16)
+
     mixed_part = mixed_matmul(scalar, x_heads, proj_weight, weight_other)
-    by_yx, mixed_part, grad_block, x_other = lax.optimization_barrier(
-        (by_yx, mixed_part, grad_block, x_other)
+    by_yx, mixed_part, grad_other, x_other = lax.optimization_barrier(
+        (by_yx, mixed_part, grad_other, x_other)
     )
-    grad_other = lax.ppermute(grad_block, "core", CORE_SWAP)
+    moments = lax.dynamic_slice_in_dim(by_yx[:, 160:], 4 * lax.axis_index("y"), 4, 0)
+    by_yx = by_yx[:, :160]
     basis_cols = by_yx.reshape(4, 4, 4, 40, 256).transpose(0, 2, 1, 3, 4).reshape(2560, 256)
 
     mixed_out = lax.psum_scatter(mixed_part, "zl", scatter_dimension=0, tiled=True)
 
-    low_own = low_matmul(basis_cols, x_heads, grad_block)
-    low_chip = low_matmul(basis_cols, x_other, grad_other, low_own)
-
-    low_yx = lax.all_to_all(low_chip.reshape(16, 40, 256), ("y", "x"), 0, 0, tiled=True)
-    basis_cols, low_chip = lax.optimization_barrier((basis_cols, low_chip))
+    reduced = reduced_matmul(basis_cols, out_grad, grad_other)
+    reduced = lax.all_to_all(reduced, "zl", 0, 0, tiled=True)
     basis_own = lax.dynamic_slice_in_dim(basis_cols, core * half, half, 0)
     basis_other = lax.ppermute(
         lax.dynamic_slice_in_dim(basis_cols, (1 - core) * half, half, 0), "core", CORE_SWAP
     )
-    low_yx, basis_other = lax.optimization_barrier((low_yx, basis_other))
+    reduced, basis_other = lax.optimization_barrier((reduced, basis_other))
+
+    low_chip = low_matmul(reduced, x_heads, x_other)
+
+    low_yx = lax.all_to_all(low_chip.reshape(16, 40, 256), ("y", "x"), 0, 0, tiled=True)
+    moments, low_chip = lax.optimization_barrier((moments, low_chip))
+    moments = lax.ppermute(moments, ("zh", "x"), TURN)
+    low_yx, moments = lax.optimization_barrier((low_yx, moments))
+    m_old = moments[:, :10].reshape(40, 256)
+    v_old = moments[:, 10:].reshape(40, 256)
     low = sum_zh(jnp.sum(low_yx.astype(F32), 0))
 
     m_new = 0.9 * m_old.astype(F32) + 0.1 * low

time: 152 us -> 157 us (1.033)
  blocking collectives: 13.5 us -> 0 us
  starting transfers between devices: 81.8 us -> 93.5 us
  waiting for transfers between devices: 19.4 us -> 24.4 us
    all_to_all x1 -> x0, blocking collectives: 13.5 us -> none  [shards(): lax.all_to_all(low_chip.reshape(16, 40, 256), ('y', 'x'), 0, 0, tiled=True)]
    all_to_all x0 -> x2, starting transfers between devices: none -> 10.4 us  [the longest x1 5.82 us: shards(): reduced = lax.all_to_all(reduced, 'zl', 0, 0, tiled=True)]
    all_gather x1, waiting for transfers between devices: 9.18 us -> 0.02 us  [shards(): grad_block = lax.all_gather(out_grad, 'zl', axis=0, tiled=True)]
    all_to_all x2, waiting for transfers between devices: 3.18 us -> 11.5 us  [spread(): return lax.all_to_all(copies, axes, 0, 0, tiled=True)]
    all_to_all x2, starting transfers between devices: 11 us -> 17.6 us  [spread(): return lax.all_to_all(copies, axes, 0, 0, tiled=True)]
    all_to_all x0 -> x2, waiting for transfers between devices: none -> 6.24 us  [the longest x1 6.23 us: shards(): lax.all_to_all(low_chip.reshape(16, 40, 256), ('y', 'x'), 0, 0, tiled=True)]
    ppermute x1, starting transfers between devices: 15.1 us -> 9.16 us  [gather_zh(): got = lax.ppermute(pair, 'zh', MIRROR)]
    ppermute x1, starting transfers between devices: 8.79 us -> 2.87 us  [shards(): weight_other = lax.ppermute(proj_weight, 'core', CORE_SWAP)]
  transfers between devices with their start and end apart: 14 -> 16, of which waited for: 7 -> 8; matrix products, arithmetic and copies ran while one was open for 3% -> 4% of each run, Pallas kernels for 5% -> 5%
where the time goes in v3:
time: 157 us; the launch traced here: 155 us
  starting transfers between devices  93.5 us (60%)
  waiting for transfers between devices  24.4 us (16%)
  between operations  14.4 us (9%)
  local copies, waits for them, and re-layouts  10.7 us (7%)
  Pallas kernels  8 us (5%)
  matrix products  3.53 us (2%)
    ppermute x2, starting transfers between devices, sum_zh(): values = sent.astype(F32) + lax.ppermute(sent, 'zh', partners).astype(F32)  20.2 us
    all_to_all x2, starting transfers between devices, spread(): return lax.all_to_all(copies, axes, 0, 0, tiled=True)  17.6 us
    all_to_all x2, waiting for transfers between devices, spread(): return lax.all_to_all(copies, axes, 0, 0, tiled=True)  11.5 us
    ppermute x1, starting transfers between devices, shards(): rows_other = lax.ppermute(rows, 'core', CORE_SWAP)  9.74 us
    ppermute x1, starting transfers between devices, gather_zh(): got = lax.ppermute(values, 'zh', PAIR)  9.63 us
    ppermute x1, starting transfers between devices, gather_zh(): got = lax.ppermute(pair, 'zh', MIRROR)  9.16 us
    ppermute x1, starting transfers between devices, shards(): lax.ppermute(lax.dynamic_slice_in_dim(basis_cols, (1 - core) * half, half...  6.25 us
    all_to_all x1, waiting for transfers between devices, shards(): lax.all_to_all(low_chip.reshape(16, 40, 256), ('y', 'x'), 0, 0, tiled=True)  6.23 us
  transfers between devices with their start and end apart: 16, of which 8 were waited for; matrix products, arithmetic and copies ran while one was open for 4% of the time, Pallas kernels for 5%

profile of v3, /device:TPU:1, one launch (start us, length us, event | category | flops | bytes accessed | tf_op | source)
XLA Modules:
  0.0 155.4 jit_solution(8339234496443500731)
XLA Ops:
  8.0 9.6 %collective-permute-start = (bf16[40,256]{1,0:T(8,128)(2,1)S(1)}, bf16[40,256]{1,0:T(8,128)(2,1)S(1)}, u32[]{:S(2)}, u32[]{:S(2)}) collective-permute-start(bf16[40,256]{1,0:T(8,128)(2,1)S(1)} %constant_dynamic-slice_fusion.2), channel_id=1, source_target_pairs={{0,32},{32,0},{64,96},{96,64},{1,33},{33,1},{65,97},{97,65},{2,34}... | collective-permute-start | bytes 61448 | tf_op jit(solution)/shard_map/ppermute | solution.py:26
  17.6 2.9 %collective-permute-start.2 = (bf16[640,1280]{1,0:T(8,128)(2,1)}, bf16[640,1280]{1,0:T(8,128)(2,1)}, u32[]{:S(2)}, u32[]{:S(2)}) collective-permute-start(bf16[640,1280]{1,0:T(8,128)(2,1)} %own_ref.7), channel_id=1, source_target_pairs={{0,4},{4,0},{1,5},{5,1},{2,6},{6,2},{3,7},{7,3},{8,12},{12,8},{9,1... | collective-permute-start | bytes 4915208 | tf_op jit(solution)/shard_map/ppermute | solution.py:149
  20.5 0.7 broadcast_select_fusion.1
  21.3 9.2 %collective-permute-start.1 = (bf16[80,256]{1,0:T(8,128)(2,1)S(1)}, bf16[80,256]{1,0:T(8,128)(2,1)S(1)}, u32[]{:S(2)}, u32[]{:S(2)}) collective-permute-start(bf16[80,256]{1,0:T(8,128)(2,1)S(1)} %pad_maximum_fusion.2), channel_id=1, source_target_pairs={{0,96},{96,0},{32,64},{64,32},{1,97},{97,1},{33,65},{65,33},{2,98}... | collective-permute-start | bytes 122888 | tf_op jit(solution)/shard_map/ppermute | solution.py:29
  31.9 1.2 broadcast_in_dim.4
  33.2 6.9 %all-to-all-start = ((bf16[16,180,256]{2,1,0:T(8,128)(2,1)}), bf16[16,180,256]{2,1,0:T(8,128)(2,1)}, u32[]{:S(2)}, u32[]{:S(2)}) async-start(bf16[16,180,256]{2,1,0:T(8,128)(2,1)} %broadcast_in_dim.4), calls=%async_computation | async-start | bytes 3014656 | tf_op jit(solution)/shard_map/all_to_all | solution.py:21
  40.2 4.9 %collective-permute-start.4 = (bf16[256,640]{1,0:T(8,128)(2,1)S(1)}, bf16[256,640]{1,0:T(8,128)(2,1)S(1)}, u32[]{:S(2)}, u32[]{:S(2)}) collective-permute-start(bf16[256,640]{1,0:T(8,128)(2,1)S(1)} %copy-done.1), channel_id=1, source_target_pairs={{0,4},{4,0},{1,5},{5,1},{2,6},{6,2},{3,7},{7,3},{8,12},{12,8},{9,1... | collective-permute-start | bytes 983048 | tf_op jit(solution)/shard_map/ppermute | solution.py:151
  45.1 1.9 %collective-permute-start.3 = (bf16[64,2560]{1,0:T(8,128)(2,1)S(1)}, bf16[64,2560]{1,0:T(8,128)(2,1)S(1)}, u32[]{:S(2)}, u32[]{:S(2)}) collective-permute-start(bf16[64,2560]{1,0:T(8,128)(2,1)S(1)} %copy-done.3), channel_id=1, source_target_pairs={{0,4},{4,0},{1,5},{5,1},{2,6},{6,2},{3,7},{7,3},{8,12},{12,8},{9,1... | collective-permute-start | bytes 983048 | tf_op jit(solution)/shard_map/ppermute | solution.py:150
  47.1 3.7 %shard_map.85 = bf16[256,2560]{1,0:T(8,128)(2,1)} custom-call(s32[1]{0:T(128)} %bitcast.3.core_ref, bf16[256,640]{1,0:T(8,128)(2,1)S(1)} %copy-done.1, bf16[640,1280]{1,0:T(8,128)(2,1)S(1)} %copy-done, bf16[640,1280]{1,0:T(8,128)(2,1)} %collective-permute-done.2.other_ref), custom_call_target="tpu_custom_call" | custom-call | flops 838860800 | bytes 5000000 | tf_op jit(solution)/shard_map/pallas_call | solution.py:64
  50.8 8.4 %all-to-all-done = bf16[16,180,256]{2,1,0:T(8,128)(2,1)} async-done(((bf16[16,180,256]{2,1,0:T(8,128)(2,1)}), bf16[16,180,256]{2,1,0:T(8,128)(2,1)}, u32[]{:S(2)}, u32[]{:S(2)}) %all-to-all-start) | async-done | bytes 1474592 | tf_op jit(solution)/shard_map/all_to_all | solution.py:21
  59.2 1.4 slice.12
  60.8 0.8 copy-done.4
  63.0 5.8 %all-to-all-start.1 = ((bf16[4,2,64,256]{3,2,1,0:T(8,128)(2,1)}), bf16[4,2,64,256]{3,2,1,0:T(8,128)(2,1)S(1)}, u32[]{:S(2)}, u32[]{:S(2)}) async-start(bf16[4,2,64,256]{3,2,1,0:T(8,128)(2,1)} %copy-done.6), calls=%async_computation.1 | async-start | bytes 524288 | tf_op jit(solution)/shard_map/all_to_all | solution.py:168
  68.8 6.3 %collective-permute-start.5 = (bf16[1280,256]{1,0:T(8,128)(2,1)S(1)}, bf16[1280,256]{1,0:T(8,128)(2,1)}, u32[]{:S(2)}, u32[]{:S(2)}) collective-permute-start(bf16[1280,256]{1,0:T(8,128)(2,1)S(1)} %constant_dynamic-slice_fusion.1), channel_id=1, source_target_pairs={{0,4},{4,0},{1,5},{5,1},{2,6},{6,2},{3,7},{7,3},{8,12},{12,8},{9,1... | collective-permute-start | bytes 1966088 | tf_op jit(solution)/shard_map/ppermute | solution.py:170
  75.1 1.8 %collective-permute-done.5 = bf16[1280,256]{1,0:T(8,128)(2,1)} collective-permute-done((bf16[1280,256]{1,0:T(8,128)(2,1)S(1)}, bf16[1280,256]{1,0:T(8,128)(2,1)}, u32[]{:S(2)}, u32[]{:S(2)}) %collective-permute-start.5) | collective-permute-done | bytes 655392 | tf_op jit(solution)/shard_map/ppermute | solution.py:170
  76.9 1.0 copy-done.10
  79.0 4.6 %all-to-all-start.2 = ((bf16[16,40,256]{2,1,0:T(8,128)(2,1)}), bf16[16,40,256]{2,1,0:T(8,128)(2,1)S(1)}, u32[]{:S(2)}, u32[]{:S(2)}) async-start(bf16[16,40,256]{2,1,0:T(8,128)(2,1)} %bitcast.24), calls=%async_computation.2 | async-start | bytes 655360 | tf_op jit(solution)/shard_map/all_to_all | solution.py:177
  83.6 0.9 slice.13
  85.3 6.2 %all-to-all-done.2 = bf16[16,40,256]{2,1,0:T(8,128)(2,1)S(1)} async-done(((bf16[16,40,256]{2,1,0:T(8,128)(2,1)}), bf16[16,40,256]{2,1,0:T(8,128)(2,1)S(1)}, u32[]{:S(2)}, u32[]{:S(2)}) %all-to-all-start.2) | async-done | bytes 327712 | tf_op jit(solution)/shard_map/all_to_all | solution.py:177
  91.6 7.4 %collective-permute-start.7 = (bf16[40,256]{1,0:T(8,128)(2,1)S(1)}, bf16[40,256]{1,0:T(8,128)(2,1)S(1)}, u32[]{:S(2)}, u32[]{:S(2)}) collective-permute-start(bf16[40,256]{1,0:T(8,128)(2,1)S(1)} %reduce_sum.12), channel_id=1, source_target_pairs={{0,32},{32,0},{64,96},{96,64},{1,33},{33,1},{65,97},{97,65},{2,34}... | collective-permute-start | bytes 61448 | tf_op jit(solution)/shard_map/ppermute | solution.py:38
  99.0 1.6 %collective-permute-done.7 = bf16[40,256]{1,0:T(8,128)(2,1)S(1)} collective-permute-done((bf16[40,256]{1,0:T(8,128)(2,1)S(1)}, bf16[40,256]{1,0:T(8,128)(2,1)S(1)}, u32[]{:S(2)}, u32[]{:S(2)}) %collective-permute-start.7) | collective-permute-done | bytes 20512 | tf_op jit(solution)/shard_map/ppermute | solution.py:38
  100.6 12.8 %collective-permute-start.8 = (bf16[40,256]{1,0:T(8,128)(2,1)S(1)}, bf16[40,256]{1,0:T(8,128)(2,1)S(1)}, u32[]{:S(2)}, u32[]{:S(2)}) collective-permute-start(bf16[40,256]{1,0:T(8,128)(2,1)S(1)} %add_convert_fusion), channel_id=1, source_target_pairs={{0,96},{96,0},{32,64},{64,32},{1,97},{97,1},{33,65},{65,33},{2,98}... | collective-permute-start | bytes 61448 | tf_op jit(solution)/shard_map/ppermute | solution.py:38
  113.5 1.2 collective-permute-done.8
  114.7 0.7 broadcast_in_dim.5
  115.5 10.7 %all-to-all-start.3 = ((bf16[16,40,256]{2,1,0:T(8,128)(2,1)}), bf16[16,40,256]{2,1,0:T(8,128)(2,1)S(1)}, u32[]{:S(2)}, u32[]{:S(2)}) async-start(bf16[16,40,256]{2,1,0:T(8,128)(2,1)} %broadcast_in_dim.5), calls=%async_computation.3 | async-start | bytes 655360 | tf_op jit(solution)/shard_map/all_to_all | solution.py:21
  126.2 1.3 copy-done.2
  127.5 3.4 %shard_map.88 = bf16[256,640]{1,0:T(8,128)(2,1)} custom-call(s32[1]{0:T(128)} %bitcast.3.core_ref, bf16[256,2560]{1,0:T(8,128)(2,1)S(1)} %copy-done.2, bf16[640,1280]{1,0:T(8,128)(2,1)S(1)} %copy-done, bf16[640,1280]{1,0:T(8,128)(2,1)} %collective-permute-done.2.other_ref), custom_call_target="tpu_custom_call" | custom-call | flops 838860800 | bytes 5000000 | tf_op jit(solution)/shard_map/pallas_call | solution.py:90
  130.9 3.2 %all-to-all-done.3 = bf16[16,40,256]{2,1,0:T(8,128)(2,1)S(1)} async-done(((bf16[16,40,256]{2,1,0:T(8,128)(2,1)}), bf16[16,40,256]{2,1,0:T(8,128)(2,1)S(1)}, u32[]{:S(2)}, u32[]{:S(2)}) %all-to-all-start.3) | async-done | bytes 327712 | tf_op jit(solution)/shard_map/all_to_all | solution.py:21
  134.1 9.7 %collective-permute-start.9 = (bf16[640,256]{1,0:T(8,128)(2,1)S(1)}, bf16[640,256]{1,0:T(8,128)(2,1)S(1)}, u32[]{:S(2)}, u32[]{:S(2)}) collective-permute-start(bf16[640,256]{1,0:T(8,128)(2,1)S(1)} %bitcast.26), channel_id=1, source_target_pairs={{0,4},{4,0},{1,5},{5,1},{2,6},{6,2},{3,7},{7,3},{8,12},{12,8},{9,1... | collective-permute-start | bytes 983048 | tf_op jit(solution)/shard_map/ppermute | solution.py:194
  143.8 1.2 collective-permute-done.9
  145.1 1.7 %fusion.9 = f32[640,1280]{1,0:T(8,128)S(1)} fusion(bf16[640,256]{1,0:T(8,128)(2,1)S(1)} %collective-permute-done.9, bf16[1280,256]{1,0:T(8,128)(2,1)} %collective-permute-done.5), kind=kOutput, calls=%fused_computation.28 | convolution fusion | flops 419430400 | bytes 4259840 | tf_op jit(solution)/shard_map/dot_general | solution.py:197
  146.8 1.8 %fusion = bf16[640,1280]{1,0:T(8,128)(2,1)} fusion(f32[640,1280]{1,0:T(8,128)S(1)} %fusion.9, bf16[640,256]{1,0:T(8,128)(2,1)S(1)} %bitcast.27, bf16[2560,256]{1,0:T(8,128)(2,1)S(1)} %bitcast.23, s32[]{:T(128)S(6)} %select_n.55), kind=kOutput, calls=%fused_computation.1 | convolution fusion | flops 421068800 | bytes 5898244 | tf_op jit(solution)/shard_map/dot_general | solution.py:197
  (52 shorter events, 5.8 us)
Async XLA Ops:
  7.2 119.1 %all-gather.2.cloned.1.call-start = ((), (), s32[]{:S(2)}) async-start(), calls=%async_computation.5 | async-start | bytes 1638400 | tf_op jit(solution)/shard_map/all_gather | solution.py:148
  8.0 12.6 %collective-permute-start = (bf16[40,256]{1,0:T(8,128)(2,1)S(1)}, bf16[40,256]{1,0:T(8,128)(2,1)S(1)}, u32[]{:S(2)}, u32[]{:S(2)}) collective-permute-start(bf16[40,256]{1,0:T(8,128)(2,1)S(1)} %constant_dynamic-slice_fusion.2), channel_id=1, source_target_pairs={{0,32},{32,0},{64,96},{96,64},{1,33},{33,1},{65,97},{97,65},{2,34}... | collective-permute-start | bytes 61448 | tf_op jit(solution)/shard_map/ppermute | solution.py:26
  17.6 29.4 %collective-permute-start.2 = (bf16[640,1280]{1,0:T(8,128)(2,1)}, bf16[640,1280]{1,0:T(8,128)(2,1)}, u32[]{:S(2)}, u32[]{:S(2)}) collective-permute-start(bf16[640,1280]{1,0:T(8,128)(2,1)} %own_ref.7), channel_id=1, source_target_pairs={{0,4},{4,0},{1,5},{5,1},{2,6},{6,2},{3,7},{7,3},{8,12},{12,8},{9,1... | collective-permute-start | bytes 4915208 | tf_op jit(solution)/shard_map/ppermute | solution.py:149
  21.3 10.6 %collective-permute-start.1 = (bf16[80,256]{1,0:T(8,128)(2,1)S(1)}, bf16[80,256]{1,0:T(8,128)(2,1)S(1)}, u32[]{:S(2)}, u32[]{:S(2)}) collective-permute-start(bf16[80,256]{1,0:T(8,128)(2,1)S(1)} %pad_maximum_fusion.2), channel_id=1, source_target_pairs={{0,96},{96,0},{32,64},{64,32},{1,97},{97,1},{33,65},{65,33},{2,98}... | collective-permute-start | bytes 122888 | tf_op jit(solution)/shard_map/ppermute | solution.py:29
  33.2 7.0 %copy-start.1 = (bf16[256,640]{1,0:T(8,128)(2,1)S(1)}, bf16[256,640]{1,0:T(8,128)(2,1)}, u32[]{:S(2)}) copy-start(bf16[256,640]{1,0:T(8,128)(2,1)} %own_ref.6) | copy-start | bytes 983044
  33.2 11.9 %copy-start.3 = (bf16[64,2560]{1,0:T(8,128)(2,1)S(1)}, bf16[64,2560]{1,0:T(8,128)(2,1)}, u32[]{:S(2)}) copy-start(bf16[64,2560]{1,0:T(8,128)(2,1)} %own_ref.5) | copy-start | bytes 983044
  33.2 13.9 %copy-start = (bf16[640,1280]{1,0:T(8,128)(2,1)S(1)}, bf16[640,1280]{1,0:T(8,128)(2,1)}, u32[]{:S(2)}) copy-start(bf16[640,1280]{1,0:T(8,128)(2,1)} %own_ref.7) | copy-start | bytes 4915204
  33.2 26.0 %all-to-all-start = ((bf16[16,180,256]{2,1,0:T(8,128)(2,1)}), bf16[16,180,256]{2,1,0:T(8,128)(2,1)}, u32[]{:S(2)}, u32[]{:S(2)}) async-start(bf16[16,180,256]{2,1,0:T(8,128)(2,1)} %broadcast_in_dim.4), calls=%async_computation | async-start | bytes 3014656 | tf_op jit(solution)/shard_map/all_to_all | solution.py:21
  40.1 94.0 %reduce-scatter.2.cloned.1.call-start = ((), (), s32[]{:S(2)}) async-start(), calls=%async_computation.6 | async-start | bytes 1638400 | tf_op jit(solution)/shard_map/reduce_scatter | solution.py:165
  40.2 10.6 %collective-permute-start.4 = (bf16[256,640]{1,0:T(8,128)(2,1)S(1)}, bf16[256,640]{1,0:T(8,128)(2,1)S(1)}, u32[]{:S(2)}, u32[]{:S(2)}) collective-permute-start(bf16[256,640]{1,0:T(8,128)(2,1)S(1)} %copy-done.1), channel_id=1, source_target_pairs={{0,4},{4,0},{1,5},{5,1},{2,6},{6,2},{3,7},{7,3},{8,12},{12,8},{9,1... | collective-permute-start | bytes 983048 | tf_op jit(solution)/shard_map/ppermute | solution.py:151
  45.1 5.7 %collective-permute-start.3 = (bf16[64,2560]{1,0:T(8,128)(2,1)S(1)}, bf16[64,2560]{1,0:T(8,128)(2,1)S(1)}, u32[]{:S(2)}, u32[]{:S(2)}) collective-permute-start(bf16[64,2560]{1,0:T(8,128)(2,1)S(1)} %copy-done.3), channel_id=1, source_target_pairs={{0,4},{4,0},{1,5},{5,1},{2,6},{6,2},{3,7},{7,3},{8,12},{12,8},{9,1... | collective-permute-start | bytes 983048 | tf_op jit(solution)/shard_map/ppermute | solution.py:150
  50.8 9.8 %copy-start.9 = (bf16[256,640]{1,0:T(8,128)(2,1)}, bf16[256,640]{1,0:T(8,128)(2,1)S(1)}, u32[]{:S(2)}) copy-start(bf16[256,640]{1,0:T(8,128)(2,1)S(1)} %collective-permute-done.4.other_ref) | copy-start | bytes 983044
  50.8 9.8 %copy-start.7 = (bf16[64,2560]{1,0:T(8,128)(2,1)}, bf16[64,2560]{1,0:T(8,128)(2,1)S(1)}, u32[]{:S(2)}) copy-start(bf16[64,2560]{1,0:T(8,128)(2,1)S(1)} %collective-permute-done.3.other_ref) | copy-start | bytes 983044
  60.6 1.0 copy-start.4
  60.6 1.1 copy-start.8
  62.3 0.7 copy-start.6
  63.0 14.0 %all-to-all-start.1 = ((bf16[4,2,64,256]{3,2,1,0:T(8,128)(2,1)}), bf16[4,2,64,256]{3,2,1,0:T(8,128)(2,1)S(1)}, u32[]{:S(2)}, u32[]{:S(2)}) async-start(bf16[4,2,64,256]{3,2,1,0:T(8,128)(2,1)} %copy-done.6), calls=%async_computation.1 | async-start | bytes 524288 | tf_op jit(solution)/shard_map/all_to_all | solution.py:168
  68.8 8.1 %collective-permute-start.5 = (bf16[1280,256]{1,0:T(8,128)(2,1)S(1)}, bf16[1280,256]{1,0:T(8,128)(2,1)}, u32[]{:S(2)}, u32[]{:S(2)}) collective-permute-start(bf16[1280,256]{1,0:T(8,128)(2,1)S(1)} %constant_dynamic-slice_fusion.1), channel_id=1, source_target_pairs={{0,4},{4,0},{1,5},{5,1},{2,6},{6,2},{3,7},{7,3},{8,12},{12,8},{9,1... | collective-permute-start | bytes 1966088 | tf_op jit(solution)/shard_map/ppermute | solution.py:170
  76.9 1.0 copy-start.10
  78.3 0.7 copy-start.5
  79.0 12.5 %all-to-all-start.2 = ((bf16[16,40,256]{2,1,0:T(8,128)(2,1)}), bf16[16,40,256]{2,1,0:T(8,128)(2,1)S(1)}, u32[]{:S(2)}, u32[]{:S(2)}) async-start(bf16[16,40,256]{2,1,0:T(8,128)(2,1)} %bitcast.24), calls=%async_computation.2 | async-start | bytes 655360 | tf_op jit(solution)/shard_map/all_to_all | solution.py:177
  84.6 0.7 collective-permute-start.6
  91.6 9.0 %collective-permute-start.7 = (bf16[40,256]{1,0:T(8,128)(2,1)S(1)}, bf16[40,256]{1,0:T(8,128)(2,1)S(1)}, u32[]{:S(2)}, u32[]{:S(2)}) collective-permute-start(bf16[40,256]{1,0:T(8,128)(2,1)S(1)} %reduce_sum.12), channel_id=1, source_target_pairs={{0,32},{32,0},{64,96},{96,64},{1,33},{33,1},{65,97},{97,65},{2,34}... | collective-permute-start | bytes 61448 | tf_op jit(solution)/shard_map/ppermute | solution.py:38
  100.6 14.1 %collective-permute-start.8 = (bf16[40,256]{1,0:T(8,128)(2,1)S(1)}, bf16[40,256]{1,0:T(8,128)(2,1)S(1)}, u32[]{:S(2)}, u32[]{:S(2)}) collective-permute-start(bf16[40,256]{1,0:T(8,128)(2,1)S(1)} %add_convert_fusion), channel_id=1, source_target_pairs={{0,96},{96,0},{32,64},{64,32},{1,97},{97,1},{33,65},{65,33},{2,98}... | collective-permute-start | bytes 61448 | tf_op jit(solution)/shard_map/ppermute | solution.py:38
  115.5 18.6 %all-to-all-start.3 = ((bf16[16,40,256]{2,1,0:T(8,128)(2,1)}), bf16[16,40,256]{2,1,0:T(8,128)(2,1)S(1)}, u32[]{:S(2)}, u32[]{:S(2)}) async-start(bf16[16,40,256]{2,1,0:T(8,128)(2,1)} %broadcast_in_dim.5), calls=%async_computation.3 | async-start | bytes 655360 | tf_op jit(solution)/shard_map/all_to_all | solution.py:21
  126.2 1.3 copy-start.2
  134.1 11.0 %collective-permute-start.9 = (bf16[640,256]{1,0:T(8,128)(2,1)S(1)}, bf16[640,256]{1,0:T(8,128)(2,1)S(1)}, u32[]{:S(2)}, u32[]{:S(2)}) collective-permute-start(bf16[640,256]{1,0:T(8,128)(2,1)S(1)} %bitcast.26), channel_id=1, source_target_pairs={{0,4},{4,0},{1,5},{5,1},{2,6},{6,2},{3,7},{7,3},{8,12},{12,8},{9,1... | collective-permute-start | bytes 983048 | tf_op jit(solution)/shard_map/ppermute | solution.py:194
Sparse Core Ops, SparseCore 0:
  17.7 42.4 all-gather.1
  63.7 45.8 reduce-scatter.1

commit v4 on v3

--- a/solution.py
+++ b/solution.py
@@ -1,5 +1,6 @@
 import jax
 import jax.numpy as jnp
+import numpy as np
 from jax import lax
 from jax.experimental import pallas as pl
 from jax.experimental.pallas import tpu as pltpu
@@ -13,7 +14,7 @@
 CORE_SWAP = [(0, 1), (1, 0)]
 PAIR = [(0, 1), (1, 0), (2, 3), (3, 2)]
 MIRROR = [(0, 3), (3, 0), (1, 2), (2, 1)]
-TURN = [(a * 4 + b, b * 4 + a) for a in range(4) for b in range(4)]
+ORDER = np.eye(640, dtype=np.float32).reshape(640, 4, 4, 4, 10).transpose(0, 1, 3, 2, 4).reshape(640, 640)
 
 
 def spread(values, axes, count):
@@ -115,7 +116,7 @@
     )(basis, grads, grads_other)
 
 
-def low_kernel(reduced_ref, own_ref, other_ref, out_ref):
+def low_kernel(reduced_ref, own_ref, other_ref, order_ref, out_ref):
     total = None
     for which, rows in ((0, own_ref), (1, other_ref)):
         reduced = reduced_ref[:, which].reshape(256, 256)
@@ -123,18 +124,44 @@
             rows[...], reduced, (((0,), (0,)), ((), ())), preferred_element_type=F32
         )
         total = part if total is None else total + part
-    out_ref[...] = total.astype(BF16)
-
-
-def low_matmul(reduced, rows, rows_other):
+    ordered = lax.dot_general(
+        order_ref[...], total.astype(BF16), (((0,), (0,)), ((), ())), preferred_element_type=F32
+    )
+    out_ref[...] = ordered.astype(BF16)
+
+
+def low_matmul(reduced, rows, rows_other, order):
     return pl.pallas_call(
         low_kernel,
         out_shape=jax.ShapeDtypeStruct((640, 256), BF16),
-        in_specs=[VMEM] * 3,
-        out_specs=VMEM,
-        compiler_params=ROOM,
-        cost_estimate=cost(2 * 512 * 256 * 640, 1_500_000),
-    )(reduced, rows, rows_other)
+        in_specs=[VMEM] * 4,
+        out_specs=VMEM,
+        compiler_params=ROOM,
+        cost_estimate=cost(2 * 640 * 256 * (512 + 640), 2_300_000),
+    )(reduced, rows, rows_other, order)
+
+
+def update_kernel(own_ref, other_ref, order_ref, basis_ref, basis_other_ref, out_ref):
+    total = None
+    for rows, basis in ((own_ref, basis_ref), (other_ref, basis_other_ref)):
+        direction = jnp.dot(order_ref[...], rows[...], preferred_element_type=F32).astype(BF16)
+        part = lax.dot_general(
+            direction, basis[...], (((1,), (1,)), ((), ())), preferred_element_type=F32
+        )
+        total = part if total is None else total + part
+    out_ref[...] = total.astype(BF16)
+
+
+def update_matmul(rows, rows_other, order, basis, basis_other):
+    half = basis.shape[0]
+    return pl.pallas_call(
+        update_kernel,
+        out_shape=jax.ShapeDtypeStruct((640, half), BF16),
+        in_specs=[VMEM] * 5,
+        out_specs=VMEM,
+        compiler_params=ROOM,
+        cost_estimate=cost(2 * 640 * 512 * (640 + half), 5_000_000),
+    )(rows, rows_other, order, basis, basis_other)
 
 
 def shards(x_heads, proj_weight, out_grad, proj_basis, first_moment, second_moment):
@@ -150,16 +177,16 @@
     grad_other = lax.ppermute(out_grad, "core", CORE_SWAP)
     x_other = lax.ppermute(x_heads, "core", CORE_SWAP)
 
-    by_zh = gather_zh(own_columns(proj_basis)).reshape(160, 256)
-    moments = [own_columns(first_moment[0]), own_columns(second_moment[0])]
-    by_yx = spread(jnp.concatenate([by_zh] + [m.astype(BF16) for m in moments], 0), ("y", "x"), 16)
+    parts = [proj_basis, first_moment[0].astype(BF16), second_moment[0].astype(BF16)]
+    by_zh = gather_zh(jnp.concatenate([own_columns(part) for part in parts], 0))
+    m_old = by_zh[:, 40:50].reshape(40, 256)
+    v_old = by_zh[:, 50:].reshape(40, 256)
+    by_yx = spread(by_zh[:, :40].reshape(160, 256), ("y", "x"), 16)
 
     mixed_part = mixed_matmul(scalar, x_heads, proj_weight, weight_other)
-    by_yx, mixed_part, grad_other, x_other = lax.optimization_barrier(
-        (by_yx, mixed_part, grad_other, x_other)
-    )
-    moments = lax.dynamic_slice_in_dim(by_yx[:, 160:], 4 * lax.axis_index("y"), 4, 0)
-    by_yx = by_yx[:, :160]
+    by_yx, mixed_part, grad_other, x_other, m_old, v_old = lax.optimization_barrier(
+        (by_yx, mixed_part, grad_other, x_other, m_old, v_old)
+    )
     basis_cols = by_yx.reshape(4, 4, 4, 40, 256).transpose(0, 2, 1, 3, 4).reshape(2560, 256)
 
     mixed_out = lax.psum_scatter(mixed_part, "zl", scatter_dimension=0, tiled=True)
@@ -172,14 +199,10 @@
     )
     reduced, basis_other = lax.optimization_barrier((reduced, basis_other))
 
-    low_chip = low_matmul(reduced, x_heads, x_other)
+    order = jnp.asarray(ORDER, BF16)
+    low_chip = low_matmul(reduced, x_heads, x_other, order)
 
     low_yx = lax.all_to_all(low_chip.reshape(16, 40, 256), ("y", "x"), 0, 0, tiled=True)
-    moments, low_chip = lax.optimization_barrier((moments, low_chip))
-    moments = lax.ppermute(moments, ("zh", "x"), TURN)
-    low_yx, moments = lax.optimization_barrier((low_yx, moments))
-    m_old = moments[:, :10].reshape(40, 256)
-    v_old = moments[:, 10:].reshape(40, 256)
     low = sum_zh(jnp.sum(low_yx.astype(F32), 0))
 
     m_new = 0.9 * m_old.astype(F32) + 0.1 * low
@@ -193,10 +216,7 @@
     rows, head_rows, mixed_out = lax.optimization_barrier((rows, head_rows, mixed_out))
     rows_other = lax.ppermute(rows, "core", CORE_SWAP)
 
-    def half_update(columns, basis):
-        return lax.dot_general(columns, basis, (((1,), (1,)), ((), ())), preferred_element_type=F32)
-
-    update = (half_update(rows, basis_own) + half_update(rows_other, basis_other)).astype(BF16)
+    update = update_matmul(rows, rows_other, order, basis_own, basis_other)
     return (mixed_out, head_rows, update)
 
 

time: 157 us -> 146 us (0.930)
  starting transfers between devices: 93.5 us -> 71.7 us
  blocking collectives: 0 us -> 11.8 us
  Pallas kernels: 8 us -> 12.7 us
  matrix products: 3.53 us -> 0 us
  waiting for transfers between devices: 24.4 us -> 22.2 us
    ppermute x2, starting transfers between devices: 20.2 us -> 7.53 us  [sum_zh(): values = sent.astype(F32) + lax.ppermute(sent, 'zh', partners).astype(F32)]
    all_to_all x0 -> x1, blocking collectives: none -> 11.8 us  [shards(): lax.all_to_all(low_chip.reshape(16, 40, 256), ('y', 'x'), 0, 0, tiled=True)]
    all_to_all x2, starting transfers between devices: 17.6 us -> 10.6 us  [spread(): return lax.all_to_all(copies, axes, 0, 0, tiled=True)]
    ppermute x2, waiting for transfers between devices: 2.8 us -> 9.45 us  [sum_zh(): values = sent.astype(F32) + lax.ppermute(sent, 'zh', partners).astype(F32)]
    all_to_all x1 -> x0, waiting for transfers between devices: 6.23 us -> none  [shards(): lax.all_to_all(low_chip.reshape(16, 40, 256), ('y', 'x'), 0, 0, tiled=True)]
    all_to_all x1 -> x0, starting transfers between devices: 4.62 us -> none  [shards(): lax.all_to_all(low_chip.reshape(16, 40, 256), ('y', 'x'), 0, 0, tiled=True)]
    all_to_all x1, starting transfers between devices: 5.82 us -> 9.59 us  [shards(): reduced = lax.all_to_all(reduced, 'zl', 0, 0, tiled=True)]
    all_to_all x2, waiting for transfers between devices: 11.5 us -> 7.81 us  [spread(): return lax.all_to_all(copies, axes, 0, 0, tiled=True)]
  transfers between devices with their start and end apart: 16 -> 14, of which waited for: 8 -> 7; matrix products, arithmetic and copies ran while one was open for 4% -> 3% of each run, Pallas kernels for 5% -> 7%
where the time goes in v4:
time: 146 us; the launch traced here: 145 us
  starting transfers between devices  71.7 us (49%)
  waiting for transfers between devices  22.2 us (15%)
  between operations  14.4 us (10%)
  Pallas kernels  12.7 us (9%)
  local copies, waits for them, and re-layouts  12.1 us (8%)
  blocking collectives  11.8 us (8%)
    all_to_all x1, blocking collectives, shards(): lax.all_to_all(low_chip.reshape(16, 40, 256), ('y', 'x'), 0, 0, tiled=True)  11.8 us
    all_to_all x2, starting transfers between devices, spread(): return lax.all_to_all(copies, axes, 0, 0, tiled=True)  10.6 us
    ppermute x1, starting transfers between devices, gather_zh(): got = lax.ppermute(values, 'zh', PAIR)  9.65 us
    all_to_all x1, starting transfers between devices, shards(): reduced = lax.all_to_all(reduced, 'zl', 0, 0, tiled=True)  9.59 us
    ppermute x2, waiting for transfers between devices, sum_zh(): values = sent.astype(F32) + lax.ppermute(sent, 'zh', partners).astype(F32)  9.45 us
    ppermute x1, starting transfers between devices, gather_zh(): got = lax.ppermute(pair, 'zh', MIRROR)  9.28 us
    ppermute x1, starting transfers between devices, shards(): rows_other = lax.ppermute(rows, 'core', CORE_SWAP)  8.97 us
    all_to_all x2, waiting for transfers between devices, spread(): return lax.all_to_all(copies, axes, 0, 0, tiled=True)  7.81 us
  transfers between devices with their start and end apart: 14, of which 7 were waited for; matrix products, arithmetic and copies ran while one was open for 3% of the time, Pallas kernels for 7%

profile of v4, /device:TPU:1, one launch (start us, length us, event | category | flops | bytes accessed | tf_op | source)
XLA Modules:
  0.0 145.1 jit_solution(8275262085279822667)
XLA Ops:
  8.7 9.6 %collective-permute-start = (bf16[60,256]{1,0:T(8,128)(2,1)S(1)}, bf16[60,256]{1,0:T(8,128)(2,1)S(1)}, u32[]{:S(2)}, u32[]{:S(2)}) collective-permute-start(bf16[60,256]{1,0:T(8,128)(2,1)S(1)} %pad_maximum_fusion.2), channel_id=1, source_target_pairs={{0,32},{32,0},{64,96},{96,64},{1,33},{33,1},{65,97},{97,65},{2,34}... | collective-permute-start | bytes 92168 | tf_op jit(solution)/shard_map/ppermute | solution.py:27
  18.4 2.9 %collective-permute-start.2 = (bf16[640,1280]{1,0:T(8,128)(2,1)}, bf16[640,1280]{1,0:T(8,128)(2,1)}, u32[]{:S(2)}, u32[]{:S(2)}) collective-permute-start(bf16[640,1280]{1,0:T(8,128)(2,1)} %own_ref.7), channel_id=1, source_target_pairs={{0,4},{4,0},{1,5},{5,1},{2,6},{6,2},{3,7},{7,3},{8,12},{12,8},{9,1... | collective-permute-start | bytes 4915208 | tf_op jit(solution)/shard_map/ppermute | solution.py:176
  21.4 9.3 %collective-permute-start.1 = (bf16[120,256]{1,0:T(8,128)(2,1)S(1)}, bf16[120,256]{1,0:T(8,128)(2,1)S(1)}, u32[]{:S(2)}, u32[]{:S(2)}) collective-permute-start(bf16[120,256]{1,0:T(8,128)(2,1)S(1)} %pad_maximum_fusion.1), channel_id=1, source_target_pairs={{0,96},{96,0},{32,64},{64,32},{1,97},{97,1},{33,65},{65,33},{2,98}... | collective-permute-start | bytes 184328 | tf_op jit(solution)/shard_map/ppermute | solution.py:30
  30.6 1.9 %collective-permute-done.1 = bf16[120,256]{1,0:T(8,128)(2,1)S(1)} collective-permute-done((bf16[120,256]{1,0:T(8,128)(2,1)S(1)}, bf16[120,256]{1,0:T(8,128)(2,1)S(1)}, u32[]{:S(2)}, u32[]{:S(2)}) %collective-permute-start.1) | collective-permute-done | bytes 61472 | tf_op jit(solution)/shard_map/ppermute | solution.py:30
  32.6 1.2 broadcast_in_dim.14
  33.9 6.9 %all-to-all-start = ((bf16[16,160,256]{2,1,0:T(8,128)(2,1)}), bf16[16,160,256]{2,1,0:T(8,128)(2,1)}, u32[]{:S(2)}, u32[]{:S(2)}) async-start(bf16[16,160,256]{2,1,0:T(8,128)(2,1)} %broadcast_in_dim.14), calls=%async_computation | async-start | bytes 2621440 | tf_op jit(solution)/shard_map/all_to_all | solution.py:22
  40.9 5.8 %collective-permute-start.4 = (bf16[256,640]{1,0:T(8,128)(2,1)S(1)}, bf16[256,640]{1,0:T(8,128)(2,1)S(1)}, u32[]{:S(2)}, u32[]{:S(2)}) collective-permute-start(bf16[256,640]{1,0:T(8,128)(2,1)S(1)} %copy-done.2), channel_id=1, source_target_pairs={{0,4},{4,0},{1,5},{5,1},{2,6},{6,2},{3,7},{7,3},{8,12},{12,8},{9,1... | collective-permute-start | bytes 983048 | tf_op jit(solution)/shard_map/ppermute | solution.py:178
  46.7 1.9 %collective-permute-start.3 = (bf16[64,2560]{1,0:T(8,128)(2,1)S(1)}, bf16[64,2560]{1,0:T(8,128)(2,1)S(1)}, u32[]{:S(2)}, u32[]{:S(2)}) collective-permute-start(bf16[64,2560]{1,0:T(8,128)(2,1)S(1)} %copy-done.4), channel_id=1, source_target_pairs={{0,4},{4,0},{1,5},{5,1},{2,6},{6,2},{3,7},{7,3},{8,12},{12,8},{9,1... | collective-permute-start | bytes 983048 | tf_op jit(solution)/shard_map/ppermute | solution.py:177
  48.7 3.7 %shard_map.94 = bf16[256,2560]{1,0:T(8,128)(2,1)} custom-call(s32[1]{0:T(128)} %bitcast.3.core_ref, bf16[256,640]{1,0:T(8,128)(2,1)S(1)} %copy-done.2, bf16[640,1280]{1,0:T(8,128)(2,1)S(1)} %copy-done.1, bf16[640,1280]{1,0:T(8,128)(2,1)} %collective-permute-done.2.other_ref), custom_call_target="tpu_custom_call" | custom-call | flops 838860800 | bytes 5000000 | tf_op jit(solution)/shard_map/pallas_call | solution.py:65
  52.5 4.7 %all-to-all-done = bf16[16,160,256]{2,1,0:T(8,128)(2,1)} async-done(((bf16[16,160,256]{2,1,0:T(8,128)(2,1)}), bf16[16,160,256]{2,1,0:T(8,128)(2,1)}, u32[]{:S(2)}, u32[]{:S(2)}) %all-to-all-start) | async-done | bytes 1310752 | tf_op jit(solution)/shard_map/all_to_all | solution.py:22
  57.3 1.5 %copy.10 = bf16[4,4,4,40,256]{4,3,2,1,0:T(8,128)(2,1)S(1)} copy(bf16[4,4,4,40,256]{4,3,1,2,0:T(8,128)(2,1)} %bitcast.5) | data formatting | bytes 2621440 | tf_op jit(solution)/shard_map/transpose | solution.py:190
  60.1 9.6 %all-to-all-start.1 = ((bf16[4,2,64,256]{3,2,1,0:T(8,128)(2,1)}), bf16[4,2,64,256]{3,2,1,0:T(8,128)(2,1)}, u32[]{:S(2)}, u32[]{:S(2)}) async-start(bf16[4,2,64,256]{3,2,1,0:T(8,128)(2,1)} %copy-done.6), calls=%async_computation.1 | async-start | bytes 524288 | tf_op jit(solution)/shard_map/all_to_all | solution.py:195
  69.7 0.9 constant_dynamic-slice_fusion
  70.6 5.4 %collective-permute-start.5 = (bf16[1280,256]{1,0:T(8,128)(2,1)S(1)}, bf16[1280,256]{1,0:T(8,128)(2,1)S(1)}, u32[]{:S(2)}, u32[]{:S(2)}) collective-permute-start(bf16[1280,256]{1,0:T(8,128)(2,1)S(1)} %get-tuple-element.26), channel_id=1, source_target_pairs={{0,4},{4,0},{1,5},{5,1},{2,6},{6,2},{3,7},{7,3},{8,12},{12,8},{9,1... | collective-permute-start | bytes 1966088 | tf_op jit(solution)/shard_map/ppermute | solution.py:197
  76.0 1.7 %collective-permute-done.5.basis_other_ref = bf16[1280,256]{1,0:T(8,128)(2,1)S(1)} collective-permute-done((bf16[1280,256]{1,0:T(8,128)(2,1)S(1)}, bf16[1280,256]{1,0:T(8,128)(2,1)S(1)}, u32[]{:S(2)}, u32[]{:S(2)}) %collective-permute-start.5) | collective-permute-done | bytes 655392 | tf_op jit(solution)/shard_map/ppermute | solution.py:197
  77.7 0.9 copy-done.14
  78.6 1.1 copy-done.7
  79.7 1.0 copy-done.11
  80.7 1.9 %shard_map.96 = bf16[640,256]{1,0:T(8,128)(2,1)S(1)} custom-call(bf16[4,2,64,256]{3,2,1,0:T(8,128)(2,1)} %all-to-all-done.1.reduced_ref, bf16[256,640]{1,0:T(8,128)(2,1)S(1)} %copy-done.2, bf16[256,640]{1,0:T(8,128)(2,1)S(1)} %copy-done.11, bf16[640,640]{1,0:T(8,128)(2,1)S(1)} %copy-done.7), custom_call_target="tpu_custom_call" | custom-call | flops 377487360 | bytes 2300000 | tf_op jit(solution)/shard_map/pallas_call | solution.py:134
  82.7 11.8 %all_to_all.20 = bf16[16,40,256]{2,1,0:T(8,128)(2,1)S(1)} all-to-all(bf16[16,40,256]{2,1,0:T(8,128)(2,1)S(1)} %bitcast.20), channel_id=1, replica_groups=mesh['y'=4,'zh'=4,'x'=4,'core'=2,'zl'=4] {'y','x'}, dimensions={0} | all-to-all | bytes 655360 | tf_op jit(solution)/shard_map/all_to_all | solution.py:205
  94.5 1.9 %collective-permute-start.6 = (bf16[40,256]{1,0:T(8,128)(2,1)S(1)}, bf16[40,256]{1,0:T(8,128)(2,1)S(1)}, u32[]{:S(2)}, u32[]{:S(2)}) collective-permute-start(bf16[40,256]{1,0:T(8,128)(2,1)S(1)} %reduce_sum.12), channel_id=1, source_target_pairs={{0,32},{32,0},{64,96},{96,64},{1,33},{33,1},{65,97},{97,65},{2,34}... | collective-permute-start | bytes 61448 | tf_op jit(solution)/shard_map/ppermute | solution.py:39
  96.5 6.6 %collective-permute-done.6 = bf16[40,256]{1,0:T(8,128)(2,1)S(1)} collective-permute-done((bf16[40,256]{1,0:T(8,128)(2,1)S(1)}, bf16[40,256]{1,0:T(8,128)(2,1)S(1)}, u32[]{:S(2)}, u32[]{:S(2)}) %collective-permute-start.6) | collective-permute-done | bytes 20512 | tf_op jit(solution)/shard_map/ppermute | solution.py:39
  103.1 5.6 %collective-permute-start.7 = (bf16[40,256]{1,0:T(8,128)(2,1)S(1)}, bf16[40,256]{1,0:T(8,128)(2,1)S(1)}, u32[]{:S(2)}, u32[]{:S(2)}) collective-permute-start(bf16[40,256]{1,0:T(8,128)(2,1)S(1)} %add_convert_fusion), channel_id=1, source_target_pairs={{0,96},{96,0},{32,64},{64,32},{1,97},{97,1},{33,65},{65,33},{2,98}... | collective-permute-start | bytes 61448 | tf_op jit(solution)/shard_map/ppermute | solution.py:39
  108.7 2.8 %collective-permute-done.7 = bf16[40,256]{1,0:T(8,128)(2,1)S(1)} collective-permute-done((bf16[40,256]{1,0:T(8,128)(2,1)S(1)}, bf16[40,256]{1,0:T(8,128)(2,1)S(1)}, u32[]{:S(2)}, u32[]{:S(2)}) %collective-permute-start.7) | collective-permute-done | bytes 20512 | tf_op jit(solution)/shard_map/ppermute | solution.py:39
  112.4 3.7 %all-to-all-start.3 = ((bf16[16,40,256]{2,1,0:T(8,128)(2,1)}), bf16[16,40,256]{2,1,0:T(8,128)(2,1)S(1)}, u32[]{:S(2)}, u32[]{:S(2)}) async-start(bf16[16,40,256]{2,1,0:T(8,128)(2,1)} %broadcast_in_dim.15), calls=%async_computation.3 | async-start | bytes 655360 | tf_op jit(solution)/shard_map/all_to_all | solution.py:22
  116.1 1.3 copy-done.3
  117.4 3.5 %shard_map.97 = bf16[256,640]{1,0:T(8,128)(2,1)} custom-call(s32[1]{0:T(128)} %bitcast.3.core_ref, bf16[256,2560]{1,0:T(8,128)(2,1)S(1)} %copy-done.3, bf16[640,1280]{1,0:T(8,128)(2,1)S(1)} %copy-done.1, bf16[640,1280]{1,0:T(8,128)(2,1)} %collective-permute-done.2.other_ref), custom_call_target="tpu_custom_call" | custom-call | flops 838860800 | bytes 5000000 | tf_op jit(solution)/shard_map/pallas_call | solution.py:91
  120.9 3.1 %all-to-all-done.3 = bf16[16,40,256]{2,1,0:T(8,128)(2,1)S(1)} async-done(((bf16[16,40,256]{2,1,0:T(8,128)(2,1)}), bf16[16,40,256]{2,1,0:T(8,128)(2,1)S(1)}, u32[]{:S(2)}, u32[]{:S(2)}) %all-to-all-start.3) | async-done | bytes 327712 | tf_op jit(solution)/shard_map/all_to_all | solution.py:22
  124.0 9.0 %collective-permute-start.8 = (bf16[640,256]{1,0:T(8,128)(2,1)S(1)}, bf16[640,256]{1,0:T(8,128)(2,1)S(1)}, u32[]{:S(2)}, u32[]{:S(2)}) collective-permute-start(bf16[640,256]{1,0:T(8,128)(2,1)S(1)} %bitcast.21), channel_id=1, source_target_pairs={{0,4},{4,0},{1,5},{5,1},{2,6},{6,2},{3,7},{7,3},{8,12},{12,8},{9,1... | collective-permute-start | bytes 983048 | tf_op jit(solution)/shard_map/ppermute | solution.py:217
  132.9 1.2 collective-permute-done.8.other_ref
  134.2 1.1 copy-done.15
  135.3 3.0 %shard_map.98 = bf16[640,1280]{1,0:T(8,128)(2,1)} custom-call(bf16[640,256]{1,0:T(8,128)(2,1)S(1)} %bitcast.22, bf16[640,256]{1,0:T(8,128)(2,1)S(1)} %collective-permute-done.8.other_ref, bf16[640,640]{1,0:T(8,128)(2,1)S(1)} %copy-done.8, bf16[1280,256]{1,0:T(8,128)(2,1)S(1)} %copy-done.9, bf16[1280,256]{1,0:T(8,128)(2,1)S(1)} %copy-done.15), custom_call_target="tpu_custom_call" | custom-call | flops 1258291200 | bytes 5000000 | tf_op jit(solution)/shard_map/pallas_call | solution.py:157
  (57 shorter events, 4.0 us)
Async XLA Ops:
  7.2 0.8 copy-start
  7.2 108.9 %all-gather.2.cloned.1.call-start = ((), (), s32[]{:S(2)}) async-start(), calls=%async_computation.5 | async-start | bytes 1638400 | tf_op jit(solution)/shard_map/all_gather | solution.py:175
  8.7 12.6 %collective-permute-start = (bf16[60,256]{1,0:T(8,128)(2,1)S(1)}, bf16[60,256]{1,0:T(8,128)(2,1)S(1)}, u32[]{:S(2)}, u32[]{:S(2)}) collective-permute-start(bf16[60,256]{1,0:T(8,128)(2,1)S(1)} %pad_maximum_fusion.2), channel_id=1, source_target_pairs={{0,32},{32,0},{64,96},{96,64},{1,33},{33,1},{65,97},{97,65},{2,34}... | collective-permute-start | bytes 92168 | tf_op jit(solution)/shard_map/ppermute | solution.py:27
  18.4 30.3 %collective-permute-start.2 = (bf16[640,1280]{1,0:T(8,128)(2,1)}, bf16[640,1280]{1,0:T(8,128)(2,1)}, u32[]{:S(2)}, u32[]{:S(2)}) collective-permute-start(bf16[640,1280]{1,0:T(8,128)(2,1)} %own_ref.7), channel_id=1, source_target_pairs={{0,4},{4,0},{1,5},{5,1},{2,6},{6,2},{3,7},{7,3},{8,12},{12,8},{9,1... | collective-permute-start | bytes 4915208 | tf_op jit(solution)/shard_map/ppermute | solution.py:176
  21.4 11.2 %collective-permute-start.1 = (bf16[120,256]{1,0:T(8,128)(2,1)S(1)}, bf16[120,256]{1,0:T(8,128)(2,1)S(1)}, u32[]{:S(2)}, u32[]{:S(2)}) collective-permute-start(bf16[120,256]{1,0:T(8,128)(2,1)S(1)} %pad_maximum_fusion.1), channel_id=1, source_target_pairs={{0,96},{96,0},{32,64},{64,32},{1,97},{97,1},{33,65},{65,33},{2,98}... | collective-permute-start | bytes 184328 | tf_op jit(solution)/shard_map/ppermute | solution.py:30
  33.9 7.0 %copy-start.2 = (bf16[256,640]{1,0:T(8,128)(2,1)S(1)}, bf16[256,640]{1,0:T(8,128)(2,1)}, u32[]{:S(2)}) copy-start(bf16[256,640]{1,0:T(8,128)(2,1)} %own_ref.6) | copy-start | bytes 983044
  33.9 12.8 %copy-start.4 = (bf16[64,2560]{1,0:T(8,128)(2,1)S(1)}, bf16[64,2560]{1,0:T(8,128)(2,1)}, u32[]{:S(2)}) copy-start(bf16[64,2560]{1,0:T(8,128)(2,1)} %own_ref.5) | copy-start | bytes 983044
  33.9 14.8 %copy-start.1 = (bf16[640,1280]{1,0:T(8,128)(2,1)S(1)}, bf16[640,1280]{1,0:T(8,128)(2,1)}, u32[]{:S(2)}) copy-start(bf16[640,1280]{1,0:T(8,128)(2,1)} %own_ref.7) | copy-start | bytes 4915204
  33.9 23.3 %all-to-all-start = ((bf16[16,160,256]{2,1,0:T(8,128)(2,1)}), bf16[16,160,256]{2,1,0:T(8,128)(2,1)}, u32[]{:S(2)}, u32[]{:S(2)}) async-start(bf16[16,160,256]{2,1,0:T(8,128)(2,1)} %broadcast_in_dim.14), calls=%async_computation | async-start | bytes 2621440 | tf_op jit(solution)/shard_map/all_to_all | solution.py:22
  40.8 83.1 %reduce-scatter.2.cloned.1.call-start = ((), (), s32[]{:S(2)}) async-start(), calls=%async_computation.6 | async-start | bytes 1638400 | tf_op jit(solution)/shard_map/reduce_scatter | solution.py:192
  40.9 11.6 %collective-permute-start.4 = (bf16[256,640]{1,0:T(8,128)(2,1)S(1)}, bf16[256,640]{1,0:T(8,128)(2,1)S(1)}, u32[]{:S(2)}, u32[]{:S(2)}) collective-permute-start(bf16[256,640]{1,0:T(8,128)(2,1)S(1)} %copy-done.2), channel_id=1, source_target_pairs={{0,4},{4,0},{1,5},{5,1},{2,6},{6,2},{3,7},{7,3},{8,12},{12,8},{9,1... | collective-permute-start | bytes 983048 | tf_op jit(solution)/shard_map/ppermute | solution.py:178
  46.7 5.8 %collective-permute-start.3 = (bf16[64,2560]{1,0:T(8,128)(2,1)S(1)}, bf16[64,2560]{1,0:T(8,128)(2,1)S(1)}, u32[]{:S(2)}, u32[]{:S(2)}) collective-permute-start(bf16[64,2560]{1,0:T(8,128)(2,1)S(1)} %copy-done.4), channel_id=1, source_target_pairs={{0,4},{4,0},{1,5},{5,1},{2,6},{6,2},{3,7},{7,3},{8,12},{12,8},{9,1... | collective-permute-start | bytes 983048 | tf_op jit(solution)/shard_map/ppermute | solution.py:177
  52.5 4.8 %copy-start.10 = (bf16[256,640]{1,0:T(8,128)(2,1)}, bf16[256,640]{1,0:T(8,128)(2,1)S(1)}, u32[]{:S(2)}) copy-start(bf16[256,640]{1,0:T(8,128)(2,1)S(1)} %collective-permute-done.4.other_ref) | copy-start | bytes 983044
  52.5 4.8 %copy-start.12 = (bf16[64,2560]{1,0:T(8,128)(2,1)}, bf16[64,2560]{1,0:T(8,128)(2,1)S(1)}, u32[]{:S(2)}) copy-start(bf16[64,2560]{1,0:T(8,128)(2,1)S(1)} %collective-permute-done.3.other_ref) | copy-start | bytes 983044
  57.3 1.5 %copy-start.5 = (bf16[64,2560]{1,0:T(8,128)(2,1)S(1)}, bf16[64,2560]{1,0:T(8,128)(2,1)}, u32[]{:S(2)}) copy-start(bf16[64,2560]{1,0:T(8,128)(2,1)} %own_ref.5) | copy-start | bytes 983044
  57.3 1.5 %copy-start.13 = (bf16[64,2560]{1,0:T(8,128)(2,1)S(1)}, bf16[64,2560]{1,0:T(8,128)(2,1)}, u32[]{:S(2)}) copy-start(bf16[64,2560]{1,0:T(8,128)(2,1)} %copy-done.12) | copy-start | bytes 983044
  59.4 0.7 copy-start.6
  60.1 18.5 %all-to-all-start.1 = ((bf16[4,2,64,256]{3,2,1,0:T(8,128)(2,1)}), bf16[4,2,64,256]{3,2,1,0:T(8,128)(2,1)}, u32[]{:S(2)}, u32[]{:S(2)}) async-start(bf16[4,2,64,256]{3,2,1,0:T(8,128)(2,1)} %copy-done.6), calls=%async_computation.1 | async-start | bytes 524288 | tf_op jit(solution)/shard_map/all_to_all | solution.py:195
  70.6 7.1 %collective-permute-start.5 = (bf16[1280,256]{1,0:T(8,128)(2,1)S(1)}, bf16[1280,256]{1,0:T(8,128)(2,1)S(1)}, u32[]{:S(2)}, u32[]{:S(2)}) collective-permute-start(bf16[1280,256]{1,0:T(8,128)(2,1)S(1)} %get-tuple-element.26), channel_id=1, source_target_pairs={{0,4},{4,0},{1,5},{5,1},{2,6},{6,2},{3,7},{7,3},{8,12},{12,8},{9,1... | collective-permute-start | bytes 1966088 | tf_op jit(solution)/shard_map/ppermute | solution.py:197
  77.7 0.9 copy-start.14
  78.6 1.1 copy-start.7
  79.7 1.0 copy-start.11
  94.5 8.6 %collective-permute-start.6 = (bf16[40,256]{1,0:T(8,128)(2,1)S(1)}, bf16[40,256]{1,0:T(8,128)(2,1)S(1)}, u32[]{:S(2)}, u32[]{:S(2)}) collective-permute-start(bf16[40,256]{1,0:T(8,128)(2,1)S(1)} %reduce_sum.12), channel_id=1, source_target_pairs={{0,32},{32,0},{64,96},{96,64},{1,33},{33,1},{65,97},{97,65},{2,34}... | collective-permute-start | bytes 61448 | tf_op jit(solution)/shard_map/ppermute | solution.py:39
  103.1 8.4 %collective-permute-start.7 = (bf16[40,256]{1,0:T(8,128)(2,1)S(1)}, bf16[40,256]{1,0:T(8,128)(2,1)S(1)}, u32[]{:S(2)}, u32[]{:S(2)}) collective-permute-start(bf16[40,256]{1,0:T(8,128)(2,1)S(1)} %add_convert_fusion), channel_id=1, source_target_pairs={{0,96},{96,0},{32,64},{64,32},{1,97},{97,1},{33,65},{65,33},{2,98}... | collective-permute-start | bytes 61448 | tf_op jit(solution)/shard_map/ppermute | solution.py:39
  112.4 11.6 %all-to-all-start.3 = ((bf16[16,40,256]{2,1,0:T(8,128)(2,1)}), bf16[16,40,256]{2,1,0:T(8,128)(2,1)S(1)}, u32[]{:S(2)}, u32[]{:S(2)}) async-start(bf16[16,40,256]{2,1,0:T(8,128)(2,1)} %broadcast_in_dim.15), calls=%async_computation.3 | async-start | bytes 655360 | tf_op jit(solution)/shard_map/all_to_all | solution.py:22
  116.1 1.3 copy-start.3
  117.4 16.8 %copy-start.8 = (bf16[640,640]{1,0:T(8,128)(2,1)S(1)}, bf16[640,640]{1,0:T(8,128)(2,1)}, u32[]{:S(2)}) copy-start(bf16[640,640]{1,0:T(8,128)(2,1)} %constant.57.clone.order_ref) | copy-start | bytes 2457604
  117.4 16.8 %copy-start.9 = (bf16[1280,256]{1,0:T(8,128)(2,1)S(1)}, bf16[1280,256]{1,0:T(8,128)(2,1)}, u32[]{:S(2)}) copy-start(bf16[1280,256]{1,0:T(8,128)(2,1)} %get-tuple-element.25.basis_ref) | copy-start | bytes 1966084
  124.0 10.2 %collective-permute-start.8 = (bf16[640,256]{1,0:T(8,128)(2,1)S(1)}, bf16[640,256]{1,0:T(8,128)(2,1)S(1)}, u32[]{:S(2)}, u32[]{:S(2)}) collective-permute-start(bf16[640,256]{1,0:T(8,128)(2,1)S(1)} %bitcast.21), channel_id=1, source_target_pairs={{0,4},{4,0},{1,5},{5,1},{2,6},{6,2},{3,7},{7,3},{8,12},{12,8},{9,1... | collective-permute-start | bytes 983048 | tf_op jit(solution)/shard_map/ppermute | solution.py:217
  134.2 1.1 copy-start.15
Sparse Core Ops, SparseCore 0:
  18.5 42.4 all-gather.1
  64.4 41.3 reduce-scatter.1

commit v5 on v4

--- a/solution.py
+++ b/solution.py
@@ -15,6 +15,7 @@
 PAIR = [(0, 1), (1, 0), (2, 3), (3, 2)]
 MIRROR = [(0, 3), (3, 0), (1, 2), (2, 1)]
 ORDER = np.eye(640, dtype=np.float32).reshape(640, 4, 4, 4, 10).transpose(0, 1, 3, 2, 4).reshape(640, 640)
+ARRIVAL = np.eye(640, dtype=np.float32).reshape(640, 4, 4, 40).transpose(0, 2, 1, 3).reshape(640, 640)
 
 
 def spread(values, axes, count):
@@ -98,47 +99,66 @@
     )(core, grads, own, other)
 
 
-def reduced_kernel(basis_ref, own_ref, other_ref, out_ref):
-    for which, grads in ((0, own_ref), (1, other_ref)):
-        part = jnp.dot(grads[...], basis_ref[...], preferred_element_type=F32).astype(BF16)
-        for target in range(out_ref.shape[0]):
-            out_ref[target, which] = part
-
-
-def reduced_matmul(basis, grads, grads_other):
+def ordered_kernel(order_ref, arrival_ref, x_ref, xo_ref, g_ref, go_ref, px_ref, pxo_ref, pg_ref):
+    for source, target in ((x_ref, px_ref), (xo_ref, pxo_ref)):
+        moved = jnp.dot(source[...], order_ref[...], preferred_element_type=F32)
+        target[...] = moved.astype(BF16)
+    for which, source in ((0, g_ref), (1, go_ref)):
+        for y in range(4):
+            cols = slice(640 * y, 640 * (y + 1))
+            moved = jnp.dot(source[:, cols], arrival_ref[...], preferred_element_type=F32)
+            pg_ref[64 * which : 64 * (which + 1), cols] = moved.astype(BF16)
+
+
+def ordered(order, arrival, rows, rows_other, grads, grads_other):
+    x_shape = jax.ShapeDtypeStruct((256, 640), BF16)
+    return pl.pallas_call(
+        ordered_kernel,
+        out_shape=(x_shape, x_shape, jax.ShapeDtypeStruct((128, 2560), BF16)),
+        in_specs=[VMEM] * 6,
+        out_specs=(VMEM,) * 3,
+        compiler_params=ROOM,
+        cost_estimate=cost(2 * 640 * 640 * 1024, 4_200_000),
+    )(order, arrival, rows, rows_other, grads, grads_other)
+
+
+def reduced_kernel(basis_ref, grad_ref, out_ref):
+    part = jnp.dot(grad_ref[...], basis_ref[...], preferred_element_type=F32).astype(BF16)
+    for target in range(out_ref.shape[0]):
+        out_ref[target] = part
+
+
+def reduced_matmul(basis, grads):
     return pl.pallas_call(
         reduced_kernel,
-        out_shape=jax.ShapeDtypeStruct((4, 2, 64, 256), BF16),
-        in_specs=[VMEM] * 3,
+        out_shape=jax.ShapeDtypeStruct((4, 128, 256), BF16),
+        in_specs=[VMEM] * 2,
         out_specs=VMEM,
         compiler_params=ROOM,
         cost_estimate=cost(2 * 128 * 256 * 2560, 2_500_000),
-    )(basis, grads, grads_other)
-
-
-def low_kernel(reduced_ref, own_ref, other_ref, order_ref, out_ref):
+    )(basis, grads)
+
+
+def low_kernel(reduced_ref, own_ref, other_ref, out_ref):
     total = None
     for which, rows in ((0, own_ref), (1, other_ref)):
-        reduced = reduced_ref[:, which].reshape(256, 256)
+        reduced = reduced_ref[:, 64 * which : 64 * (which + 1)].reshape(256, 256)
         part = lax.dot_general(
             rows[...], reduced, (((0,), (0,)), ((), ())), preferred_element_type=F32
         )
         total = part if total is None else total + part
-    ordered = lax.dot_general(
-        order_ref[...], total.astype(BF16), (((0,), (0,)), ((), ())), preferred_element_type=F32
-    )
-    out_ref[...] = ordered.astype(BF16)
-
-
-def low_matmul(reduced, rows, rows_other, order):
+    out_ref[...] = total.astype(BF16)
+
+
+def low_matmul(reduced, rows, rows_other):
     return pl.pallas_call(
         low_kernel,
         out_shape=jax.ShapeDtypeStruct((640, 256), BF16),
-        in_specs=[VMEM] * 4,
-        out_specs=VMEM,
-        compiler_params=ROOM,
-        cost_estimate=cost(2 * 640 * 256 * (512 + 640), 2_300_000),
-    )(reduced, rows, rows_other, order)
+        in_specs=[VMEM] * 3,
+        out_specs=VMEM,
+        compiler_params=ROOM,
+        cost_estimate=cost(2 * 512 * 256 * 640, 1_500_000),
+    )(reduced, rows, rows_other)
 
 
 def update_kernel(own_ref, other_ref, order_ref, basis_ref, basis_other_ref, out_ref):
@@ -184,25 +204,34 @@
     by_yx = spread(by_zh[:, :40].reshape(160, 256), ("y", "x"), 16)
 
     mixed_part = mixed_matmul(scalar, x_heads, proj_weight, weight_other)
-    by_yx, mixed_part, grad_other, x_other, m_old, v_old = lax.optimization_barrier(
-        (by_yx, mixed_part, grad_other, x_other, m_old, v_old)
-    )
-    basis_cols = by_yx.reshape(4, 4, 4, 40, 256).transpose(0, 2, 1, 3, 4).reshape(2560, 256)
+    order, arrival = jnp.asarray(ORDER, BF16), jnp.asarray(ARRIVAL, BF16)
+    x_own, x_other, grads = ordered(order, arrival, x_heads, x_other, out_grad, grad_other)
+    by_yx, mixed_part, x_own, x_other, grads, m_old, v_old = lax.optimization_barrier(
+        (by_yx, mixed_part, x_own, x_other, grads, m_old, v_old)
+    )
 
     mixed_out = lax.psum_scatter(mixed_part, "zl", scatter_dimension=0, tiled=True)
 
-    reduced = reduced_matmul(basis_cols, out_grad, grad_other)
+    reduced = reduced_matmul(by_yx.reshape(2560, 256), grads)
     reduced = lax.all_to_all(reduced, "zl", 0, 0, tiled=True)
-    basis_own = lax.dynamic_slice_in_dim(basis_cols, core * half, half, 0)
+    by_y = by_yx.reshape(2, 8, 160, 256)
+    basis_own = lax.dynamic_index_in_dim(by_y, core, 0, keepdims=False)
     basis_other = lax.ppermute(
-        lax.dynamic_slice_in_dim(basis_cols, (1 - core) * half, half, 0), "core", CORE_SWAP
+        lax.dynamic_index_in_dim(by_y, 1 - core, 0, keepdims=False), "core", CORE_SWAP
     )
     reduced, basis_other = lax.optimization_barrier((reduced, basis_other))
 
-    order = jnp.asarray(ORDER, BF16)
-    low_chip = low_matmul(reduced, x_heads, x_other, order)
+    low_chip = low_matmul(reduced, x_own, x_other)
 
     low_yx = lax.all_to_all(low_chip.reshape(16, 40, 256), ("y", "x"), 0, 0, tiled=True)
+    basis_own, basis_other, low_chip = lax.optimization_barrier((basis_own, basis_other, low_chip))
+
+    def natural(rows):
+        return rows.reshape(2, 4, 4, 40, 256).transpose(0, 2, 1, 3, 4).reshape(half, 256)
+
+    low_yx, basis_own, basis_other = lax.optimization_barrier(
+        (low_yx, natural(basis_own), natural(basis_other))
+    )
     low = sum_zh(jnp.sum(low_yx.astype(F32), 0))
 
     m_new = 0.9 * m_old.astype(F32) + 0.1 * low

time: 146 us -> 146 us (level)
  blocking collectives: 11.8 us -> 0 us
  starting transfers between devices: 71.7 us -> 78.9 us
  local copies, waits for them, and re-layouts: 12.1 us -> 17.5 us
  waiting for transfers between devices: 22.2 us -> 19.7 us
    all_to_all x1 -> x0, blocking collectives: 11.8 us -> none  [shards(): lax.all_to_all(low_chip.reshape(16, 40, 256), ('y', 'x'), 0, 0, tiled=True)]
    ppermute x2, starting transfers between devices: 7.53 us -> 14.5 us  [sum_zh(): values = sent.astype(F32) + lax.ppermute(sent, 'zh', partners).astype(F32)]
    unnamed x34 -> x36, local copies, waits for them, and re-layouts: 6.88 us -> 13.7 us
    all_to_all x0 -> x1, waiting for transfers between devices: none -> 6.76 us  [shards(): lax.all_to_all(low_chip.reshape(16, 40, 256), ('y', 'x'), 0, 0, tiled=True)]
    ppermute x2, waiting for transfers between devices: 9.45 us -> 2.99 us  [sum_zh(): values = sent.astype(F32) + lax.ppermute(sent, 'zh', partners).astype(F32)]
    all_to_all x0 -> x1, starting transfers between devices: none -> 5.23 us  [shards(): lax.all_to_all(low_chip.reshape(16, 40, 256), ('y', 'x'), 0, 0, tiled=True)]
    all_to_all x1, starting transfers between devices: 9.59 us -> 4.92 us  [shards(): reduced = lax.all_to_all(reduced, 'zl', 0, 0, tiled=True)]
    all_to_all x2, waiting for transfers between devices: 7.81 us -> 3.19 us  [spread(): return lax.all_to_all(copies, axes, 0, 0, tiled=True)]
  transfers between devices with their start and end apart: 14 -> 15, of which waited for: 7 -> 8; matrix products, arithmetic and copies ran while one was open for 3% -> 2% of each run, Pallas kernels for 7% -> 8%
where the time goes in v5:
time: 146 us; the launch traced here: 145 us
  starting transfers between devices  78.9 us (54%)
  waiting for transfers between devices  19.7 us (13%)
  local copies, waits for them, and re-layouts  17.5 us (12%)
  between operations  14.4 us (10%)
  Pallas kernels  14.1 us (10%)
    ppermute x2, starting transfers between devices, sum_zh(): values = sent.astype(F32) + lax.ppermute(sent, 'zh', partners).astype(F32)  14.5 us
    unnamed x36, local copies, waits for them, and re-layouts  13.7 us
    all_to_all x2, starting transfers between devices, spread(): return lax.all_to_all(copies, axes, 0, 0, tiled=True)  10.6 us
    ppermute x1, starting transfers between devices, gather_zh(): got = lax.ppermute(values, 'zh', PAIR)  9.65 us
    ppermute x1, starting transfers between devices, gather_zh(): got = lax.ppermute(pair, 'zh', MIRROR)  9.28 us
    ppermute x1, starting transfers between devices, shards(): rows_other = lax.ppermute(rows, 'core', CORE_SWAP)  8.68 us
    all_to_all x1, waiting for transfers between devices, shards(): lax.all_to_all(low_chip.reshape(16, 40, 256), ('y', 'x'), 0, 0, tiled=True)  6.76 us
    ppermute x1, starting transfers between devices, shards(): x_other = lax.ppermute(x_heads, 'core', CORE_SWAP)  5.81 us
  transfers between devices with their start and end apart: 15, of which 8 were waited for; matrix products, arithmetic and copies ran while one was open for 2% of the time, Pallas kernels for 8%

profile of v5, /device:TPU:1, one launch (start us, length us, event | category | flops | bytes accessed | tf_op | source)
XLA Modules:
  0.0 144.7 jit_solution(1200328782116512325)
XLA Ops:
  8.7 9.6 %collective-permute-start = (bf16[60,256]{1,0:T(8,128)(2,1)S(1)}, bf16[60,256]{1,0:T(8,128)(2,1)S(1)}, u32[]{:S(2)}, u32[]{:S(2)}) collective-permute-start(bf16[60,256]{1,0:T(8,128)(2,1)S(1)} %pad_maximum_fusion.2), channel_id=1, source_target_pairs={{0,32},{32,0},{64,96},{96,64},{1,33},{33,1},{65,97},{97,65},{2,34}... | collective-permute-start | bytes 92168 | tf_op jit(solution)/shard_map/ppermute | solution.py:28
  18.4 2.9 %collective-permute-start.2 = (bf16[640,1280]{1,0:T(8,128)(2,1)}, bf16[640,1280]{1,0:T(8,128)(2,1)}, u32[]{:S(2)}, u32[]{:S(2)}) collective-permute-start(bf16[640,1280]{1,0:T(8,128)(2,1)} %own_ref.3), channel_id=1, source_target_pairs={{0,4},{4,0},{1,5},{5,1},{2,6},{6,2},{3,7},{7,3},{8,12},{12,8},{9,1... | collective-permute-start | bytes 4915208 | tf_op jit(solution)/shard_map/ppermute | solution.py:196
  21.4 9.3 %collective-permute-start.1 = (bf16[120,256]{1,0:T(8,128)(2,1)S(1)}, bf16[120,256]{1,0:T(8,128)(2,1)S(1)}, u32[]{:S(2)}, u32[]{:S(2)}) collective-permute-start(bf16[120,256]{1,0:T(8,128)(2,1)S(1)} %pad_maximum_fusion.1), channel_id=1, source_target_pairs={{0,96},{96,0},{32,64},{64,32},{1,97},{97,1},{33,65},{65,33},{2,98}... | collective-permute-start | bytes 184328 | tf_op jit(solution)/shard_map/ppermute | solution.py:31
  30.6 1.9 %collective-permute-done.1 = bf16[120,256]{1,0:T(8,128)(2,1)S(1)} collective-permute-done((bf16[120,256]{1,0:T(8,128)(2,1)S(1)}, bf16[120,256]{1,0:T(8,128)(2,1)S(1)}, u32[]{:S(2)}, u32[]{:S(2)}) %collective-permute-start.1) | collective-permute-done | bytes 61472 | tf_op jit(solution)/shard_map/ppermute | solution.py:31
  32.6 1.2 broadcast_in_dim.14
  33.8 6.9 %all-to-all-start = ((bf16[16,160,256]{2,1,0:T(8,128)(2,1)}), bf16[16,160,256]{2,1,0:T(8,128)(2,1)S(1)}, u32[]{:S(2)}, u32[]{:S(2)}) async-start(bf16[16,160,256]{2,1,0:T(8,128)(2,1)} %broadcast_in_dim.14), calls=%async_computation | async-start | bytes 2621440 | tf_op jit(solution)/shard_map/all_to_all | solution.py:23
  40.8 5.8 %collective-permute-start.3 = (bf16[256,640]{1,0:T(8,128)(2,1)S(1)}, bf16[256,640]{1,0:T(8,128)(2,1)}, u32[]{:S(2)}, u32[]{:S(2)}) collective-permute-start(bf16[256,640]{1,0:T(8,128)(2,1)S(1)} %copy-done.6), channel_id=1, source_target_pairs={{0,4},{4,0},{1,5},{5,1},{2,6},{6,2},{3,7},{7,3},{8,12},{12,8},{9,1... | collective-permute-start | bytes 983048 | tf_op jit(solution)/shard_map/ppermute | solution.py:198
  46.6 1.9 %collective-permute-start.4 = (bf16[64,2560]{1,0:T(8,128)(2,1)}, bf16[64,2560]{1,0:T(8,128)(2,1)}, u32[]{:S(2)}, u32[]{:S(2)}) collective-permute-start(bf16[64,2560]{1,0:T(8,128)(2,1)} %g_ref.1), channel_id=1, source_target_pairs={{0,4},{4,0},{1,5},{5,1},{2,6},{6,2},{3,7},{7,3},{8,12},{12,8},{9,1... | collective-permute-start | bytes 983048 | tf_op jit(solution)/shard_map/ppermute | solution.py:197
  48.6 1.8 %collective-permute-done.4.go_ref = bf16[64,2560]{1,0:T(8,128)(2,1)} collective-permute-done((bf16[64,2560]{1,0:T(8,128)(2,1)}, bf16[64,2560]{1,0:T(8,128)(2,1)}, u32[]{:S(2)}, u32[]{:S(2)}) %collective-permute-start.4) | collective-permute-done | bytes 327712 | tf_op jit(solution)/shard_map/ppermute | solution.py:197
  50.5 1.2 copy-done.11
  51.7 1.1 copy-done.13
  52.8 2.9 %shard_map.104 = (bf16[256,640]{1,0:T(8,128)(2,1)S(1)}, bf16[256,640]{1,0:T(8,128)(2,1)S(1)}, bf16[128,2560]{1,0:T(8,128)(2,1)S(1)}) custom-call(bf16[640,640]{1,0:T(8,128)(2,1)S(1)} %copy-done.11, bf16[640,640]{1,0:T(8,128)(2,1)S(1)} %copy-done.13, bf16[256,640]{1,0:T(8,128)(2,1)S(1)} %copy-done.6, bf16[256,640]{1,0:T(8,128)(2,1)} %collective-permute-done.3.xo_ref, ...), custom_call_target="tpu_custom_call" | custom-call | flops 838860800 | bytes 4200000 | tf_op jit(solution)/shard_map/pallas_call | solution.py:115
  58.0 2.6 %shard_map.103 = bf16[256,2560]{1,0:T(8,128)(2,1)S(1)} custom-call(s32[1]{0:T(128)} %bitcast.3.core_ref, bf16[256,640]{1,0:T(8,128)(2,1)S(1)} %copy-done.6, bf16[640,1280]{1,0:T(8,128)(2,1)S(1)} %copy-done.1, bf16[640,1280]{1,0:T(8,128)(2,1)} %collective-permute-done.2.other_ref), custom_call_target="tpu_custom_call" | custom-call | flops 838860800 | bytes 5000000 | tf_op jit(solution)/shard_map/pallas_call | solution.py:66
  61.8 1.1 copy-done.5
  63.9 4.9 %all-to-all-start.1 = ((bf16[4,128,256]{2,1,0:T(8,128)(2,1)}), bf16[4,128,256]{2,1,0:T(8,128)(2,1)S(1)}, u32[]{:S(2)}, u32[]{:S(2)}) async-start(bf16[4,128,256]{2,1,0:T(8,128)(2,1)} %shard_map.105), calls=%async_computation.1 | async-start | bytes 524288 | tf_op jit(solution)/shard_map/all_to_all | solution.py:216
  69.8 5.4 %collective-permute-start.5 = (bf16[8,160,256]{2,1,0:T(8,128)(2,1)S(1)}, bf16[8,160,256]{2,1,0:T(8,128)(2,1)S(1)}, u32[]{:S(2)}, u32[]{:S(2)}) collective-permute-start(bf16[8,160,256]{2,1,0:T(8,128)(2,1)S(1)} %get-tuple-element.44), channel_id=1, source_target_pairs={{0,4},{4,0},{1,5},{5,1},{2,6},{6,2},{3,7},{7,3},{8,12},{12,8},{9,1... | collective-permute-start | bytes 1966088 | tf_op jit(solution)/shard_map/ppermute | solution.py:219
  75.2 1.7 %collective-permute-done.5 = bf16[8,160,256]{2,1,0:T(8,128)(2,1)S(1)} collective-permute-done((bf16[8,160,256]{2,1,0:T(8,128)(2,1)S(1)}, bf16[8,160,256]{2,1,0:T(8,128)(2,1)S(1)}, u32[]{:S(2)}, u32[]{:S(2)}) %collective-permute-start.5) | collective-permute-done | bytes 655392 | tf_op jit(solution)/shard_map/ppermute | solution.py:219
  79.6 1.1 shard_map.106
  80.8 5.2 %all-to-all-start.2 = ((bf16[16,40,256]{2,1,0:T(8,128)(2,1)}), bf16[16,40,256]{2,1,0:T(8,128)(2,1)S(1)}, u32[]{:S(2)}, u32[]{:S(2)}) async-start(bf16[16,40,256]{2,1,0:T(8,128)(2,1)} %bitcast.7), calls=%async_computation.2 | async-start | bytes 655360 | tf_op jit(solution)/shard_map/all_to_all | solution.py:226
  87.1 6.8 %all-to-all-done.2 = bf16[16,40,256]{2,1,0:T(8,128)(2,1)S(1)} async-done(((bf16[16,40,256]{2,1,0:T(8,128)(2,1)}), bf16[16,40,256]{2,1,0:T(8,128)(2,1)S(1)}, u32[]{:S(2)}, u32[]{:S(2)}) %all-to-all-start.2) | async-done | bytes 327712 | tf_op jit(solution)/shard_map/all_to_all | solution.py:226
  93.9 6.8 %collective-permute-start.6 = (bf16[40,256]{1,0:T(8,128)(2,1)S(1)}, bf16[40,256]{1,0:T(8,128)(2,1)S(1)}, u32[]{:S(2)}, u32[]{:S(2)}) collective-permute-start(bf16[40,256]{1,0:T(8,128)(2,1)S(1)} %reduce_sum.12), channel_id=1, source_target_pairs={{0,32},{32,0},{64,96},{96,64},{1,33},{33,1},{65,97},{97,65},{2,34}... | collective-permute-start | bytes 61448 | tf_op jit(solution)/shard_map/ppermute | solution.py:40
  100.7 1.8 %collective-permute-done.6 = bf16[40,256]{1,0:T(8,128)(2,1)S(1)} collective-permute-done((bf16[40,256]{1,0:T(8,128)(2,1)S(1)}, bf16[40,256]{1,0:T(8,128)(2,1)S(1)}, u32[]{:S(2)}, u32[]{:S(2)}) %collective-permute-start.6) | collective-permute-done | bytes 20512 | tf_op jit(solution)/shard_map/ppermute | solution.py:40
  102.5 7.7 %collective-permute-start.7 = (bf16[40,256]{1,0:T(8,128)(2,1)S(1)}, bf16[40,256]{1,0:T(8,128)(2,1)S(1)}, u32[]{:S(2)}, u32[]{:S(2)}) collective-permute-start(bf16[40,256]{1,0:T(8,128)(2,1)S(1)} %add_convert_fusion), channel_id=1, source_target_pairs={{0,96},{96,0},{32,64},{64,32},{1,97},{97,1},{33,65},{65,33},{2,98}... | collective-permute-start | bytes 61448 | tf_op jit(solution)/shard_map/ppermute | solution.py:40
  110.3 1.2 collective-permute-done.7
  112.2 3.7 %all-to-all-start.3 = ((bf16[16,40,256]{2,1,0:T(8,128)(2,1)}), bf16[16,40,256]{2,1,0:T(8,128)(2,1)S(1)}, u32[]{:S(2)}, u32[]{:S(2)}) async-start(bf16[16,40,256]{2,1,0:T(8,128)(2,1)} %broadcast_in_dim.15), calls=%async_computation.3 | async-start | bytes 655360 | tf_op jit(solution)/shard_map/all_to_all | solution.py:23
  116.0 1.3 copy-done.3
  117.3 3.4 %shard_map.107 = bf16[256,640]{1,0:T(8,128)(2,1)} custom-call(s32[1]{0:T(128)} %bitcast.3.core_ref, bf16[256,2560]{1,0:T(8,128)(2,1)S(1)} %copy-done.3, bf16[640,1280]{1,0:T(8,128)(2,1)S(1)} %copy-done.1, bf16[640,1280]{1,0:T(8,128)(2,1)} %collective-permute-done.2.other_ref), custom_call_target="tpu_custom_call" | custom-call | flops 838860800 | bytes 5000000 | tf_op jit(solution)/shard_map/pallas_call | solution.py:92
  120.6 3.2 %all-to-all-done.3 = bf16[16,40,256]{2,1,0:T(8,128)(2,1)S(1)} async-done(((bf16[16,40,256]{2,1,0:T(8,128)(2,1)}), bf16[16,40,256]{2,1,0:T(8,128)(2,1)S(1)}, u32[]{:S(2)}, u32[]{:S(2)}) %all-to-all-start.3) | async-done | bytes 327712 | tf_op jit(solution)/shard_map/all_to_all | solution.py:23
  123.8 8.7 %collective-permute-start.8 = (bf16[640,256]{1,0:T(8,128)(2,1)S(1)}, bf16[640,256]{1,0:T(8,128)(2,1)S(1)}, u32[]{:S(2)}, u32[]{:S(2)}) collective-permute-start(bf16[640,256]{1,0:T(8,128)(2,1)S(1)} %bitcast.32), channel_id=1, source_target_pairs={{0,4},{4,0},{1,5},{5,1},{2,6},{6,2},{3,7},{7,3},{8,12},{12,8},{9,1... | collective-permute-start | bytes 983048 | tf_op jit(solution)/shard_map/ppermute | solution.py:246
  132.5 1.2 collective-permute-done.8.other_ref
  133.7 1.1 copy-done.12
  134.9 3.0 %shard_map.108 = bf16[640,1280]{1,0:T(8,128)(2,1)} custom-call(bf16[640,256]{1,0:T(8,128)(2,1)S(1)} %bitcast.33, bf16[640,256]{1,0:T(8,128)(2,1)S(1)} %collective-permute-done.8.other_ref, bf16[640,640]{1,0:T(8,128)(2,1)S(1)} %copy-done.12, bf16[1280,256]{1,0:T(8,128)(2,1)S(1)} %bitcast.30, bf16[1280,256]{1,0:T(8,128)(2,1)S(1)} %bitcast.31), custom_call_target="tpu_custom_call" | custom-call | flops 1258291200 | bytes 5000000 | tf_op jit(solution)/shard_map/pallas_call | solution.py:177
  (62 shorter events, 11.9 us)
Async XLA Ops:
  7.2 0.8 copy-start
  7.2 108.8 %all-gather.2.cloned.1.call-start = ((), (), s32[]{:S(2)}) async-start(), calls=%async_computation.5 | async-start | bytes 1638400 | tf_op jit(solution)/shard_map/all_gather | solution.py:195
  8.7 12.6 %collective-permute-start = (bf16[60,256]{1,0:T(8,128)(2,1)S(1)}, bf16[60,256]{1,0:T(8,128)(2,1)S(1)}, u32[]{:S(2)}, u32[]{:S(2)}) collective-permute-start(bf16[60,256]{1,0:T(8,128)(2,1)S(1)} %pad_maximum_fusion.2), channel_id=1, source_target_pairs={{0,32},{32,0},{64,96},{96,64},{1,33},{33,1},{65,97},{97,65},{2,34}... | collective-permute-start | bytes 92168 | tf_op jit(solution)/shard_map/ppermute | solution.py:28
  18.4 39.6 %collective-permute-start.2 = (bf16[640,1280]{1,0:T(8,128)(2,1)}, bf16[640,1280]{1,0:T(8,128)(2,1)}, u32[]{:S(2)}, u32[]{:S(2)}) collective-permute-start(bf16[640,1280]{1,0:T(8,128)(2,1)} %own_ref.3), channel_id=1, source_target_pairs={{0,4},{4,0},{1,5},{5,1},{2,6},{6,2},{3,7},{7,3},{8,12},{12,8},{9,1... | collective-permute-start | bytes 4915208 | tf_op jit(solution)/shard_map/ppermute | solution.py:196
  21.4 11.2 %collective-permute-start.1 = (bf16[120,256]{1,0:T(8,128)(2,1)S(1)}, bf16[120,256]{1,0:T(8,128)(2,1)S(1)}, u32[]{:S(2)}, u32[]{:S(2)}) collective-permute-start(bf16[120,256]{1,0:T(8,128)(2,1)S(1)} %pad_maximum_fusion.1), channel_id=1, source_target_pairs={{0,96},{96,0},{32,64},{64,32},{1,97},{97,1},{33,65},{65,33},{2,98}... | collective-permute-start | bytes 184328 | tf_op jit(solution)/shard_map/ppermute | solution.py:31
  33.8 6.9 %copy-start.6 = (bf16[256,640]{1,0:T(8,128)(2,1)S(1)}, bf16[256,640]{1,0:T(8,128)(2,1)}, u32[]{:S(2)}) copy-start(bf16[256,640]{1,0:T(8,128)(2,1)} %x_ref.3) | copy-start | bytes 983044
  33.8 27.9 %all-to-all-start = ((bf16[16,160,256]{2,1,0:T(8,128)(2,1)}), bf16[16,160,256]{2,1,0:T(8,128)(2,1)S(1)}, u32[]{:S(2)}, u32[]{:S(2)}) async-start(bf16[16,160,256]{2,1,0:T(8,128)(2,1)} %broadcast_in_dim.14), calls=%async_computation | async-start | bytes 2621440 | tf_op jit(solution)/shard_map/all_to_all | solution.py:23
  40.7 83.1 %reduce-scatter.2.cloned.1.call-start = ((), (), s32[]{:S(2)}) async-start(), calls=%async_computation.6 | async-start | bytes 1638400 | tf_op jit(solution)/shard_map/reduce_scatter | solution.py:213
  40.8 7.8 %collective-permute-start.3 = (bf16[256,640]{1,0:T(8,128)(2,1)S(1)}, bf16[256,640]{1,0:T(8,128)(2,1)}, u32[]{:S(2)}, u32[]{:S(2)}) collective-permute-start(bf16[256,640]{1,0:T(8,128)(2,1)S(1)} %copy-done.6), channel_id=1, source_target_pairs={{0,4},{4,0},{1,5},{5,1},{2,6},{6,2},{3,7},{7,3},{8,12},{12,8},{9,1... | collective-permute-start | bytes 983048 | tf_op jit(solution)/shard_map/ppermute | solution.py:198
  46.6 3.9 %collective-permute-start.4 = (bf16[64,2560]{1,0:T(8,128)(2,1)}, bf16[64,2560]{1,0:T(8,128)(2,1)}, u32[]{:S(2)}, u32[]{:S(2)}) collective-permute-start(bf16[64,2560]{1,0:T(8,128)(2,1)} %g_ref.1), channel_id=1, source_target_pairs={{0,4},{4,0},{1,5},{5,1},{2,6},{6,2},{3,7},{7,3},{8,12},{12,8},{9,1... | collective-permute-start | bytes 983048 | tf_op jit(solution)/shard_map/ppermute | solution.py:197
  48.6 9.4 %copy-start.1 = (bf16[640,1280]{1,0:T(8,128)(2,1)S(1)}, bf16[640,1280]{1,0:T(8,128)(2,1)}, u32[]{:S(2)}) copy-start(bf16[640,1280]{1,0:T(8,128)(2,1)} %own_ref.3) | copy-start | bytes 4915204
  50.5 1.2 copy-start.11
  51.6 1.1 copy-start.13
  55.7 0.8 copy-start.4
  56.6 0.7 copy-start.7
  57.3 0.7 copy-start.9
  60.7 1.1 copy-start.2
  61.8 1.1 copy-start.5
  63.9 13.8 %all-to-all-start.1 = ((bf16[4,128,256]{2,1,0:T(8,128)(2,1)}), bf16[4,128,256]{2,1,0:T(8,128)(2,1)S(1)}, u32[]{:S(2)}, u32[]{:S(2)}) async-start(bf16[4,128,256]{2,1,0:T(8,128)(2,1)} %shard_map.105), calls=%async_computation.1 | async-start | bytes 524288 | tf_op jit(solution)/shard_map/all_to_all | solution.py:216
  69.8 7.1 %collective-permute-start.5 = (bf16[8,160,256]{2,1,0:T(8,128)(2,1)S(1)}, bf16[8,160,256]{2,1,0:T(8,128)(2,1)S(1)}, u32[]{:S(2)}, u32[]{:S(2)}) collective-permute-start(bf16[8,160,256]{2,1,0:T(8,128)(2,1)S(1)} %get-tuple-element.44), channel_id=1, source_target_pairs={{0,4},{4,0},{1,5},{5,1},{2,6},{6,2},{3,7},{7,3},{8,12},{12,8},{9,1... | collective-permute-start | bytes 1966088 | tf_op jit(solution)/shard_map/ppermute | solution.py:219
  76.9 0.8 copy-start.15
  77.7 1.0 copy-start.8
  78.7 1.0 copy-start.10
  79.6 6.4 %copy-start.14 = (bf16[8,160,256]{2,1,0:T(8,128)(2,1)S(1)}, bf16[8,160,256]{2,1,0:T(8,128)(2,1)}, u32[]{:S(2)}) copy-start(bf16[8,160,256]{2,1,0:T(8,128)(2,1)} %get-tuple-element.33) | copy-start | bytes 1966084
  80.8 13.1 %all-to-all-start.2 = ((bf16[16,40,256]{2,1,0:T(8,128)(2,1)}), bf16[16,40,256]{2,1,0:T(8,128)(2,1)S(1)}, u32[]{:S(2)}, u32[]{:S(2)}) async-start(bf16[16,40,256]{2,1,0:T(8,128)(2,1)} %bitcast.7), calls=%async_computation.2 | async-start | bytes 655360 | tf_op jit(solution)/shard_map/all_to_all | solution.py:226
  86.0 1.1 copy-start.16
  93.9 8.6 %collective-permute-start.6 = (bf16[40,256]{1,0:T(8,128)(2,1)S(1)}, bf16[40,256]{1,0:T(8,128)(2,1)S(1)}, u32[]{:S(2)}, u32[]{:S(2)}) collective-permute-start(bf16[40,256]{1,0:T(8,128)(2,1)S(1)} %reduce_sum.12), channel_id=1, source_target_pairs={{0,32},{32,0},{64,96},{96,64},{1,33},{33,1},{65,97},{97,65},{2,34}... | collective-permute-start | bytes 61448 | tf_op jit(solution)/shard_map/ppermute | solution.py:40
  102.5 8.9 %collective-permute-start.7 = (bf16[40,256]{1,0:T(8,128)(2,1)S(1)}, bf16[40,256]{1,0:T(8,128)(2,1)S(1)}, u32[]{:S(2)}, u32[]{:S(2)}) collective-permute-start(bf16[40,256]{1,0:T(8,128)(2,1)S(1)} %add_convert_fusion), channel_id=1, source_target_pairs={{0,96},{96,0},{32,64},{64,32},{1,97},{97,1},{33,65},{65,33},{2,98}... | collective-permute-start | bytes 61448 | tf_op jit(solution)/shard_map/ppermute | solution.py:40
  112.2 11.6 %all-to-all-start.3 = ((bf16[16,40,256]{2,1,0:T(8,128)(2,1)}), bf16[16,40,256]{2,1,0:T(8,128)(2,1)S(1)}, u32[]{:S(2)}, u32[]{:S(2)}) async-start(bf16[16,40,256]{2,1,0:T(8,128)(2,1)} %broadcast_in_dim.15), calls=%async_computation.3 | async-start | bytes 655360 | tf_op jit(solution)/shard_map/all_to_all | solution.py:23
  116.0 1.3 copy-start.3
  123.8 9.9 %collective-permute-start.8 = (bf16[640,256]{1,0:T(8,128)(2,1)S(1)}, bf16[640,256]{1,0:T(8,128)(2,1)S(1)}, u32[]{:S(2)}, u32[]{:S(2)}) collective-permute-start(bf16[640,256]{1,0:T(8,128)(2,1)S(1)} %bitcast.32), channel_id=1, source_target_pairs={{0,4},{4,0},{1,5},{5,1},{2,6},{6,2},{3,7},{7,3},{8,12},{12,8},{9,1... | collective-permute-start | bytes 983048 | tf_op jit(solution)/shard_map/ppermute | solution.py:246
  133.7 1.1 copy-start.12
Sparse Core Ops, SparseCore 0:
  18.5 42.4 all-gather.1
  64.4 41.4 reduce-scatter.1

commit v6 on v5

--- a/solution.py
+++ b/solution.py
@@ -41,9 +41,9 @@
     return values
 
 
-VMEM = pl.BlockSpec(memory_space=pltpu.VMEM)
+WHOLE = pl.BlockSpec()
 SMEM = pl.BlockSpec(memory_space=pltpu.SMEM)
-ROOM = pltpu.CompilerParams(vmem_limit_bytes=40 * 2**20)
+ROOM = pltpu.CompilerParams(vmem_limit_bytes=63 * 2**20)
 
 
 def cost(flops, moved):
@@ -66,8 +66,8 @@
     return pl.pallas_call(
         mixed_kernel,
         out_shape=jax.ShapeDtypeStruct((256, 2560), BF16),
-        in_specs=[SMEM, VMEM, VMEM, VMEM],
-        out_specs=VMEM,
+        in_specs=[SMEM, WHOLE, WHOLE, WHOLE],
+        out_specs=WHOLE,
         compiler_params=ROOM,
         cost_estimate=cost(2 * 256 * 640 * 2560, 5_000_000),
     )(core, x_heads, own, other)
@@ -92,8 +92,8 @@
     return pl.pallas_call(
         head_kernel,
         out_shape=jax.ShapeDtypeStruct((256, 640), BF16),
-        in_specs=[SMEM, VMEM, VMEM, VMEM],
-        out_specs=VMEM,
+        in_specs=[SMEM, WHOLE, WHOLE, WHOLE],
+        out_specs=WHOLE,
         compiler_params=ROOM,
         cost_estimate=cost(2 * 256 * 640 * 2560, 5_000_000),
     )(core, grads, own, other)
@@ -115,8 +115,8 @@
     return pl.pallas_call(
         ordered_kernel,
         out_shape=(x_shape, x_shape, jax.ShapeDtypeStruct((128, 2560), BF16)),
-        in_specs=[VMEM] * 6,
-        out_specs=(VMEM,) * 3,
+        in_specs=[WHOLE] * 6,
+        out_specs=(WHOLE,) * 3,
         compiler_params=ROOM,
         cost_estimate=cost(2 * 640 * 640 * 1024, 4_200_000),
     )(order, arrival, rows, rows_other, grads, grads_other)
@@ -132,8 +132,8 @@
     return pl.pallas_call(
         reduced_kernel,
         out_shape=jax.ShapeDtypeStruct((4, 128, 256), BF16),
-        in_specs=[VMEM] * 2,
-        out_specs=VMEM,
+        in_specs=[WHOLE] * 2,
+        out_specs=WHOLE,
         compiler_params=ROOM,
         cost_estimate=cost(2 * 128 * 256 * 2560, 2_500_000),
     )(basis, grads)
@@ -154,8 +154,8 @@
     return pl.pallas_call(
         low_kernel,
         out_shape=jax.ShapeDtypeStruct((640, 256), BF16),
-        in_specs=[VMEM] * 3,
-        out_specs=VMEM,
+        in_specs=[WHOLE] * 3,
+        out_specs=WHOLE,
         compiler_params=ROOM,
         cost_estimate=cost(2 * 512 * 256 * 640, 1_500_000),
     )(reduced, rows, rows_other)
@@ -177,8 +177,8 @@
     return pl.pallas_call(
         update_kernel,
         out_shape=jax.ShapeDtypeStruct((640, half), BF16),
-        in_specs=[VMEM] * 5,
-        out_specs=VMEM,
+        in_specs=[WHOLE] * 5,
+        out_specs=WHOLE,
         compiler_params=ROOM,
         cost_estimate=cost(2 * 640 * 512 * (640 + half), 5_000_000),
     )(rows, rows_other, order, basis, basis_other)

time: 146 us -> 146 us (level)
  Pallas kernels: 14.1 us -> 22.4 us
  local copies, waits for them, and re-layouts: 17.5 us -> 10.6 us
  starting transfers between devices: 78.9 us -> 77.3 us
    unnamed x36 -> x18, local copies, waits for them, and re-layouts: 13.7 us -> 2.9 us
    ppermute x2, starting transfers between devices: 14.5 us -> 10.6 us  [sum_zh(): values = sent.astype(F32) + lax.ppermute(sent, 'zh', partners).astype(F32)]
    ppermute x2, waiting for transfers between devices: 2.99 us -> 6.41 us  [sum_zh(): values = sent.astype(F32) + lax.ppermute(sent, 'zh', partners).astype(F32)]
    all_to_all x1, starting transfers between devices: 4.92 us -> 7.82 us  [shards(): reduced = lax.all_to_all(reduced, 'zl', 0, 0, tiled=True)]
    transpose x2, local copies, waits for them, and re-layouts: 0.09 us -> 2.88 us  [natural(): rows.reshape(2, 4, 4, 40, 256).transpose(0, 2, 1, 3, 4).reshape(half, 256)]
    all_to_all x1, waiting for transfers between devices: 6.76 us -> 5 us  [shards(): lax.all_to_all(low_chip.reshape(16, 40, 256), ('y', 'x'), 0, 0, tiled=True)]
    pallas_call x1, Pallas kernels: 3 us -> 4.72 us  [update_matmul(): pl.pallas_call(update_kernel, out_shape=jax.ShapeDtypeStruct((640, half),...]
    pallas_call x1, Pallas kernels: 2.64 us -> 4.26 us  [mixed_matmul(): pl.pallas_call(mixed_kernel, out_shape=jax.ShapeDtypeStruct((256, 2560),...]
  transfers between devices with their start and end apart: 15 -> 15, of which waited for: 8 -> 8; matrix products, arithmetic and copies ran while one was open for 2% -> 5% of each run, Pallas kernels for 8% -> 12%
where the time goes in v6:
time: 146 us; the launch traced here: 145 us
  starting transfers between devices  77.3 us (53%)
  Pallas kernels  22.4 us (15%)
  waiting for transfers between devices  20.4 us (14%)
  between operations  14.3 us (10%)
  local copies, waits for them, and re-layouts  10.6 us (7%)
    ppermute x2, starting transfers between devices, sum_zh(): values = sent.astype(F32) + lax.ppermute(sent, 'zh', partners).astype(F32)  10.6 us
    all_to_all x2, starting transfers between devices, spread(): return lax.all_to_all(copies, axes, 0, 0, tiled=True)  10.6 us
    ppermute x1, starting transfers between devices, gather_zh(): got = lax.ppermute(values, 'zh', PAIR)  9.65 us
    ppermute x1, starting transfers between devices, gather_zh(): got = lax.ppermute(pair, 'zh', MIRROR)  9.28 us
    ppermute x1, starting transfers between devices, shards(): rows_other = lax.ppermute(rows, 'core', CORE_SWAP)  9.06 us
    all_to_all x1, starting transfers between devices, shards(): reduced = lax.all_to_all(reduced, 'zl', 0, 0, tiled=True)  7.82 us
    ppermute x2, waiting for transfers between devices, sum_zh(): values = sent.astype(F32) + lax.ppermute(sent, 'zh', partners).astype(F32)  6.41 us
    ppermute x1, starting transfers between devices, shards(): x_other = lax.ppermute(x_heads, 'core', CORE_SWAP)  5.81 us
  transfers between devices with their start and end apart: 15, of which 8 were waited for; matrix products, arithmetic and copies ran while one was open for 5% of the time, Pallas kernels for 12%

profile of v6, /device:TPU:1, one launch (start us, length us, event | category | flops | bytes accessed | tf_op | source)
XLA Modules:
  0.0 145.2 jit_solution(11698853410039089039)
XLA Ops:
  8.0 0.7 dynamic-slice_convert_fusion
  8.7 9.6 %collective-permute-start = (bf16[60,256]{1,0:T(8,128)(2,1)S(1)}, bf16[60,256]{1,0:T(8,128)(2,1)S(1)}, u32[]{:S(2)}, u32[]{:S(2)}) collective-permute-start(bf16[60,256]{1,0:T(8,128)(2,1)S(1)} %pad_maximum_fusion.2), channel_id=1, source_target_pairs={{0,32},{32,0},{64,96},{96,64},{1,33},{33,1},{65,97},{97,65},{2,34}... | collective-permute-start | bytes 92168 | tf_op jit(solution)/shard_map/ppermute | solution.py:28
  18.4 2.9 %collective-permute-start.2 = (bf16[640,1280]{1,0:T(8,128)(2,1)}, bf16[640,1280]{1,0:T(8,128)(2,1)}, u32[]{:S(2)}, u32[]{:S(2)}) collective-permute-start(bf16[640,1280]{1,0:T(8,128)(2,1)} %own_ref.3), channel_id=1, source_target_pairs={{0,4},{4,0},{1,5},{5,1},{2,6},{6,2},{3,7},{7,3},{8,12},{12,8},{9,1... | collective-permute-start | bytes 4915208 | tf_op jit(solution)/shard_map/ppermute | solution.py:196
  21.4 9.3 %collective-permute-start.1 = (bf16[120,256]{1,0:T(8,128)(2,1)S(1)}, bf16[120,256]{1,0:T(8,128)(2,1)S(1)}, u32[]{:S(2)}, u32[]{:S(2)}) collective-permute-start(bf16[120,256]{1,0:T(8,128)(2,1)S(1)} %pad_maximum_fusion.1), channel_id=1, source_target_pairs={{0,96},{96,0},{32,64},{64,32},{1,97},{97,1},{33,65},{65,33},{2,98}... | collective-permute-start | bytes 184328 | tf_op jit(solution)/shard_map/ppermute | solution.py:31
  30.6 1.9 %collective-permute-done.1 = bf16[120,256]{1,0:T(8,128)(2,1)S(1)} collective-permute-done((bf16[120,256]{1,0:T(8,128)(2,1)S(1)}, bf16[120,256]{1,0:T(8,128)(2,1)S(1)}, u32[]{:S(2)}, u32[]{:S(2)}) %collective-permute-start.1) | collective-permute-done | bytes 61472 | tf_op jit(solution)/shard_map/ppermute | solution.py:31
  32.7 1.3 broadcast_in_dim.14
  33.9 6.9 %all-to-all-start = ((bf16[16,160,256]{2,1,0:T(8,128)(2,1)}), bf16[16,160,256]{2,1,0:T(8,128)(2,1)}, u32[]{:S(2)}, u32[]{:S(2)}) async-start(bf16[16,160,256]{2,1,0:T(8,128)(2,1)} %broadcast_in_dim.14), calls=%async_computation | async-start | bytes 2621440 | tf_op jit(solution)/shard_map/all_to_all | solution.py:23
  40.9 5.8 %collective-permute-start.3 = (bf16[256,640]{1,0:T(8,128)(2,1)S(1)}, bf16[256,640]{1,0:T(8,128)(2,1)S(1)}, u32[]{:S(2)}, u32[]{:S(2)}) collective-permute-start(bf16[256,640]{1,0:T(8,128)(2,1)S(1)} %copy-done.2), channel_id=1, source_target_pairs={{0,4},{4,0},{1,5},{5,1},{2,6},{6,2},{3,7},{7,3},{8,12},{12,8},{9,1... | collective-permute-start | bytes 983048 | tf_op jit(solution)/shard_map/ppermute | solution.py:198
  46.7 1.9 %collective-permute-start.4 = (bf16[64,2560]{1,0:T(8,128)(2,1)S(1)}, bf16[64,2560]{1,0:T(8,128)(2,1)}, u32[]{:S(2)}, u32[]{:S(2)}) collective-permute-start(bf16[64,2560]{1,0:T(8,128)(2,1)S(1)} %copy-done.3), channel_id=1, source_target_pairs={{0,4},{4,0},{1,5},{5,1},{2,6},{6,2},{3,7},{7,3},{8,12},{12,8},{9,1... | collective-permute-start | bytes 983048 | tf_op jit(solution)/shard_map/ppermute | solution.py:197
  50.4 4.4 %shard_map.104 = (bf16[256,640]{1,0:T(8,128)(2,1)}, bf16[256,640]{1,0:T(8,128)(2,1)}, bf16[128,2560]{1,0:T(8,128)(2,1)}) custom-call(bf16[640,640]{1,0:T(8,128)(2,1)} %constant.63.clone.order_ref, bf16[640,640]{1,0:T(8,128)(2,1)} %constant.64.clone.arrival_ref, bf16[256,640]{1,0:T(8,128)(2,1)} %x_ref.3, bf16[256,640]{1,0:T(8,128)(2,1)} %copy-done.6, ...), custom_call_target="tpu_custom_call" | custom-call | flops 838860800 | bytes 4200000 | tf_op jit(solution)/shard_map/pallas_call | solution.py:115
  54.8 4.3 %shard_map.103 = bf16[256,2560]{1,0:T(8,128)(2,1)} custom-call(s32[1]{0:T(128)} %bitcast.3.core_ref, bf16[256,640]{1,0:T(8,128)(2,1)} %x_ref.3, bf16[640,1280]{1,0:T(8,128)(2,1)} %own_ref.3, bf16[640,1280]{1,0:T(8,128)(2,1)} %collective-permute-done.2.other_ref), custom_call_target="tpu_custom_call" | custom-call | flops 838860800 | bytes 5000000 | tf_op jit(solution)/shard_map/pallas_call | solution.py:66
  59.1 2.5 %shard_map.105 = bf16[4,128,256]{2,1,0:T(8,128)(2,1)} custom-call(bf16[2560,256]{1,0:T(8,128)(2,1)} %bitcast.4.basis_ref, bf16[128,2560]{1,0:T(8,128)(2,1)} %get-tuple-element.28.grad_ref), custom_call_target="tpu_custom_call" | custom-call | flops 167772160 | bytes 2500000 | tf_op jit(solution)/shard_map/pallas_call | solution.py:132
  61.6 7.8 %all-to-all-start.1 = ((bf16[4,128,256]{2,1,0:T(8,128)(2,1)}), bf16[4,128,256]{2,1,0:T(8,128)(2,1)S(1)}, u32[]{:S(2)}, u32[]{:S(2)}) async-start(bf16[4,128,256]{2,1,0:T(8,128)(2,1)} %shard_map.105), calls=%async_computation.1 | async-start | bytes 524288 | tf_op jit(solution)/shard_map/all_to_all | solution.py:216
  69.4 1.4 dynamic-slice_bitcast_fusion
  70.8 5.4 %collective-permute-start.5 = (bf16[8,160,256]{2,1,0:T(8,128)(2,1)S(1)}, bf16[8,160,256]{2,1,0:T(8,128)(2,1)}, u32[]{:S(2)}, u32[]{:S(2)}) collective-permute-start(bf16[8,160,256]{2,1,0:T(8,128)(2,1)S(1)} %get-tuple-element.44), channel_id=1, source_target_pairs={{0,4},{4,0},{1,5},{5,1},{2,6},{6,2},{3,7},{7,3},{8,12},{12,8},{9,1... | collective-permute-start | bytes 1966088 | tf_op jit(solution)/shard_map/ppermute | solution.py:219
  76.2 1.8 %collective-permute-done.5 = bf16[8,160,256]{2,1,0:T(8,128)(2,1)} collective-permute-done((bf16[8,160,256]{2,1,0:T(8,128)(2,1)S(1)}, bf16[8,160,256]{2,1,0:T(8,128)(2,1)}, u32[]{:S(2)}, u32[]{:S(2)}) %collective-permute-start.5) | collective-permute-done | bytes 655392 | tf_op jit(solution)/shard_map/ppermute | solution.py:219
  78.7 2.3 %shard_map.106 = bf16[640,256]{1,0:T(8,128)(2,1)} custom-call(bf16[4,128,256]{2,1,0:T(8,128)(2,1)} %copy-done.1, bf16[256,640]{1,0:T(8,128)(2,1)} %get-tuple-element.30.own_ref, bf16[256,640]{1,0:T(8,128)(2,1)} %get-tuple-element.31.other_ref), custom_call_target="tpu_custom_call" | custom-call | flops 167772160 | bytes 1500000 | tf_op jit(solution)/shard_map/pallas_call | solution.py:154
  81.0 4.3 %all-to-all-start.2 = ((bf16[16,40,256]{2,1,0:T(8,128)(2,1)}), bf16[16,40,256]{2,1,0:T(8,128)(2,1)S(1)}, u32[]{:S(2)}, u32[]{:S(2)}) async-start(bf16[16,40,256]{2,1,0:T(8,128)(2,1)} %bitcast.29), calls=%async_computation.2 | async-start | bytes 655360 | tf_op jit(solution)/shard_map/all_to_all | solution.py:226
  85.3 0.9 copy.11
  86.2 2.0 %copy.12 = bf16[2,4,4,40,256]{4,3,2,1,0:T(8,128)(2,1)} copy(bf16[2,4,4,40,256]{4,3,1,2,0:T(8,128)(2,1)} %bitcast.13) | data formatting | bytes 1310720 | tf_op jit(solution)/shard_map/transpose | solution.py:230
  88.2 5.0 %all-to-all-done.2 = bf16[16,40,256]{2,1,0:T(8,128)(2,1)S(1)} async-done(((bf16[16,40,256]{2,1,0:T(8,128)(2,1)}), bf16[16,40,256]{2,1,0:T(8,128)(2,1)S(1)}, u32[]{:S(2)}, u32[]{:S(2)}) %all-to-all-start.2) | async-done | bytes 327712 | tf_op jit(solution)/shard_map/all_to_all | solution.py:226
  93.3 5.0 %collective-permute-start.6 = (bf16[40,256]{1,0:T(8,128)(2,1)S(1)}, bf16[40,256]{1,0:T(8,128)(2,1)S(1)}, u32[]{:S(2)}, u32[]{:S(2)}) collective-permute-start(bf16[40,256]{1,0:T(8,128)(2,1)S(1)} %reduce_sum.12), channel_id=1, source_target_pairs={{0,32},{32,0},{64,96},{96,64},{1,33},{33,1},{65,97},{97,65},{2,34}... | collective-permute-start | bytes 61448 | tf_op jit(solution)/shard_map/ppermute | solution.py:40
  98.2 3.6 %collective-permute-done.6 = bf16[40,256]{1,0:T(8,128)(2,1)S(1)} collective-permute-done((bf16[40,256]{1,0:T(8,128)(2,1)S(1)}, bf16[40,256]{1,0:T(8,128)(2,1)S(1)}, u32[]{:S(2)}, u32[]{:S(2)}) %collective-permute-start.6) | collective-permute-done | bytes 20512 | tf_op jit(solution)/shard_map/ppermute | solution.py:40
  101.8 5.6 %collective-permute-start.7 = (bf16[40,256]{1,0:T(8,128)(2,1)S(1)}, bf16[40,256]{1,0:T(8,128)(2,1)S(1)}, u32[]{:S(2)}, u32[]{:S(2)}) collective-permute-start(bf16[40,256]{1,0:T(8,128)(2,1)S(1)} %add_convert_fusion), channel_id=1, source_target_pairs={{0,96},{96,0},{32,64},{64,32},{1,97},{97,1},{33,65},{65,33},{2,98}... | collective-permute-start | bytes 61448 | tf_op jit(solution)/shard_map/ppermute | solution.py:40
  107.4 2.8 %collective-permute-done.7 = bf16[40,256]{1,0:T(8,128)(2,1)S(1)} collective-permute-done((bf16[40,256]{1,0:T(8,128)(2,1)S(1)}, bf16[40,256]{1,0:T(8,128)(2,1)S(1)}, u32[]{:S(2)}, u32[]{:S(2)}) %collective-permute-start.7) | collective-permute-done | bytes 20512 | tf_op jit(solution)/shard_map/ppermute | solution.py:40
  110.3 0.8 broadcast_in_dim.15
  111.1 3.6 %all-to-all-start.3 = ((bf16[16,40,256]{2,1,0:T(8,128)(2,1)}), bf16[16,40,256]{2,1,0:T(8,128)(2,1)S(1)}, u32[]{:S(2)}, u32[]{:S(2)}) async-start(bf16[16,40,256]{2,1,0:T(8,128)(2,1)} %broadcast_in_dim.15), calls=%async_computation.3 | async-start | bytes 655360 | tf_op jit(solution)/shard_map/all_to_all | solution.py:23
  114.7 4.2 %shard_map.107 = bf16[256,640]{1,0:T(8,128)(2,1)} custom-call(s32[1]{0:T(128)} %bitcast.3.core_ref, bf16[256,2560]{1,0:T(8,128)(2,1)} %all-gather.2.cloned.1.call-done.grad_ref, bf16[640,1280]{1,0:T(8,128)(2,1)} %own_ref.3, bf16[640,1280]{1,0:T(8,128)(2,1)} %collective-permute-done.2.other_ref), custom_call_target="tpu_custom_call" | custom-call | flops 838860800 | bytes 5000000 | tf_op jit(solution)/shard_map/pallas_call | solution.py:92
  119.0 3.6 %all-to-all-done.3 = bf16[16,40,256]{2,1,0:T(8,128)(2,1)S(1)} async-done(((bf16[16,40,256]{2,1,0:T(8,128)(2,1)}), bf16[16,40,256]{2,1,0:T(8,128)(2,1)S(1)}, u32[]{:S(2)}, u32[]{:S(2)}) %all-to-all-start.3) | async-done | bytes 327712 | tf_op jit(solution)/shard_map/all_to_all | solution.py:23
  122.6 9.1 %collective-permute-start.8 = (bf16[640,256]{1,0:T(8,128)(2,1)S(1)}, bf16[640,256]{1,0:T(8,128)(2,1)S(1)}, u32[]{:S(2)}, u32[]{:S(2)}) collective-permute-start(bf16[640,256]{1,0:T(8,128)(2,1)S(1)} %bitcast.32), channel_id=1, source_target_pairs={{0,4},{4,0},{1,5},{5,1},{2,6},{6,2},{3,7},{7,3},{8,12},{12,8},{9,1... | collective-permute-start | bytes 983048 | tf_op jit(solution)/shard_map/ppermute | solution.py:246
  131.7 1.2 collective-permute-done.8.other_ref
  133.6 4.7 %shard_map.108 = bf16[640,1280]{1,0:T(8,128)(2,1)} custom-call(bf16[640,256]{1,0:T(8,128)(2,1)} %bitcast.33, bf16[640,256]{1,0:T(8,128)(2,1)} %copy-done.7, bf16[640,640]{1,0:T(8,128)(2,1)} %constant.63.clone.order_ref, bf16[1280,256]{1,0:T(8,128)(2,1)} %bitcast.30, bf16[1280,256]{1,0:T(8,128)(2,1)} %bitcast.31), custom_call_target="tpu_custom_call" | custom-call | flops 1258291200 | bytes 5000000 | tf_op jit(solution)/shard_map/pallas_call | solution.py:177
  (44 shorter events, 4.3 us)
Async XLA Ops:
  7.2 0.8 copy-start
  7.2 107.6 %all-gather.2.cloned.1.call-start = ((), (), s32[]{:S(2)}) async-start(), calls=%async_computation.5 | async-start | bytes 1638400 | tf_op jit(solution)/shard_map/all_gather | solution.py:195
  8.7 12.6 %collective-permute-start = (bf16[60,256]{1,0:T(8,128)(2,1)S(1)}, bf16[60,256]{1,0:T(8,128)(2,1)S(1)}, u32[]{:S(2)}, u32[]{:S(2)}) collective-permute-start(bf16[60,256]{1,0:T(8,128)(2,1)S(1)} %pad_maximum_fusion.2), channel_id=1, source_target_pairs={{0,32},{32,0},{64,96},{96,64},{1,33},{33,1},{65,97},{97,65},{2,34}... | collective-permute-start | bytes 92168 | tf_op jit(solution)/shard_map/ppermute | solution.py:28
  18.4 36.4 %collective-permute-start.2 = (bf16[640,1280]{1,0:T(8,128)(2,1)}, bf16[640,1280]{1,0:T(8,128)(2,1)}, u32[]{:S(2)}, u32[]{:S(2)}) collective-permute-start(bf16[640,1280]{1,0:T(8,128)(2,1)} %own_ref.3), channel_id=1, source_target_pairs={{0,4},{4,0},{1,5},{5,1},{2,6},{6,2},{3,7},{7,3},{8,12},{12,8},{9,1... | collective-permute-start | bytes 4915208 | tf_op jit(solution)/shard_map/ppermute | solution.py:196
  21.4 11.2 %collective-permute-start.1 = (bf16[120,256]{1,0:T(8,128)(2,1)S(1)}, bf16[120,256]{1,0:T(8,128)(2,1)S(1)}, u32[]{:S(2)}, u32[]{:S(2)}) collective-permute-start(bf16[120,256]{1,0:T(8,128)(2,1)S(1)} %pad_maximum_fusion.1), channel_id=1, source_target_pairs={{0,96},{96,0},{32,64},{64,32},{1,97},{97,1},{33,65},{65,33},{2,98}... | collective-permute-start | bytes 184328 | tf_op jit(solution)/shard_map/ppermute | solution.py:31
  33.9 7.0 %copy-start.2 = (bf16[256,640]{1,0:T(8,128)(2,1)S(1)}, bf16[256,640]{1,0:T(8,128)(2,1)}, u32[]{:S(2)}) copy-start(bf16[256,640]{1,0:T(8,128)(2,1)} %x_ref.3) | copy-start | bytes 983044
  33.9 12.8 %copy-start.3 = (bf16[64,2560]{1,0:T(8,128)(2,1)S(1)}, bf16[64,2560]{1,0:T(8,128)(2,1)}, u32[]{:S(2)}) copy-start(bf16[64,2560]{1,0:T(8,128)(2,1)} %g_ref.1) | copy-start | bytes 983044
  33.9 25.1 %all-to-all-start = ((bf16[16,160,256]{2,1,0:T(8,128)(2,1)}), bf16[16,160,256]{2,1,0:T(8,128)(2,1)}, u32[]{:S(2)}, u32[]{:S(2)}) async-start(bf16[16,160,256]{2,1,0:T(8,128)(2,1)} %broadcast_in_dim.14), calls=%async_computation | async-start | bytes 2621440 | tf_op jit(solution)/shard_map/all_to_all | solution.py:23
  40.8 81.8 %reduce-scatter.2.cloned.1.call-start = ((), (), s32[]{:S(2)}) async-start(), calls=%async_computation.6 | async-start | bytes 1638400 | tf_op jit(solution)/shard_map/reduce_scatter | solution.py:213
  40.9 8.4 %collective-permute-start.3 = (bf16[256,640]{1,0:T(8,128)(2,1)S(1)}, bf16[256,640]{1,0:T(8,128)(2,1)S(1)}, u32[]{:S(2)}, u32[]{:S(2)}) collective-permute-start(bf16[256,640]{1,0:T(8,128)(2,1)S(1)} %copy-done.2), channel_id=1, source_target_pairs={{0,4},{4,0},{1,5},{5,1},{2,6},{6,2},{3,7},{7,3},{8,12},{12,8},{9,1... | collective-permute-start | bytes 983048 | tf_op jit(solution)/shard_map/ppermute | solution.py:198
  46.7 3.7 %collective-permute-start.4 = (bf16[64,2560]{1,0:T(8,128)(2,1)S(1)}, bf16[64,2560]{1,0:T(8,128)(2,1)}, u32[]{:S(2)}, u32[]{:S(2)}) collective-permute-start(bf16[64,2560]{1,0:T(8,128)(2,1)S(1)} %copy-done.3), channel_id=1, source_target_pairs={{0,4},{4,0},{1,5},{5,1},{2,6},{6,2},{3,7},{7,3},{8,12},{12,8},{9,1... | collective-permute-start | bytes 983048 | tf_op jit(solution)/shard_map/ppermute | solution.py:197
  49.3 0.7 copy-start.6
  61.6 16.4 %all-to-all-start.1 = ((bf16[4,128,256]{2,1,0:T(8,128)(2,1)}), bf16[4,128,256]{2,1,0:T(8,128)(2,1)S(1)}, u32[]{:S(2)}, u32[]{:S(2)}) async-start(bf16[4,128,256]{2,1,0:T(8,128)(2,1)} %shard_map.105), calls=%async_computation.1 | async-start | bytes 524288 | tf_op jit(solution)/shard_map/all_to_all | solution.py:216
  70.8 7.2 %collective-permute-start.5 = (bf16[8,160,256]{2,1,0:T(8,128)(2,1)S(1)}, bf16[8,160,256]{2,1,0:T(8,128)(2,1)}, u32[]{:S(2)}, u32[]{:S(2)}) collective-permute-start(bf16[8,160,256]{2,1,0:T(8,128)(2,1)S(1)} %get-tuple-element.44), channel_id=1, source_target_pairs={{0,4},{4,0},{1,5},{5,1},{2,6},{6,2},{3,7},{7,3},{8,12},{12,8},{9,1... | collective-permute-start | bytes 1966088 | tf_op jit(solution)/shard_map/ppermute | solution.py:219
  78.0 0.7 copy-start.1
  81.0 12.2 %all-to-all-start.2 = ((bf16[16,40,256]{2,1,0:T(8,128)(2,1)}), bf16[16,40,256]{2,1,0:T(8,128)(2,1)S(1)}, u32[]{:S(2)}, u32[]{:S(2)}) async-start(bf16[16,40,256]{2,1,0:T(8,128)(2,1)} %bitcast.29), calls=%async_computation.2 | async-start | bytes 655360 | tf_op jit(solution)/shard_map/all_to_all | solution.py:226
  85.3 25.0 %copy-start.5 = (bf16[40,256]{1,0:T(8,128)(2,1)S(1)}, bf16[40,256]{1,0:T(8,128)(2,1)}, u32[]{:S(2)}) copy-start(bf16[40,256]{1,0:T(8,128)(2,1)} %reshape.50) | copy-start | bytes 61444
  93.3 8.6 %collective-permute-start.6 = (bf16[40,256]{1,0:T(8,128)(2,1)S(1)}, bf16[40,256]{1,0:T(8,128)(2,1)S(1)}, u32[]{:S(2)}, u32[]{:S(2)}) collective-permute-start(bf16[40,256]{1,0:T(8,128)(2,1)S(1)} %reduce_sum.12), channel_id=1, source_target_pairs={{0,32},{32,0},{64,96},{96,64},{1,33},{33,1},{65,97},{97,65},{2,34}... | collective-permute-start | bytes 61448 | tf_op jit(solution)/shard_map/ppermute | solution.py:40
  101.8 8.4 %collective-permute-start.7 = (bf16[40,256]{1,0:T(8,128)(2,1)S(1)}, bf16[40,256]{1,0:T(8,128)(2,1)S(1)}, u32[]{:S(2)}, u32[]{:S(2)}) collective-permute-start(bf16[40,256]{1,0:T(8,128)(2,1)S(1)} %add_convert_fusion), channel_id=1, source_target_pairs={{0,96},{96,0},{32,64},{64,32},{1,97},{97,1},{33,65},{65,33},{2,98}... | collective-permute-start | bytes 61448 | tf_op jit(solution)/shard_map/ppermute | solution.py:40
  111.1 11.5 %all-to-all-start.3 = ((bf16[16,40,256]{2,1,0:T(8,128)(2,1)}), bf16[16,40,256]{2,1,0:T(8,128)(2,1)S(1)}, u32[]{:S(2)}, u32[]{:S(2)}) async-start(bf16[16,40,256]{2,1,0:T(8,128)(2,1)} %broadcast_in_dim.15), calls=%async_computation.3 | async-start | bytes 655360 | tf_op jit(solution)/shard_map/all_to_all | solution.py:23
  122.6 10.3 %copy-start.4 = (bf16[16,40,256]{2,1,0:T(8,128)(2,1)}, bf16[16,40,256]{2,1,0:T(8,128)(2,1)S(1)}, u32[]{:S(2)}) copy-start(bf16[16,40,256]{2,1,0:T(8,128)(2,1)S(1)} %all-to-all-done.3) | copy-start | bytes 983044
  122.6 10.3 %collective-permute-start.8 = (bf16[640,256]{1,0:T(8,128)(2,1)S(1)}, bf16[640,256]{1,0:T(8,128)(2,1)S(1)}, u32[]{:S(2)}, u32[]{:S(2)}) collective-permute-start(bf16[640,256]{1,0:T(8,128)(2,1)S(1)} %bitcast.32), channel_id=1, source_target_pairs={{0,4},{4,0},{1,5},{5,1},{2,6},{6,2},{3,7},{7,3},{8,12},{12,8},{9,1... | collective-permute-start | bytes 983048 | tf_op jit(solution)/shard_map/ppermute | solution.py:246
  132.9 0.7 copy-start.7
Sparse Core Ops, SparseCore 0:
  18.5 42.5 all-gather.1
  64.5 41.3 reduce-scatter.1

commit v7 on v6

--- a/solution.py
+++ b/solution.py
@@ -42,6 +42,7 @@
 
 
 WHOLE = pl.BlockSpec()
+FAR = pl.BlockSpec(memory_space=pltpu.HBM)
 SMEM = pl.BlockSpec(memory_space=pltpu.SMEM)
 ROOM = pltpu.CompilerParams(vmem_limit_bytes=63 * 2**20)
 
@@ -122,29 +123,56 @@
     )(order, arrival, rows, rows_other, grads, grads_other)
 
 
-def reduced_kernel(basis_ref, grad_ref, out_ref):
-    part = jnp.dot(grad_ref[...], basis_ref[...], preferred_element_type=F32).astype(BF16)
+def fetch(pairs, sems):
+    copies = [
+        pltpu.make_async_copy(source, target, sems.at[i]) for i, (source, target) in enumerate(pairs)
+    ]
+    for copy in copies:
+        copy.start()
+    return copies
+
+
+def reduced_kernel(basis_hbm, grad_hbm, out_ref, basis_ref, grad_ref, sems):
+    blocks = [slice(640 * y, 640 * (y + 1)) for y in range(4)]
+    pairs = [(grad_hbm, grad_ref)]
+    pairs += [(basis_hbm.at[block], basis_ref.at[block]) for block in blocks]
+    copies = fetch(pairs, sems)
+    copies[0].wait()
+    total = None
+    for block, copy in zip(blocks, copies[1:]):
+        copy.wait()
+        part = jnp.dot(grad_ref[:, block], basis_ref[block], preferred_element_type=F32)
+        total = part if total is None else total + part
     for target in range(out_ref.shape[0]):
-        out_ref[target] = part
+        out_ref[target] = total.astype(BF16)
 
 
 def reduced_matmul(basis, grads):
     return pl.pallas_call(
         reduced_kernel,
         out_shape=jax.ShapeDtypeStruct((4, 128, 256), BF16),
-        in_specs=[WHOLE] * 2,
+        in_specs=[FAR, FAR],
         out_specs=WHOLE,
+        scratch_shapes=[
+            pltpu.VMEM((2560, 256), BF16),
+            pltpu.VMEM((128, 2560), BF16),
+            pltpu.SemaphoreType.DMA((5,)),
+        ],
         compiler_params=ROOM,
         cost_estimate=cost(2 * 128 * 256 * 2560, 2_500_000),
     )(basis, grads)
 
 
-def low_kernel(reduced_ref, own_ref, other_ref, out_ref):
+def low_kernel(reduced_hbm, own_hbm, other_hbm, out_ref, reduced_ref, rows_ref, sems):
+    pairs = [(own_hbm, rows_ref.at[0]), (other_hbm, rows_ref.at[1]), (reduced_hbm, reduced_ref)]
+    copies = fetch(pairs, sems)
+    copies[2].wait()
     total = None
-    for which, rows in ((0, own_ref), (1, other_ref)):
+    for which in range(2):
+        copies[which].wait()
         reduced = reduced_ref[:, 64 * which : 64 * (which + 1)].reshape(256, 256)
         part = lax.dot_general(
-            rows[...], reduced, (((0,), (0,)), ((), ())), preferred_element_type=F32
+            rows_ref[which], reduced, (((0,), (0,)), ((), ())), preferred_element_type=F32
         )
         total = part if total is None else total + part
     out_ref[...] = total.astype(BF16)
@@ -154,22 +182,58 @@
     return pl.pallas_call(
         low_kernel,
         out_shape=jax.ShapeDtypeStruct((640, 256), BF16),
-        in_specs=[WHOLE] * 3,
+        in_specs=[FAR, FAR, FAR],
         out_specs=WHOLE,
+        scratch_shapes=[
+            pltpu.VMEM((4, 128, 256), BF16),
+            pltpu.VMEM((2, 256, 640), BF16),
+            pltpu.SemaphoreType.DMA((3,)),
+        ],
         compiler_params=ROOM,
         cost_estimate=cost(2 * 512 * 256 * 640, 1_500_000),
     )(reduced, rows, rows_other)
 
 
-def update_kernel(own_ref, other_ref, order_ref, basis_ref, basis_other_ref, out_ref):
-    total = None
-    for rows, basis in ((own_ref, basis_ref), (other_ref, basis_other_ref)):
-        direction = jnp.dot(order_ref[...], rows[...], preferred_element_type=F32).astype(BF16)
-        part = lax.dot_general(
-            direction, basis[...], (((1,), (1,)), ((), ())), preferred_element_type=F32
-        )
-        total = part if total is None else total + part
-    out_ref[...] = total.astype(BF16)
+def update_kernel(
+    own_hbm, other_hbm, order_hbm, basis_hbm, basis_other_hbm, out_hbm,
+    rows_ref, order_ref, basis_ref, out_ref, sems, out_sems,
+):
+    copies = fetch(
+        [
+            (order_hbm, order_ref),
+            (own_hbm, rows_ref.at[0]),
+            (other_hbm, rows_ref.at[1]),
+            (basis_hbm, basis_ref.at[0]),
+            (basis_other_hbm, basis_ref.at[1]),
+        ],
+        sems,
+    )
+    copies[0].wait()
+    directions = []
+    for which in range(2):
+        copies[1 + which].wait()
+        moved = jnp.dot(order_ref[...], rows_ref[which], preferred_element_type=F32)
+        directions.append(moved.astype(BF16))
+    copies[3].wait()
+    copies[4].wait()
+    leaving = []
+    for block in range(out_ref.shape[0]):
+        cols = slice(256 * block, 256 * (block + 1))
+        parts = [
+            lax.dot_general(
+                directions[which],
+                basis_ref[which, cols],
+                (((1,), (1,)), ((), ())),
+                preferred_element_type=F32,
+            )
+            for which in range(2)
+        ]
+        out_ref[block] = (parts[0] + parts[1]).astype(BF16)
+        copy = pltpu.make_async_copy(out_ref.at[block], out_hbm.at[:, cols], out_sems.at[block])
+        copy.start()
+        leaving.append(copy)
+    for copy in leaving:
+        copy.wait()
 
 
 def update_matmul(rows, rows_other, order, basis, basis_other):
@@ -177,8 +241,16 @@
     return pl.pallas_call(
         update_kernel,
         out_shape=jax.ShapeDtypeStruct((640, half), BF16),
-        in_specs=[WHOLE] * 5,
-        out_specs=WHOLE,
+        in_specs=[FAR] * 5,
+        out_specs=FAR,
+        scratch_shapes=[
+            pltpu.VMEM((2, 640, 256), BF16),
+            pltpu.VMEM((640, 640), BF16),
+            pltpu.VMEM((2, half, 256), BF16),
+            pltpu.VMEM((half // 256, 640, 256), BF16),
+            pltpu.SemaphoreType.DMA((5,)),
+            pltpu.SemaphoreType.DMA((half // 256,)),
+        ],
         compiler_params=ROOM,
         cost_estimate=cost(2 * 640 * 512 * (640 + half), 5_000_000),
     )(rows, rows_other, order, basis, basis_other)

time: 146 us -> 146 us (level)
  no operation moved by 1% of the time
where the time goes in v7:
time: 146 us; the launch traced here: 145 us
  starting transfers between devices  77.3 us (53%)
  Pallas kernels  22.3 us (15%)
  waiting for transfers between devices  20.4 us (14%)
  between operations  14.3 us (10%)
  local copies, waits for them, and re-layouts  10.6 us (7%)
    ppermute x2, starting transfers between devices, sum_zh(): values = sent.astype(F32) + lax.ppermute(sent, 'zh', partners).astype(F32)  10.6 us
    all_to_all x2, starting transfers between devices, spread(): return lax.all_to_all(copies, axes, 0, 0, tiled=True)  10.6 us
    ppermute x1, starting transfers between devices, gather_zh(): got = lax.ppermute(values, 'zh', PAIR)  9.65 us
    ppermute x1, starting transfers between devices, gather_zh(): got = lax.ppermute(pair, 'zh', MIRROR)  9.28 us
    ppermute x1, starting transfers between devices, shards(): rows_other = lax.ppermute(rows, 'core', CORE_SWAP)  9 us
    all_to_all x1, starting transfers between devices, shards(): reduced = lax.all_to_all(reduced, 'zl', 0, 0, tiled=True)  7.81 us
    ppermute x2, waiting for transfers between devices, sum_zh(): values = sent.astype(F32) + lax.ppermute(sent, 'zh', partners).astype(F32)  6.39 us
    ppermute x1, starting transfers between devices, shards(): x_other = lax.ppermute(x_heads, 'core', CORE_SWAP)  5.81 us
  transfers between devices with their start and end apart: 15, of which 8 were waited for; matrix products, arithmetic and copies ran while one was open for 5% of the time, Pallas kernels for 12%

profile of v7, /device:TPU:1, one launch (start us, length us, event | category | flops | bytes accessed | tf_op | source)
XLA Modules:
  0.0 145.1 jit_solution(2589807324490198057)
XLA Ops:
  8.0 0.7 dynamic-slice_convert_fusion
  8.7 9.6 %collective-permute-start = (bf16[60,256]{1,0:T(8,128)(2,1)S(1)}, bf16[60,256]{1,0:T(8,128)(2,1)S(1)}, u32[]{:S(2)}, u32[]{:S(2)}) collective-permute-start(bf16[60,256]{1,0:T(8,128)(2,1)S(1)} %pad_maximum_fusion.2), channel_id=1, source_target_pairs={{0,32},{32,0},{64,96},{96,64},{1,33},{33,1},{65,97},{97,65},{2,34}... | collective-permute-start | bytes 92168 | tf_op jit(solution)/shard_map/ppermute | solution.py:28
  18.4 2.9 %collective-permute-start.2 = (bf16[640,1280]{1,0:T(8,128)(2,1)}, bf16[640,1280]{1,0:T(8,128)(2,1)}, u32[]{:S(2)}, u32[]{:S(2)}) collective-permute-start(bf16[640,1280]{1,0:T(8,128)(2,1)} %own_ref.3), channel_id=1, source_target_pairs={{0,4},{4,0},{1,5},{5,1},{2,6},{6,2},{3,7},{7,3},{8,12},{12,8},{9,1... | collective-permute-start | bytes 4915208 | tf_op jit(solution)/shard_map/ppermute | solution.py:268
  21.4 9.3 %collective-permute-start.1 = (bf16[120,256]{1,0:T(8,128)(2,1)S(1)}, bf16[120,256]{1,0:T(8,128)(2,1)S(1)}, u32[]{:S(2)}, u32[]{:S(2)}) collective-permute-start(bf16[120,256]{1,0:T(8,128)(2,1)S(1)} %pad_maximum_fusion.1), channel_id=1, source_target_pairs={{0,96},{96,0},{32,64},{64,32},{1,97},{97,1},{33,65},{65,33},{2,98}... | collective-permute-start | bytes 184328 | tf_op jit(solution)/shard_map/ppermute | solution.py:31
  30.6 1.9 %collective-permute-done.1 = bf16[120,256]{1,0:T(8,128)(2,1)S(1)} collective-permute-done((bf16[120,256]{1,0:T(8,128)(2,1)S(1)}, bf16[120,256]{1,0:T(8,128)(2,1)S(1)}, u32[]{:S(2)}, u32[]{:S(2)}) %collective-permute-start.1) | collective-permute-done | bytes 61472 | tf_op jit(solution)/shard_map/ppermute | solution.py:31
  32.7 1.3 broadcast_in_dim.14
  33.9 6.9 %all-to-all-start = ((bf16[16,160,256]{2,1,0:T(8,128)(2,1)}), bf16[16,160,256]{2,1,0:T(8,128)(2,1)}, u32[]{:S(2)}, u32[]{:S(2)}) async-start(bf16[16,160,256]{2,1,0:T(8,128)(2,1)} %broadcast_in_dim.14), calls=%async_computation | async-start | bytes 2621440 | tf_op jit(solution)/shard_map/all_to_all | solution.py:23
  40.9 5.8 %collective-permute-start.3 = (bf16[256,640]{1,0:T(8,128)(2,1)S(1)}, bf16[256,640]{1,0:T(8,128)(2,1)S(1)}, u32[]{:S(2)}, u32[]{:S(2)}) collective-permute-start(bf16[256,640]{1,0:T(8,128)(2,1)S(1)} %copy-done.2), channel_id=1, source_target_pairs={{0,4},{4,0},{1,5},{5,1},{2,6},{6,2},{3,7},{7,3},{8,12},{12,8},{9,1... | collective-permute-start | bytes 983048 | tf_op jit(solution)/shard_map/ppermute | solution.py:270
  46.7 1.9 %collective-permute-start.4 = (bf16[64,2560]{1,0:T(8,128)(2,1)S(1)}, bf16[64,2560]{1,0:T(8,128)(2,1)}, u32[]{:S(2)}, u32[]{:S(2)}) collective-permute-start(bf16[64,2560]{1,0:T(8,128)(2,1)S(1)} %copy-done.3), channel_id=1, source_target_pairs={{0,4},{4,0},{1,5},{5,1},{2,6},{6,2},{3,7},{7,3},{8,12},{12,8},{9,1... | collective-permute-start | bytes 983048 | tf_op jit(solution)/shard_map/ppermute | solution.py:269
  50.4 4.4 %shard_map.104 = (bf16[256,640]{1,0:T(8,128)(2,1)}, bf16[256,640]{1,0:T(8,128)(2,1)}, bf16[128,2560]{1,0:T(8,128)(2,1)}) custom-call(bf16[640,640]{1,0:T(8,128)(2,1)} %constant.63.clone.order_ref.order_hbm, bf16[640,640]{1,0:T(8,128)(2,1)} %constant.64.clone.arrival_ref, bf16[256,640]{1,0:T(8,128)(2,1)} %x_ref.3, bf16[256,640]{1,0:T(8,128)(2,1)} %copy-done.6, ...), custom_call_target="tpu_custom_call" | custom-call | flops 838860800 | bytes 4200000 | tf_op jit(solution)/shard_map/pallas_call | solution.py:116
  54.8 4.3 %shard_map.103 = bf16[256,2560]{1,0:T(8,128)(2,1)} custom-call(s32[1]{0:T(128)} %bitcast.3.core_ref, bf16[256,640]{1,0:T(8,128)(2,1)} %x_ref.3, bf16[640,1280]{1,0:T(8,128)(2,1)} %own_ref.3, bf16[640,1280]{1,0:T(8,128)(2,1)} %collective-permute-done.2.other_ref), custom_call_target="tpu_custom_call" | custom-call | flops 838860800 | bytes 5000000 | tf_op jit(solution)/shard_map/pallas_call | solution.py:67
  59.1 2.7 %shard_map.105 = bf16[4,128,256]{2,1,0:T(8,128)(2,1)} custom-call(bf16[2560,256]{1,0:T(8,128)(2,1)} %bitcast.4.basis_hbm, bf16[128,2560]{1,0:T(8,128)(2,1)} %get-tuple-element.28.grad_hbm), custom_call_target="tpu_custom_call" | custom-call | flops 167772160 | bytes 2500000 | tf_op jit(solution)/shard_map/pallas_call | solution.py:151
  61.8 7.8 %all-to-all-start.1 = ((bf16[4,128,256]{2,1,0:T(8,128)(2,1)}), bf16[4,128,256]{2,1,0:T(8,128)(2,1)S(1)}, u32[]{:S(2)}, u32[]{:S(2)}) async-start(bf16[4,128,256]{2,1,0:T(8,128)(2,1)} %shard_map.105), calls=%async_computation.1 | async-start | bytes 524288 | tf_op jit(solution)/shard_map/all_to_all | solution.py:288
  69.6 1.4 dynamic-slice_bitcast_fusion
  71.0 5.4 %collective-permute-start.5 = (bf16[8,160,256]{2,1,0:T(8,128)(2,1)S(1)}, bf16[8,160,256]{2,1,0:T(8,128)(2,1)}, u32[]{:S(2)}, u32[]{:S(2)}) collective-permute-start(bf16[8,160,256]{2,1,0:T(8,128)(2,1)S(1)} %get-tuple-element.44), channel_id=1, source_target_pairs={{0,4},{4,0},{1,5},{5,1},{2,6},{6,2},{3,7},{7,3},{8,12},{12,8},{9,1... | collective-permute-start | bytes 1966088 | tf_op jit(solution)/shard_map/ppermute | solution.py:291
  76.4 1.8 %collective-permute-done.5 = bf16[8,160,256]{2,1,0:T(8,128)(2,1)} collective-permute-done((bf16[8,160,256]{2,1,0:T(8,128)(2,1)S(1)}, bf16[8,160,256]{2,1,0:T(8,128)(2,1)}, u32[]{:S(2)}, u32[]{:S(2)}) %collective-permute-start.5) | collective-permute-done | bytes 655392 | tf_op jit(solution)/shard_map/ppermute | solution.py:291
  78.9 2.3 %shard_map.106 = bf16[640,256]{1,0:T(8,128)(2,1)} custom-call(bf16[4,128,256]{2,1,0:T(8,128)(2,1)} %copy-done.1, bf16[256,640]{1,0:T(8,128)(2,1)} %get-tuple-element.30.own_hbm, bf16[256,640]{1,0:T(8,128)(2,1)} %get-tuple-element.31.other_hbm), custom_call_target="tpu_custom_call" | custom-call | flops 167772160 | bytes 1500000 | tf_op jit(solution)/shard_map/pallas_call | solution.py:182
  81.2 4.3 %all-to-all-start.2 = ((bf16[16,40,256]{2,1,0:T(8,128)(2,1)}), bf16[16,40,256]{2,1,0:T(8,128)(2,1)S(1)}, u32[]{:S(2)}, u32[]{:S(2)}) async-start(bf16[16,40,256]{2,1,0:T(8,128)(2,1)} %bitcast.29), calls=%async_computation.2 | async-start | bytes 655360 | tf_op jit(solution)/shard_map/all_to_all | solution.py:298
  85.6 0.9 copy.11
  86.5 2.0 %copy.12 = bf16[2,4,4,40,256]{4,3,2,1,0:T(8,128)(2,1)} copy(bf16[2,4,4,40,256]{4,3,1,2,0:T(8,128)(2,1)} %bitcast.13) | data formatting | bytes 1310720 | tf_op jit(solution)/shard_map/transpose | solution.py:302
  88.5 5.0 %all-to-all-done.2 = bf16[16,40,256]{2,1,0:T(8,128)(2,1)S(1)} async-done(((bf16[16,40,256]{2,1,0:T(8,128)(2,1)}), bf16[16,40,256]{2,1,0:T(8,128)(2,1)S(1)}, u32[]{:S(2)}, u32[]{:S(2)}) %all-to-all-start.2) | async-done | bytes 327712 | tf_op jit(solution)/shard_map/all_to_all | solution.py:298
  93.5 5.0 %collective-permute-start.6 = (bf16[40,256]{1,0:T(8,128)(2,1)S(1)}, bf16[40,256]{1,0:T(8,128)(2,1)S(1)}, u32[]{:S(2)}, u32[]{:S(2)}) collective-permute-start(bf16[40,256]{1,0:T(8,128)(2,1)S(1)} %reduce_sum.12), channel_id=1, source_target_pairs={{0,32},{32,0},{64,96},{96,64},{1,33},{33,1},{65,97},{97,65},{2,34}... | collective-permute-start | bytes 61448 | tf_op jit(solution)/shard_map/ppermute | solution.py:40
  98.5 3.6 %collective-permute-done.6 = bf16[40,256]{1,0:T(8,128)(2,1)S(1)} collective-permute-done((bf16[40,256]{1,0:T(8,128)(2,1)S(1)}, bf16[40,256]{1,0:T(8,128)(2,1)S(1)}, u32[]{:S(2)}, u32[]{:S(2)}) %collective-permute-start.6) | collective-permute-done | bytes 20512 | tf_op jit(solution)/shard_map/ppermute | solution.py:40
  102.1 5.6 %collective-permute-start.7 = (bf16[40,256]{1,0:T(8,128)(2,1)S(1)}, bf16[40,256]{1,0:T(8,128)(2,1)S(1)}, u32[]{:S(2)}, u32[]{:S(2)}) collective-permute-start(bf16[40,256]{1,0:T(8,128)(2,1)S(1)} %add_convert_fusion), channel_id=1, source_target_pairs={{0,96},{96,0},{32,64},{64,32},{1,97},{97,1},{33,65},{65,33},{2,98}... | collective-permute-start | bytes 61448 | tf_op jit(solution)/shard_map/ppermute | solution.py:40
  107.7 2.8 %collective-permute-done.7 = bf16[40,256]{1,0:T(8,128)(2,1)S(1)} collective-permute-done((bf16[40,256]{1,0:T(8,128)(2,1)S(1)}, bf16[40,256]{1,0:T(8,128)(2,1)S(1)}, u32[]{:S(2)}, u32[]{:S(2)}) %collective-permute-start.7) | collective-permute-done | bytes 20512 | tf_op jit(solution)/shard_map/ppermute | solution.py:40
  110.6 0.8 broadcast_in_dim.15
  111.3 3.6 %all-to-all-start.3 = ((bf16[16,40,256]{2,1,0:T(8,128)(2,1)}), bf16[16,40,256]{2,1,0:T(8,128)(2,1)S(1)}, u32[]{:S(2)}, u32[]{:S(2)}) async-start(bf16[16,40,256]{2,1,0:T(8,128)(2,1)} %broadcast_in_dim.15), calls=%async_computation.3 | async-start | bytes 655360 | tf_op jit(solution)/shard_map/all_to_all | solution.py:23
  115.0 4.2 %shard_map.107 = bf16[256,640]{1,0:T(8,128)(2,1)} custom-call(s32[1]{0:T(128)} %bitcast.3.core_ref, bf16[256,2560]{1,0:T(8,128)(2,1)} %all-gather.2.cloned.1.call-done.grad_ref, bf16[640,1280]{1,0:T(8,128)(2,1)} %own_ref.3, bf16[640,1280]{1,0:T(8,128)(2,1)} %collective-permute-done.2.other_ref), custom_call_target="tpu_custom_call" | custom-call | flops 838860800 | bytes 5000000 | tf_op jit(solution)/shard_map/pallas_call | solution.py:93
  119.3 3.6 %all-to-all-done.3 = bf16[16,40,256]{2,1,0:T(8,128)(2,1)S(1)} async-done(((bf16[16,40,256]{2,1,0:T(8,128)(2,1)}), bf16[16,40,256]{2,1,0:T(8,128)(2,1)S(1)}, u32[]{:S(2)}, u32[]{:S(2)}) %all-to-all-start.3) | async-done | bytes 327712 | tf_op jit(solution)/shard_map/all_to_all | solution.py:23
  122.9 9.0 %collective-permute-start.8 = (bf16[640,256]{1,0:T(8,128)(2,1)S(1)}, bf16[640,256]{1,0:T(8,128)(2,1)S(1)}, u32[]{:S(2)}, u32[]{:S(2)}) collective-permute-start(bf16[640,256]{1,0:T(8,128)(2,1)S(1)} %bitcast.32), channel_id=1, source_target_pairs={{0,4},{4,0},{1,5},{5,1},{2,6},{6,2},{3,7},{7,3},{8,12},{12,8},{9,1... | collective-permute-start | bytes 983048 | tf_op jit(solution)/shard_map/ppermute | solution.py:318
  131.9 1.2 collective-permute-done.8.other_hbm
  133.8 4.4 %shard_map.108 = bf16[640,1280]{1,0:T(8,128)(2,1)} custom-call(bf16[640,256]{1,0:T(8,128)(2,1)} %bitcast.33, bf16[640,256]{1,0:T(8,128)(2,1)} %copy-done.7, bf16[640,640]{1,0:T(8,128)(2,1)} %constant.63.clone.order_ref.order_hbm, bf16[1280,256]{1,0:T(8,128)(2,1)} %bitcast.30, bf16[1280,256]{1,0:T(8,128)(2,1)} %bitcast.31), custom_call_target="tpu_custom_call" | custom-call | flops 1258291200 | bytes 5000000 | tf_op jit(solution)/shard_map/pallas_call | solution.py:241
  (44 shorter events, 4.3 us)
Async XLA Ops:
  7.2 0.8 copy-start
  7.2 107.8 %all-gather.2.cloned.1.call-start = ((), (), s32[]{:S(2)}) async-start(), calls=%async_computation.5 | async-start | bytes 1638400 | tf_op jit(solution)/shard_map/all_gather | solution.py:267
  8.7 12.6 %collective-permute-start = (bf16[60,256]{1,0:T(8,128)(2,1)S(1)}, bf16[60,256]{1,0:T(8,128)(2,1)S(1)}, u32[]{:S(2)}, u32[]{:S(2)}) collective-permute-start(bf16[60,256]{1,0:T(8,128)(2,1)S(1)} %pad_maximum_fusion.2), channel_id=1, source_target_pairs={{0,32},{32,0},{64,96},{96,64},{1,33},{33,1},{65,97},{97,65},{2,34}... | collective-permute-start | bytes 92168 | tf_op jit(solution)/shard_map/ppermute | solution.py:28
  18.4 36.4 %collective-permute-start.2 = (bf16[640,1280]{1,0:T(8,128)(2,1)}, bf16[640,1280]{1,0:T(8,128)(2,1)}, u32[]{:S(2)}, u32[]{:S(2)}) collective-permute-start(bf16[640,1280]{1,0:T(8,128)(2,1)} %own_ref.3), channel_id=1, source_target_pairs={{0,4},{4,0},{1,5},{5,1},{2,6},{6,2},{3,7},{7,3},{8,12},{12,8},{9,1... | collective-permute-start | bytes 4915208 | tf_op jit(solution)/shard_map/ppermute | solution.py:268
  21.4 11.2 %collective-permute-start.1 = (bf16[120,256]{1,0:T(8,128)(2,1)S(1)}, bf16[120,256]{1,0:T(8,128)(2,1)S(1)}, u32[]{:S(2)}, u32[]{:S(2)}) collective-permute-start(bf16[120,256]{1,0:T(8,128)(2,1)S(1)} %pad_maximum_fusion.1), channel_id=1, source_target_pairs={{0,96},{96,0},{32,64},{64,32},{1,97},{97,1},{33,65},{65,33},{2,98}... | collective-permute-start | bytes 184328 | tf_op jit(solution)/shard_map/ppermute | solution.py:31
  33.9 7.0 %copy-start.2 = (bf16[256,640]{1,0:T(8,128)(2,1)S(1)}, bf16[256,640]{1,0:T(8,128)(2,1)}, u32[]{:S(2)}) copy-start(bf16[256,640]{1,0:T(8,128)(2,1)} %x_ref.3) | copy-start | bytes 983044
  33.9 12.8 %copy-start.3 = (bf16[64,2560]{1,0:T(8,128)(2,1)S(1)}, bf16[64,2560]{1,0:T(8,128)(2,1)}, u32[]{:S(2)}) copy-start(bf16[64,2560]{1,0:T(8,128)(2,1)} %g_ref.1) | copy-start | bytes 983044
  33.9 25.1 %all-to-all-start = ((bf16[16,160,256]{2,1,0:T(8,128)(2,1)}), bf16[16,160,256]{2,1,0:T(8,128)(2,1)}, u32[]{:S(2)}, u32[]{:S(2)}) async-start(bf16[16,160,256]{2,1,0:T(8,128)(2,1)} %broadcast_in_dim.14), calls=%async_computation | async-start | bytes 2621440 | tf_op jit(solution)/shard_map/all_to_all | solution.py:23
  40.8 82.0 %reduce-scatter.2.cloned.1.call-start = ((), (), s32[]{:S(2)}) async-start(), calls=%async_computation.6 | async-start | bytes 1638400 | tf_op jit(solution)/shard_map/reduce_scatter | solution.py:285
  40.9 8.4 %collective-permute-start.3 = (bf16[256,640]{1,0:T(8,128)(2,1)S(1)}, bf16[256,640]{1,0:T(8,128)(2,1)S(1)}, u32[]{:S(2)}, u32[]{:S(2)}) collective-permute-start(bf16[256,640]{1,0:T(8,128)(2,1)S(1)} %copy-done.2), channel_id=1, source_target_pairs={{0,4},{4,0},{1,5},{5,1},{2,6},{6,2},{3,7},{7,3},{8,12},{12,8},{9,1... | collective-permute-start | bytes 983048 | tf_op jit(solution)/shard_map/ppermute | solution.py:270
  46.7 3.7 %collective-permute-start.4 = (bf16[64,2560]{1,0:T(8,128)(2,1)S(1)}, bf16[64,2560]{1,0:T(8,128)(2,1)}, u32[]{:S(2)}, u32[]{:S(2)}) collective-permute-start(bf16[64,2560]{1,0:T(8,128)(2,1)S(1)} %copy-done.3), channel_id=1, source_target_pairs={{0,4},{4,0},{1,5},{5,1},{2,6},{6,2},{3,7},{7,3},{8,12},{12,8},{9,1... | collective-permute-start | bytes 983048 | tf_op jit(solution)/shard_map/ppermute | solution.py:269
  49.3 0.7 copy-start.6
  61.8 16.4 %all-to-all-start.1 = ((bf16[4,128,256]{2,1,0:T(8,128)(2,1)}), bf16[4,128,256]{2,1,0:T(8,128)(2,1)S(1)}, u32[]{:S(2)}, u32[]{:S(2)}) async-start(bf16[4,128,256]{2,1,0:T(8,128)(2,1)} %shard_map.105), calls=%async_computation.1 | async-start | bytes 524288 | tf_op jit(solution)/shard_map/all_to_all | solution.py:288
  71.0 7.2 %collective-permute-start.5 = (bf16[8,160,256]{2,1,0:T(8,128)(2,1)S(1)}, bf16[8,160,256]{2,1,0:T(8,128)(2,1)}, u32[]{:S(2)}, u32[]{:S(2)}) collective-permute-start(bf16[8,160,256]{2,1,0:T(8,128)(2,1)S(1)} %get-tuple-element.44), channel_id=1, source_target_pairs={{0,4},{4,0},{1,5},{5,1},{2,6},{6,2},{3,7},{7,3},{8,12},{12,8},{9,1... | collective-permute-start | bytes 1966088 | tf_op jit(solution)/shard_map/ppermute | solution.py:291
  78.2 0.7 copy-start.1
  81.2 12.2 %all-to-all-start.2 = ((bf16[16,40,256]{2,1,0:T(8,128)(2,1)}), bf16[16,40,256]{2,1,0:T(8,128)(2,1)S(1)}, u32[]{:S(2)}, u32[]{:S(2)}) async-start(bf16[16,40,256]{2,1,0:T(8,128)(2,1)} %bitcast.29), calls=%async_computation.2 | async-start | bytes 655360 | tf_op jit(solution)/shard_map/all_to_all | solution.py:298
  85.6 25.0 %copy-start.5 = (bf16[40,256]{1,0:T(8,128)(2,1)S(1)}, bf16[40,256]{1,0:T(8,128)(2,1)}, u32[]{:S(2)}) copy-start(bf16[40,256]{1,0:T(8,128)(2,1)} %reshape.50) | copy-start | bytes 61444
  93.5 8.6 %collective-permute-start.6 = (bf16[40,256]{1,0:T(8,128)(2,1)S(1)}, bf16[40,256]{1,0:T(8,128)(2,1)S(1)}, u32[]{:S(2)}, u32[]{:S(2)}) collective-permute-start(bf16[40,256]{1,0:T(8,128)(2,1)S(1)} %reduce_sum.12), channel_id=1, source_target_pairs={{0,32},{32,0},{64,96},{96,64},{1,33},{33,1},{65,97},{97,65},{2,34}... | collective-permute-start | bytes 61448 | tf_op jit(solution)/shard_map/ppermute | solution.py:40
  102.1 8.4 %collective-permute-start.7 = (bf16[40,256]{1,0:T(8,128)(2,1)S(1)}, bf16[40,256]{1,0:T(8,128)(2,1)S(1)}, u32[]{:S(2)}, u32[]{:S(2)}) collective-permute-start(bf16[40,256]{1,0:T(8,128)(2,1)S(1)} %add_convert_fusion), channel_id=1, source_target_pairs={{0,96},{96,0},{32,64},{64,32},{1,97},{97,1},{33,65},{65,33},{2,98}... | collective-permute-start | bytes 61448 | tf_op jit(solution)/shard_map/ppermute | solution.py:40
  111.3 11.5 %all-to-all-start.3 = ((bf16[16,40,256]{2,1,0:T(8,128)(2,1)}), bf16[16,40,256]{2,1,0:T(8,128)(2,1)S(1)}, u32[]{:S(2)}, u32[]{:S(2)}) async-start(bf16[16,40,256]{2,1,0:T(8,128)(2,1)} %broadcast_in_dim.15), calls=%async_computation.3 | async-start | bytes 655360 | tf_op jit(solution)/shard_map/all_to_all | solution.py:23
  122.9 10.2 %copy-start.4 = (bf16[16,40,256]{2,1,0:T(8,128)(2,1)}, bf16[16,40,256]{2,1,0:T(8,128)(2,1)S(1)}, u32[]{:S(2)}) copy-start(bf16[16,40,256]{2,1,0:T(8,128)(2,1)S(1)} %all-to-all-done.3) | copy-start | bytes 983044
  122.9 10.2 %collective-permute-start.8 = (bf16[640,256]{1,0:T(8,128)(2,1)S(1)}, bf16[640,256]{1,0:T(8,128)(2,1)S(1)}, u32[]{:S(2)}, u32[]{:S(2)}) collective-permute-start(bf16[640,256]{1,0:T(8,128)(2,1)S(1)} %bitcast.32), channel_id=1, source_target_pairs={{0,4},{4,0},{1,5},{5,1},{2,6},{6,2},{3,7},{7,3},{8,12},{12,8},{9,1... | collective-permute-start | bytes 983048 | tf_op jit(solution)/shard_map/ppermute | solution.py:318
  133.1 0.7 copy-start.7
Sparse Core Ops, SparseCore 0:
  18.5 42.4 all-gather.1
  64.4 41.3 reduce-scatter.1

commit v8 on v2

--- a/solution.py
+++ b/solution.py
@@ -1,5 +1,6 @@
 import jax
 import jax.numpy as jnp
+import numpy as np
 from jax import lax
 from jax.experimental import pallas as pl
 from jax.experimental.pallas import tpu as pltpu
@@ -13,7 +14,7 @@
 CORE_SWAP = [(0, 1), (1, 0)]
 PAIR = [(0, 1), (1, 0), (2, 3), (3, 2)]
 MIRROR = [(0, 3), (3, 0), (1, 2), (2, 1)]
-TURN = [(a * 4 + b, b * 4 + a) for a in range(4) for b in range(4)]
+ORDER = np.eye(640, dtype=np.float32).reshape(640, 4, 4, 4, 10).transpose(0, 1, 3, 2, 4).reshape(640, 640)
 
 
 def spread(values, axes, count):
@@ -97,6 +98,25 @@
     )(core, grads, own, other)
 
 
+def ordered_kernel(order_ref, x_ref, xo_ref, px_ref, pxo_ref):
+    for source, target in ((x_ref, px_ref), (xo_ref, pxo_ref)):
+        moved = jnp.dot(source[...], order_ref[...], preferred_element_type=F32)
+        target[...] = moved.astype(BF16)
+
+
+def ordered(order, rows, rows_other):
+    x_shape = jax.ShapeDtypeStruct((256, 640), BF16)
+    whole = pl.BlockSpec()
+    return pl.pallas_call(
+        ordered_kernel,
+        out_shape=(x_shape, x_shape),
+        in_specs=[whole] * 3,
+        out_specs=(whole,) * 2,
+        compiler_params=pltpu.CompilerParams(vmem_limit_bytes=63 * 2**20),
+        cost_estimate=cost(2 * 640 * 640 * 512, 2_200_000),
+    )(order, rows, rows_other)
+
+
 def low_kernel(basis_ref, x_ref, grad_ref, *refs):
     out_ref = refs[-1]
     reduced = jnp.dot(grad_ref[...], basis_ref[...], preferred_element_type=F32).astype(BF16)
@@ -119,46 +139,70 @@
     )(basis, rows, grads, *before)
 
 
+def update_kernel(own_ref, other_ref, order_ref, basis_ref, basis_other_ref, out_ref):
+    total = None
+    for rows, basis in ((own_ref, basis_ref), (other_ref, basis_other_ref)):
+        direction = jnp.dot(order_ref[...], rows[...], preferred_element_type=F32).astype(BF16)
+        part = lax.dot_general(
+            direction, basis[...], (((1,), (1,)), ((), ())), preferred_element_type=F32
+        )
+        total = part if total is None else total + part
+    out_ref[...] = total.astype(BF16)
+
+
+def update_matmul(rows, rows_other, order, basis, basis_other):
+    half = basis.shape[0]
+    return pl.pallas_call(
+        update_kernel,
+        out_shape=jax.ShapeDtypeStruct((640, half), BF16),
+        in_specs=[VMEM] * 5,
+        out_specs=VMEM,
+        compiler_params=ROOM,
+        cost_estimate=cost(2 * 640 * 512 * (640 + half), 5_000_000),
+    )(rows, rows_other, order, basis, basis_other)
+
+
 def shards(x_heads, proj_weight, out_grad, proj_basis, first_moment, second_moment):
     core = lax.axis_index("core")
     half = proj_weight.shape[1]
-
     scalar = core.reshape(1).astype(jnp.int32)
-
-    grad_block = lax.all_gather(out_grad, "zl", axis=0, tiled=True)
 
     def own_columns(values):
         return lax.dynamic_slice_in_dim(values, core * 256, 256, 1)
 
-    moments = jnp.concatenate([own_columns(first_moment[0]), own_columns(second_moment[0])], 0)
-    moments = lax.ppermute(moments.astype(BF16), ("zh", "x"), TURN)
-
+    grad_block = lax.all_gather(out_grad, "zl", axis=0, tiled=True)
     weight_other = lax.ppermute(proj_weight, "core", CORE_SWAP)
     x_other = lax.ppermute(x_heads, "core", CORE_SWAP)
-    by_zh = gather_zh(jnp.concatenate([own_columns(proj_basis), moments], 0))
-    by_zh, weight_other = lax.optimization_barrier((by_zh, weight_other))
+
+    parts = [proj_basis, first_moment[0].astype(BF16), second_moment[0].astype(BF16)]
+    by_zh = gather_zh(jnp.concatenate([own_columns(part) for part in parts], 0))
     m_old = by_zh[:, 40:50].reshape(40, 256)
     v_old = by_zh[:, 50:].reshape(40, 256)
     by_yx = spread(by_zh[:, :40].reshape(160, 256), ("y", "x"), 16)
+
     mixed_part = mixed_matmul(scalar, x_heads, proj_weight, weight_other)
-    by_yx, mixed_part, grad_block, x_other = lax.optimization_barrier(
-        (by_yx, mixed_part, grad_block, x_other)
-    )
+    order = jnp.asarray(ORDER, BF16)
+    x_own, x_other = ordered(order, x_heads, x_other)
+    by_yx, mixed_part, x_own, x_other, m_old, v_old = lax.optimization_barrier(
+        (by_yx, mixed_part, x_own, x_other, m_old, v_old)
+    )
+    basis_cols = by_yx.reshape(4, 4, 4, 40, 256).transpose(0, 2, 1, 3, 4).reshape(2560, 256)
+
+    mixed_out = lax.psum_scatter(mixed_part, "zl", scatter_dimension=0, tiled=True)
+
+    basis_own = lax.dynamic_slice_in_dim(basis_cols, core * half, half, 0)
+    basis_sent = lax.dynamic_slice_in_dim(basis_cols, (1 - core) * half, half, 0)
+    basis_cols, basis_own, basis_sent, grad_block = lax.optimization_barrier(
+        (basis_cols, basis_own, basis_sent, grad_block)
+    )
+    basis_other = lax.ppermute(basis_sent, "core", CORE_SWAP)
+
     grad_other = lax.ppermute(grad_block, "core", CORE_SWAP)
-    basis_cols = by_yx.reshape(4, 4, 4, 40, 256).transpose(0, 2, 1, 3, 4).reshape(2560, 256)
-
-    mixed_out = lax.psum_scatter(mixed_part, "zl", scatter_dimension=0, tiled=True)
-
-    low_own = low_matmul(basis_cols, x_heads, grad_block)
+    low_own = low_matmul(basis_cols, x_own, grad_block)
+    low_own, basis_other = lax.optimization_barrier((low_own, basis_other))
     low_chip = low_matmul(basis_cols, x_other, grad_other, low_own)
 
     low_yx = lax.all_to_all(low_chip.reshape(16, 40, 256), ("y", "x"), 0, 0, tiled=True)
-    basis_cols, low_chip = lax.optimization_barrier((basis_cols, low_chip))
-    basis_own = lax.dynamic_slice_in_dim(basis_cols, core * half, half, 0)
-    basis_other = lax.ppermute(
-        lax.dynamic_slice_in_dim(basis_cols, (1 - core) * half, half, 0), "core", CORE_SWAP
-    )
-    low_yx, basis_other = lax.optimization_barrier((low_yx, basis_other))
     low = sum_zh(jnp.sum(low_yx.astype(F32), 0))
 
     m_new = 0.9 * m_old.astype(F32) + 0.1 * low
@@ -172,10 +216,7 @@
     rows, head_rows, mixed_out = lax.optimization_barrier((rows, head_rows, mixed_out))
     rows_other = lax.ppermute(rows, "core", CORE_SWAP)
 
-    def half_update(columns, basis):
-        return lax.dot_general(columns, basis, (((1,), (1,)), ((), ())), preferred_element_type=F32)
-
-    update = (half_update(rows, basis_own) + half_update(rows_other, basis_other)).astype(BF16)
+    update = update_matmul(rows, rows_other, order, basis_own, basis_other)
     return (mixed_out, head_rows, update)
 
 

time: 152 us -> 138 us (0.908)
  starting transfers between devices: 81.8 us -> 69 us
  Pallas kernels: 7.3 us -> 14.7 us
  waiting for transfers between devices: 19.4 us -> 14.6 us
  matrix products: 3.52 us -> 0 us
    all_gather x1, waiting for transfers between devices: 9.18 us -> 1.36 us  [shards(): grad_block = lax.all_gather(out_grad, 'zl', axis=0, tiled=True)]
    ppermute x1, starting transfers between devices: 8.79 us -> 2.87 us  [shards(): weight_other = lax.ppermute(proj_weight, 'core', CORE_SWAP)]
    ppermute x1, starting transfers between devices: 15.1 us -> 9.28 us  [gather_zh(): got = lax.ppermute(pair, 'zh', MIRROR)]
    pallas_call x0 -> x2, Pallas kernels: none -> 5.78 us  [the longest x1 3 us: update_matmul(): pl.pallas_call(update_kernel, out_shape=jax.ShapeDtypeStruct((640, half),...]
    dot_general x2 -> x0, matrix products: 3.52 us -> none  [half_update(): lax.dot_general(columns, basis, (((1,), (1,)), ((), ())), preferred_eleme...]
    all_to_all x2, waiting for transfers between devices: 3.18 us -> 5.65 us  [spread(): return lax.all_to_all(copies, axes, 0, 0, tiled=True)]
    ppermute x1, starting transfers between devices: 12 us -> 9.65 us  [gather_zh(): got = lax.ppermute(values, 'zh', PAIR)]
    ppermute x2, starting transfers between devices: 14.4 us -> 16.5 us  [sum_zh(): values = sent.astype(F32) + lax.ppermute(sent, 'zh', partners).astype(F32)]
  transfers between devices with their start and end apart: 14 -> 13, of which waited for: 7 -> 8; matrix products, arithmetic and copies ran while one was open for 3% -> 3% of each run, Pallas kernels for 5% -> 9%
where the time goes in v8:
time: 138 us; the launch traced here: 137 us
  starting transfers between devices  69 us (50%)
  Pallas kernels  14.7 us (11%)
  waiting for transfers between devices  14.6 us (11%)
  between operations  14.4 us (10%)
  local copies, waits for them, and re-layouts  12.1 us (9%)
  blocking collectives  12 us (9%)
    ppermute x2, starting transfers between devices, sum_zh(): values = sent.astype(F32) + lax.ppermute(sent, 'zh', partners).astype(F32)  16.5 us
    all_to_all x1, blocking collectives, shards(): lax.all_to_all(low_chip.reshape(16, 40, 256), ('y', 'x'), 0, 0, tiled=True)  12 us
    all_to_all x2, starting transfers between devices, spread(): return lax.all_to_all(copies, axes, 0, 0, tiled=True)  10.5 us
    ppermute x1, starting transfers between devices, gather_zh(): got = lax.ppermute(values, 'zh', PAIR)  9.65 us
    ppermute x1, starting transfers between devices, gather_zh(): got = lax.ppermute(pair, 'zh', MIRROR)  9.28 us
    unnamed x28, local copies, waits for them, and re-layouts  6.85 us
    ppermute x1, starting transfers between devices, shards(): rows_other = lax.ppermute(rows, 'core', CORE_SWAP)  6.4 us
    ppermute x1, starting transfers between devices, shards(): x_other = lax.ppermute(x_heads, 'core', CORE_SWAP)  5.94 us
  transfers between devices with their start and end apart: 13, of which 8 were waited for; matrix products, arithmetic and copies ran while one was open for 3% of the time, Pallas kernels for 9%

profile of v8, /device:TPU:1, one launch (start us, length us, event | category | flops | bytes accessed | tf_op | source)
XLA Modules:
  0.0 136.9 jit_solution(1595685056990157313)
XLA Ops:
  8.7 9.6 %collective-permute-start = (bf16[60,256]{1,0:T(8,128)(2,1)S(1)}, bf16[60,256]{1,0:T(8,128)(2,1)S(1)}, u32[]{:S(2)}, u32[]{:S(2)}) collective-permute-start(bf16[60,256]{1,0:T(8,128)(2,1)S(1)} %pad_maximum_fusion.2), channel_id=1, source_target_pairs={{0,32},{32,0},{64,96},{96,64},{1,33},{33,1},{65,97},{97,65},{2,34}... | collective-permute-start | bytes 92168 | tf_op jit(solution)/shard_map/ppermute | solution.py:27
  18.4 2.9 %collective-permute-start.2 = (bf16[640,1280]{1,0:T(8,128)(2,1)}, bf16[640,1280]{1,0:T(8,128)(2,1)}, u32[]{:S(2)}, u32[]{:S(2)}) collective-permute-start(bf16[640,1280]{1,0:T(8,128)(2,1)} %own_ref.3), channel_id=1, source_target_pairs={{0,4},{4,0},{1,5},{5,1},{2,6},{6,2},{3,7},{7,3},{8,12},{12,8},{9,1... | collective-permute-start | bytes 4915208 | tf_op jit(solution)/shard_map/ppermute | solution.py:174
  21.4 9.3 %collective-permute-start.1 = (bf16[120,256]{1,0:T(8,128)(2,1)S(1)}, bf16[120,256]{1,0:T(8,128)(2,1)S(1)}, u32[]{:S(2)}, u32[]{:S(2)}) collective-permute-start(bf16[120,256]{1,0:T(8,128)(2,1)S(1)} %pad_maximum_fusion.1), channel_id=1, source_target_pairs={{0,96},{96,0},{32,64},{64,32},{1,97},{97,1},{33,65},{65,33},{2,98}... | collective-permute-start | bytes 184328 | tf_op jit(solution)/shard_map/ppermute | solution.py:30
  30.6 1.9 %collective-permute-done.1 = bf16[120,256]{1,0:T(8,128)(2,1)S(1)} collective-permute-done((bf16[120,256]{1,0:T(8,128)(2,1)S(1)}, bf16[120,256]{1,0:T(8,128)(2,1)S(1)}, u32[]{:S(2)}, u32[]{:S(2)}) %collective-permute-start.1) | collective-permute-done | bytes 61472 | tf_op jit(solution)/shard_map/ppermute | solution.py:30
  32.6 1.2 broadcast_in_dim.14
  33.9 6.9 %all-to-all-start = ((bf16[16,160,256]{2,1,0:T(8,128)(2,1)}), bf16[16,160,256]{2,1,0:T(8,128)(2,1)}, u32[]{:S(2)}, u32[]{:S(2)}) async-start(bf16[16,160,256]{2,1,0:T(8,128)(2,1)} %broadcast_in_dim.14), calls=%async_computation | async-start | bytes 2621440 | tf_op jit(solution)/shard_map/all_to_all | solution.py:22
  40.9 5.9 %collective-permute-start.3 = (bf16[256,640]{1,0:T(8,128)(2,1)S(1)}, bf16[256,640]{1,0:T(8,128)(2,1)}, u32[]{:S(2)}, u32[]{:S(2)}) collective-permute-start(bf16[256,640]{1,0:T(8,128)(2,1)S(1)} %copy-done.6), channel_id=1, source_target_pairs={{0,4},{4,0},{1,5},{5,1},{2,6},{6,2},{3,7},{7,3},{8,12},{12,8},{9,1... | collective-permute-start | bytes 983048 | tf_op jit(solution)/shard_map/ppermute | solution.py:175
  46.9 1.3 collective-permute-done.3.xo_ref
  48.2 2.8 %shard_map.95 = (bf16[256,640]{1,0:T(8,128)(2,1)}, bf16[256,640]{1,0:T(8,128)(2,1)}) custom-call(bf16[640,640]{1,0:T(8,128)(2,1)} %constant.57.clone.order_ref, bf16[256,640]{1,0:T(8,128)(2,1)} %x_ref.3, bf16[256,640]{1,0:T(8,128)(2,1)} %collective-permute-done.3.xo_ref), custom_call_target="tpu_custom_call" | custom-call | flops 419430400 | bytes 2200000 | tf_op jit(solution)/shard_map/pallas_call | solution.py:110
  51.0 1.4 %copy-done.1 = bf16[640,1280]{1,0:T(8,128)(2,1)S(1)} copy-done((bf16[640,1280]{1,0:T(8,128)(2,1)S(1)}, bf16[640,1280]{1,0:T(8,128)(2,1)}, u32[]{:S(2)}) %copy-start.1) | copy-done | bytes 1638424
  52.4 3.7 %shard_map.94 = bf16[256,2560]{1,0:T(8,128)(2,1)} custom-call(s32[1]{0:T(128)} %bitcast.3.core_ref, bf16[256,640]{1,0:T(8,128)(2,1)S(1)} %copy-done.7, bf16[640,1280]{1,0:T(8,128)(2,1)S(1)} %copy-done.1, bf16[640,1280]{1,0:T(8,128)(2,1)} %collective-permute-done.2.other_ref), custom_call_target="tpu_custom_call" | custom-call | flops 838860800 | bytes 5000000 | tf_op jit(solution)/shard_map/pallas_call | solution.py:65
  56.2 1.1 all-to-all-done
  57.2 1.4 %copy.10 = bf16[4,4,4,40,256]{4,3,2,1,0:T(8,128)(2,1)S(1)} copy(bf16[4,4,4,40,256]{4,3,1,2,0:T(8,128)(2,1)} %bitcast.5) | data formatting | bytes 2621440 | tf_op jit(solution)/shard_map/transpose | solution.py:189
  58.7 0.9 constant_dynamic-slice_fusion
  59.7 1.4 all-gather.2.cloned.1.call-done.grad_ref
  61.0 5.9 %collective-permute-start.4 = (bf16[256,2560]{1,0:T(8,128)(2,1)}, bf16[256,2560]{1,0:T(8,128)(2,1)S(1)}, u32[]{:S(2)}, u32[]{:S(2)}) collective-permute-start(bf16[256,2560]{1,0:T(8,128)(2,1)} %all-gather.2.cloned.1.call-done.grad_ref), channel_id=1, source_target_pairs={{0,4},{4,0},{1,5},{5,1},{2,6},{6,2},{3,7},{7,3},{8,12},{12,8},{9,1... | collective-permute-start | bytes 3932168 | tf_op jit(solution)/shard_map/ppermute | solution.py:200
  67.0 1.9 %collective-permute-start.5 = (bf16[1280,256]{1,0:T(8,128)(2,1)S(1)}, bf16[1280,256]{1,0:T(8,128)(2,1)S(1)}, u32[]{:S(2)}, u32[]{:S(2)}) collective-permute-start(bf16[1280,256]{1,0:T(8,128)(2,1)S(1)} %get-tuple-element.28), channel_id=1, source_target_pairs={{0,4},{4,0},{1,5},{5,1},{2,6},{6,2},{3,7},{7,3},{8,12},{12,8},{9,1... | collective-permute-start | bytes 1966088 | tf_op jit(solution)/shard_map/ppermute | solution.py:198
  68.9 1.3 copy-done.3
  72.1 12.0 %all_to_all.15 = bf16[16,40,256]{2,1,0:T(8,128)(2,1)S(1)} all-to-all(bf16[16,40,256]{2,1,0:T(8,128)(2,1)S(1)} %bitcast.21), channel_id=1, replica_groups=mesh['y'=4,'zh'=4,'x'=4,'core'=2,'zl'=4] {'y','x'}, dimensions={0} | all-to-all | bytes 655360 | tf_op jit(solution)/shard_map/all_to_all | solution.py:205
  84.2 7.4 %collective-permute-start.6 = (bf16[40,256]{1,0:T(8,128)(2,1)S(1)}, bf16[40,256]{1,0:T(8,128)(2,1)S(1)}, u32[]{:S(2)}, u32[]{:S(2)}) collective-permute-start(bf16[40,256]{1,0:T(8,128)(2,1)S(1)} %reduce_sum.12), channel_id=1, source_target_pairs={{0,32},{32,0},{64,96},{96,64},{1,33},{33,1},{65,97},{97,65},{2,34}... | collective-permute-start | bytes 61448 | tf_op jit(solution)/shard_map/ppermute | solution.py:39
  91.5 1.3 collective-permute-done.6
  92.9 9.2 %collective-permute-start.7 = (bf16[40,256]{1,0:T(8,128)(2,1)S(1)}, bf16[40,256]{1,0:T(8,128)(2,1)S(1)}, u32[]{:S(2)}, u32[]{:S(2)}) collective-permute-start(bf16[40,256]{1,0:T(8,128)(2,1)S(1)} %add_convert_fusion), channel_id=1, source_target_pairs={{0,96},{96,0},{32,64},{64,32},{1,97},{97,1},{33,65},{65,33},{2,98}... | collective-permute-start | bytes 61448 | tf_op jit(solution)/shard_map/ppermute | solution.py:39
  102.0 1.8 %collective-permute-done.7 = bf16[40,256]{1,0:T(8,128)(2,1)S(1)} collective-permute-done((bf16[40,256]{1,0:T(8,128)(2,1)S(1)}, bf16[40,256]{1,0:T(8,128)(2,1)S(1)}, u32[]{:S(2)}, u32[]{:S(2)}) %collective-permute-start.7) | collective-permute-done | bytes 20512 | tf_op jit(solution)/shard_map/ppermute | solution.py:39
  104.6 3.5 %all-to-all-start.2 = ((bf16[16,40,256]{2,1,0:T(8,128)(2,1)}), bf16[16,40,256]{2,1,0:T(8,128)(2,1)S(1)}, u32[]{:S(2)}, u32[]{:S(2)}) async-start(bf16[16,40,256]{2,1,0:T(8,128)(2,1)} %broadcast_in_dim.15), calls=%async_computation.2 | async-start | bytes 655360 | tf_op jit(solution)/shard_map/all_to_all | solution.py:22
  108.2 3.4 %shard_map.98 = bf16[256,640]{1,0:T(8,128)(2,1)} custom-call(s32[1]{0:T(128)} %bitcast.3.core_ref, bf16[256,2560]{1,0:T(8,128)(2,1)S(1)} %copy-done.4, bf16[640,1280]{1,0:T(8,128)(2,1)S(1)} %copy-done.2, bf16[640,1280]{1,0:T(8,128)(2,1)} %collective-permute-done.2.other_ref), custom_call_target="tpu_custom_call" | custom-call | flops 838860800 | bytes 5000000 | tf_op jit(solution)/shard_map/pallas_call | solution.py:91
  111.5 4.6 %all-to-all-done.2 = bf16[16,40,256]{2,1,0:T(8,128)(2,1)S(1)} async-done(((bf16[16,40,256]{2,1,0:T(8,128)(2,1)}), bf16[16,40,256]{2,1,0:T(8,128)(2,1)S(1)}, u32[]{:S(2)}, u32[]{:S(2)}) %all-to-all-start.2) | async-done | bytes 327712 | tf_op jit(solution)/shard_map/all_to_all | solution.py:22
  116.1 6.4 %collective-permute-start.8 = (bf16[640,256]{1,0:T(8,128)(2,1)S(1)}, bf16[640,256]{1,0:T(8,128)(2,1)S(1)}, u32[]{:S(2)}, u32[]{:S(2)}) collective-permute-start(bf16[640,256]{1,0:T(8,128)(2,1)S(1)} %bitcast.22), channel_id=1, source_target_pairs={{0,4},{4,0},{1,5},{5,1},{2,6},{6,2},{3,7},{7,3},{8,12},{12,8},{9,1... | collective-permute-start | bytes 983048 | tf_op jit(solution)/shard_map/ppermute | solution.py:217
  122.5 1.2 collective-permute-done.8.other_ref
  123.8 1.1 copy-done.5
  124.9 1.1 copy-done.11
  125.9 1.1 copy-done.12
  127.1 3.0 %shard_map.99 = bf16[640,1280]{1,0:T(8,128)(2,1)} custom-call(bf16[640,256]{1,0:T(8,128)(2,1)S(1)} %bitcast.23, bf16[640,256]{1,0:T(8,128)(2,1)S(1)} %collective-permute-done.8.other_ref, bf16[640,640]{1,0:T(8,128)(2,1)S(1)} %copy-done.12, bf16[1280,256]{1,0:T(8,128)(2,1)S(1)} %copy-done.5, bf16[1280,256]{1,0:T(8,128)(2,1)S(1)} %copy-done.11), custom_call_target="tpu_custom_call" | custom-call | flops 1258291200 | bytes 5000000 | tf_op jit(solution)/shard_map/pallas_call | solution.py:155
  (50 shorter events, 4.5 us)
Async XLA Ops:
  7.2 0.8 copy-start
  7.2 53.9 %all-gather.2.cloned.1.call-start = ((), (), s32[]{:S(2)}) async-start(), calls=%async_computation.4 | async-start | bytes 1638400 | tf_op jit(solution)/shard_map/all_gather | solution.py:173
  8.7 12.6 %collective-permute-start = (bf16[60,256]{1,0:T(8,128)(2,1)S(1)}, bf16[60,256]{1,0:T(8,128)(2,1)S(1)}, u32[]{:S(2)}, u32[]{:S(2)}) collective-permute-start(bf16[60,256]{1,0:T(8,128)(2,1)S(1)} %pad_maximum_fusion.2), channel_id=1, source_target_pairs={{0,32},{32,0},{64,96},{96,64},{1,33},{33,1},{65,97},{97,65},{2,34}... | collective-permute-start | bytes 92168 | tf_op jit(solution)/shard_map/ppermute | solution.py:27
  18.4 32.6 %collective-permute-start.2 = (bf16[640,1280]{1,0:T(8,128)(2,1)}, bf16[640,1280]{1,0:T(8,128)(2,1)}, u32[]{:S(2)}, u32[]{:S(2)}) collective-permute-start(bf16[640,1280]{1,0:T(8,128)(2,1)} %own_ref.3), channel_id=1, source_target_pairs={{0,4},{4,0},{1,5},{5,1},{2,6},{6,2},{3,7},{7,3},{8,12},{12,8},{9,1... | collective-permute-start | bytes 4915208 | tf_op jit(solution)/shard_map/ppermute | solution.py:174
  21.4 11.2 %collective-permute-start.1 = (bf16[120,256]{1,0:T(8,128)(2,1)S(1)}, bf16[120,256]{1,0:T(8,128)(2,1)S(1)}, u32[]{:S(2)}, u32[]{:S(2)}) collective-permute-start(bf16[120,256]{1,0:T(8,128)(2,1)S(1)} %pad_maximum_fusion.1), channel_id=1, source_target_pairs={{0,96},{96,0},{32,64},{64,32},{1,97},{97,1},{33,65},{65,33},{2,98}... | collective-permute-start | bytes 184328 | tf_op jit(solution)/shard_map/ppermute | solution.py:30
  33.9 7.0 %copy-start.6 = (bf16[256,640]{1,0:T(8,128)(2,1)S(1)}, bf16[256,640]{1,0:T(8,128)(2,1)}, u32[]{:S(2)}) copy-start(bf16[256,640]{1,0:T(8,128)(2,1)} %x_ref.3) | copy-start | bytes 983044
  33.9 23.3 %all-to-all-start = ((bf16[16,160,256]{2,1,0:T(8,128)(2,1)}), bf16[16,160,256]{2,1,0:T(8,128)(2,1)}, u32[]{:S(2)}, u32[]{:S(2)}) async-start(bf16[16,160,256]{2,1,0:T(8,128)(2,1)} %broadcast_in_dim.14), calls=%async_computation | async-start | bytes 2621440 | tf_op jit(solution)/shard_map/all_to_all | solution.py:22
  40.8 10.2 %copy-start.7 = (bf16[256,640]{1,0:T(8,128)(2,1)S(1)}, bf16[256,640]{1,0:T(8,128)(2,1)}, u32[]{:S(2)}) copy-start(bf16[256,640]{1,0:T(8,128)(2,1)} %x_ref.3) | copy-start | bytes 983044
  40.9 75.3 %reduce-scatter.2.cloned.1.call-start = ((), (), s32[]{:S(2)}) async-start(), calls=%async_computation.5 | async-start | bytes 1638400 | tf_op jit(solution)/shard_map/reduce_scatter | solution.py:191
  40.9 7.3 %collective-permute-start.3 = (bf16[256,640]{1,0:T(8,128)(2,1)S(1)}, bf16[256,640]{1,0:T(8,128)(2,1)}, u32[]{:S(2)}, u32[]{:S(2)}) collective-permute-start(bf16[256,640]{1,0:T(8,128)(2,1)S(1)} %copy-done.6), channel_id=1, source_target_pairs={{0,4},{4,0},{1,5},{5,1},{2,6},{6,2},{3,7},{7,3},{8,12},{12,8},{9,1... | collective-permute-start | bytes 983048 | tf_op jit(solution)/shard_map/ppermute | solution.py:175
  51.0 1.4 %copy-start.1 = (bf16[640,1280]{1,0:T(8,128)(2,1)S(1)}, bf16[640,1280]{1,0:T(8,128)(2,1)}, u32[]{:S(2)}) copy-start(bf16[640,1280]{1,0:T(8,128)(2,1)} %own_ref.3) | copy-start | bytes 4915204
  58.7 10.2 %copy-start.8 = (bf16[256,640]{1,0:T(8,128)(2,1)S(1)}, bf16[256,640]{1,0:T(8,128)(2,1)}, u32[]{:S(2)}) copy-start(bf16[256,640]{1,0:T(8,128)(2,1)} %get-tuple-element.27.x_ref) | copy-start | bytes 983044
  61.0 10.1 %collective-permute-start.4 = (bf16[256,2560]{1,0:T(8,128)(2,1)}, bf16[256,2560]{1,0:T(8,128)(2,1)S(1)}, u32[]{:S(2)}, u32[]{:S(2)}) collective-permute-start(bf16[256,2560]{1,0:T(8,128)(2,1)} %all-gather.2.cloned.1.call-done.grad_ref), channel_id=1, source_target_pairs={{0,4},{4,0},{1,5},{5,1},{2,6},{6,2},{3,7},{7,3},{8,12},{12,8},{9,1... | collective-permute-start | bytes 3932168 | tf_op jit(solution)/shard_map/ppermute | solution.py:200
  67.0 4.2 %collective-permute-start.5 = (bf16[1280,256]{1,0:T(8,128)(2,1)S(1)}, bf16[1280,256]{1,0:T(8,128)(2,1)S(1)}, u32[]{:S(2)}, u32[]{:S(2)}) collective-permute-start(bf16[1280,256]{1,0:T(8,128)(2,1)S(1)} %get-tuple-element.28), channel_id=1, source_target_pairs={{0,4},{4,0},{1,5},{5,1},{2,6},{6,2},{3,7},{7,3},{8,12},{12,8},{9,1... | collective-permute-start | bytes 1966088 | tf_op jit(solution)/shard_map/ppermute | solution.py:198
  68.9 1.3 copy-start.3
  70.2 1.0 copy-start.9
  71.1 1.0 copy-start.10
  71.2 37.0 %copy-start.4 = (bf16[256,2560]{1,0:T(8,128)(2,1)S(1)}, bf16[256,2560]{1,0:T(8,128)(2,1)}, u32[]{:S(2)}) copy-start(bf16[256,2560]{1,0:T(8,128)(2,1)} %all-gather.2.cloned.1.call-done.grad_ref) | copy-start | bytes 3932164
  72.1 36.1 %copy-start.2 = (bf16[640,1280]{1,0:T(8,128)(2,1)S(1)}, bf16[640,1280]{1,0:T(8,128)(2,1)}, u32[]{:S(2)}) copy-start(bf16[640,1280]{1,0:T(8,128)(2,1)} %own_ref.3) | copy-start | bytes 4915204
  84.2 8.7 %collective-permute-start.6 = (bf16[40,256]{1,0:T(8,128)(2,1)S(1)}, bf16[40,256]{1,0:T(8,128)(2,1)S(1)}, u32[]{:S(2)}, u32[]{:S(2)}) collective-permute-start(bf16[40,256]{1,0:T(8,128)(2,1)S(1)} %reduce_sum.12), channel_id=1, source_target_pairs={{0,32},{32,0},{64,96},{96,64},{1,33},{33,1},{65,97},{97,65},{2,34}... | collective-permute-start | bytes 61448 | tf_op jit(solution)/shard_map/ppermute | solution.py:39
  92.9 10.9 %collective-permute-start.7 = (bf16[40,256]{1,0:T(8,128)(2,1)S(1)}, bf16[40,256]{1,0:T(8,128)(2,1)S(1)}, u32[]{:S(2)}, u32[]{:S(2)}) collective-permute-start(bf16[40,256]{1,0:T(8,128)(2,1)S(1)} %add_convert_fusion), channel_id=1, source_target_pairs={{0,96},{96,0},{32,64},{64,32},{1,97},{97,1},{33,65},{65,33},{2,98}... | collective-permute-start | bytes 61448 | tf_op jit(solution)/shard_map/ppermute | solution.py:39
  104.6 11.5 %all-to-all-start.2 = ((bf16[16,40,256]{2,1,0:T(8,128)(2,1)}), bf16[16,40,256]{2,1,0:T(8,128)(2,1)S(1)}, u32[]{:S(2)}, u32[]{:S(2)}) async-start(bf16[16,40,256]{2,1,0:T(8,128)(2,1)} %broadcast_in_dim.15), calls=%async_computation.2 | async-start | bytes 655360 | tf_op jit(solution)/shard_map/all_to_all | solution.py:22
  116.1 7.6 %collective-permute-start.8 = (bf16[640,256]{1,0:T(8,128)(2,1)S(1)}, bf16[640,256]{1,0:T(8,128)(2,1)S(1)}, u32[]{:S(2)}, u32[]{:S(2)}) collective-permute-start(bf16[640,256]{1,0:T(8,128)(2,1)S(1)} %bitcast.22), channel_id=1, source_target_pairs={{0,4},{4,0},{1,5},{5,1},{2,6},{6,2},{3,7},{7,3},{8,12},{12,8},{9,1... | collective-permute-start | bytes 983048 | tf_op jit(solution)/shard_map/ppermute | solution.py:217
  123.8 1.1 copy-start.5
  124.9 1.1 copy-start.11
  125.9 1.1 copy-start.12
Sparse Core Ops, SparseCore 0:
  18.5 42.4 all-gather.1
  64.4 42.4 reduce-scatter.1

commit v9 on v8

--- a/solution.py
+++ b/solution.py
@@ -42,7 +42,9 @@
 
 VMEM = pl.BlockSpec(memory_space=pltpu.VMEM)
 SMEM = pl.BlockSpec(memory_space=pltpu.SMEM)
+FAR = pl.BlockSpec(memory_space=pltpu.HBM)
 ROOM = pltpu.CompilerParams(vmem_limit_bytes=40 * 2**20)
+ALL = pltpu.CompilerParams(vmem_limit_bytes=63 * 2**20)
 
 
 def cost(flops, moved):
@@ -112,7 +114,7 @@
         out_shape=(x_shape, x_shape),
         in_specs=[whole] * 3,
         out_specs=(whole,) * 2,
-        compiler_params=pltpu.CompilerParams(vmem_limit_bytes=63 * 2**20),
+        compiler_params=ALL,
         cost_estimate=cost(2 * 640 * 640 * 512, 2_200_000),
     )(order, rows, rows_other)
 
@@ -139,27 +141,74 @@
     )(basis, rows, grads, *before)
 
 
-def update_kernel(own_ref, other_ref, order_ref, basis_ref, basis_other_ref, out_ref):
-    total = None
-    for rows, basis in ((own_ref, basis_ref), (other_ref, basis_other_ref)):
-        direction = jnp.dot(order_ref[...], rows[...], preferred_element_type=F32).astype(BF16)
-        part = lax.dot_general(
-            direction, basis[...], (((1,), (1,)), ((), ())), preferred_element_type=F32
-        )
-        total = part if total is None else total + part
-    out_ref[...] = total.astype(BF16)
-
-
-def update_matmul(rows, rows_other, order, basis, basis_other):
+def fetch(pairs, sems):
+    copies = [
+        pltpu.make_async_copy(source, target, sems.at[i]) for i, (source, target) in enumerate(pairs)
+    ]
+    for copy in copies:
+        copy.start()
+    return copies
+
+
+def update_kernel(
+    place_ref, own_hbm, other_hbm, basis_hbm, basis_other_hbm, out_hbm,
+    rows_ref, basis_ref, out_ref, sems, out_sems,
+):
+    copies = fetch(
+        [
+            (own_hbm, rows_ref.at[0]),
+            (other_hbm, rows_ref.at[1]),
+            (basis_hbm, basis_ref.at[0]),
+            (basis_other_hbm, basis_ref.at[1]),
+        ],
+        sems,
+    )
+    natural = lax.broadcasted_iota(jnp.int32, (640, 640), 0)
+    order = jnp.where(natural == place_ref[...], 1.0, 0.0).astype(BF16)
+    directions = []
+    for which in range(2):
+        copies[which].wait()
+        moved = jnp.dot(order, rows_ref[which], preferred_element_type=F32)
+        directions.append(moved.astype(BF16))
+    copies[2].wait()
+    copies[3].wait()
+    leaving = []
+    for block in range(out_ref.shape[0]):
+        cols = slice(256 * block, 256 * (block + 1))
+        parts = [
+            lax.dot_general(
+                directions[which],
+                basis_ref[which, cols],
+                (((1,), (1,)), ((), ())),
+                preferred_element_type=F32,
+            )
+            for which in range(2)
+        ]
+        out_ref[block] = (parts[0] + parts[1]).astype(BF16)
+        copy = pltpu.make_async_copy(out_ref.at[block], out_hbm.at[:, cols], out_sems.at[block])
+        copy.start()
+        leaving.append(copy)
+    for copy in leaving:
+        copy.wait()
+
+
+def update_matmul(place, rows, rows_other, basis, basis_other):
     half = basis.shape[0]
     return pl.pallas_call(
         update_kernel,
         out_shape=jax.ShapeDtypeStruct((640, half), BF16),
-        in_specs=[VMEM] * 5,
-        out_specs=VMEM,
-        compiler_params=ROOM,
+        in_specs=[pl.BlockSpec()] + [FAR] * 4,
+        out_specs=FAR,
+        scratch_shapes=[
+            pltpu.VMEM((2, 640, 256), BF16),
+            pltpu.VMEM((2, half, 256), BF16),
+            pltpu.VMEM((half // 256, 640, 256), BF16),
+            pltpu.SemaphoreType.DMA((4,)),
+            pltpu.SemaphoreType.DMA((half // 256,)),
+        ],
+        compiler_params=ALL,
         cost_estimate=cost(2 * 640 * 512 * (640 + half), 5_000_000),
-    )(rows, rows_other, order, basis, basis_other)
+    )(place, rows, rows_other, basis, basis_other)
 
 
 def shards(x_heads, proj_weight, out_grad, proj_basis, first_moment, second_moment):
@@ -216,7 +265,8 @@
     rows, head_rows, mixed_out = lax.optimization_barrier((rows, head_rows, mixed_out))
     rows_other = lax.ppermute(rows, "core", CORE_SWAP)
 
-    update = update_matmul(rows, rows_other, order, basis_own, basis_other)
+    place = jnp.asarray(ORDER.argmax(0).reshape(1, 640), jnp.int32)
+    update = update_matmul(place, rows, rows_other, basis_own, basis_other)
     return (mixed_out, head_rows, update)
 
 

time: 138 us -> 138 us (level)
  Pallas kernels: 14.7 us -> 16.5 us
  local copies, waits for them, and re-layouts: 12.1 us -> 10.3 us
    pallas_call x1, Pallas kernels: 3 us -> 4.81 us  [update_matmul(): pl.pallas_call(update_kernel, out_shape=jax.ShapeDtypeStruct((640, half),...]
    unnamed x28 -> x26, local copies, waits for them, and re-layouts: 6.85 us -> 5.05 us
where the time goes in v9:
time: 138 us; the launch traced here: 137 us
  starting transfers between devices  69.1 us (50%)
  Pallas kernels  16.5 us (12%)
  waiting for transfers between devices  14.5 us (11%)
  between operations  14.4 us (10%)
  blocking collectives  12 us (9%)
  local copies, waits for them, and re-layouts  10.3 us (7%)
    ppermute x2, starting transfers between devices, sum_zh(): values = sent.astype(F32) + lax.ppermute(sent, 'zh', partners).astype(F32)  16.5 us
    all_to_all x1, blocking collectives, shards(): lax.all_to_all(low_chip.reshape(16, 40, 256), ('y', 'x'), 0, 0, tiled=True)  12 us
    all_to_all x2, starting transfers between devices, spread(): return lax.all_to_all(copies, axes, 0, 0, tiled=True)  10.5 us
    ppermute x1, starting transfers between devices, gather_zh(): got = lax.ppermute(values, 'zh', PAIR)  9.65 us
    ppermute x1, starting transfers between devices, gather_zh(): got = lax.ppermute(pair, 'zh', MIRROR)  9.28 us
    ppermute x1, starting transfers between devices, shards(): rows_other = lax.ppermute(rows, 'core', CORE_SWAP)  6.4 us
    ppermute x1, starting transfers between devices, shards(): x_other = lax.ppermute(x_heads, 'core', CORE_SWAP)  5.94 us
    ppermute x1, starting transfers between devices, shards(): grad_other = lax.ppermute(grad_block, 'core', CORE_SWAP)  5.93 us
  transfers between devices with their start and end apart: 13, of which 8 were waited for; matrix products, arithmetic and copies ran while one was open for 3% of the time, Pallas kernels for 9%

profile of v9, /device:TPU:1, one launch (start us, length us, event | category | flops | bytes accessed | tf_op | source)
XLA Modules:
  0.0 137.0 jit_solution(13264500850296790369)
XLA Ops:
  8.7 9.6 %collective-permute-start = (bf16[60,256]{1,0:T(8,128)(2,1)S(1)}, bf16[60,256]{1,0:T(8,128)(2,1)S(1)}, u32[]{:S(2)}, u32[]{:S(2)}) collective-permute-start(bf16[60,256]{1,0:T(8,128)(2,1)S(1)} %pad_maximum_fusion.2), channel_id=1, source_target_pairs={{0,32},{32,0},{64,96},{96,64},{1,33},{33,1},{65,97},{97,65},{2,34}... | collective-permute-start | bytes 92168 | tf_op jit(solution)/shard_map/ppermute | solution.py:27
  18.4 2.9 %collective-permute-start.2 = (bf16[640,1280]{1,0:T(8,128)(2,1)}, bf16[640,1280]{1,0:T(8,128)(2,1)}, u32[]{:S(2)}, u32[]{:S(2)}) collective-permute-start(bf16[640,1280]{1,0:T(8,128)(2,1)} %own_ref.3), channel_id=1, source_target_pairs={{0,4},{4,0},{1,5},{5,1},{2,6},{6,2},{3,7},{7,3},{8,12},{12,8},{9,1... | collective-permute-start | bytes 4915208 | tf_op jit(solution)/shard_map/ppermute | solution.py:223
  21.4 9.3 %collective-permute-start.1 = (bf16[120,256]{1,0:T(8,128)(2,1)S(1)}, bf16[120,256]{1,0:T(8,128)(2,1)S(1)}, u32[]{:S(2)}, u32[]{:S(2)}) collective-permute-start(bf16[120,256]{1,0:T(8,128)(2,1)S(1)} %pad_maximum_fusion.1), channel_id=1, source_target_pairs={{0,96},{96,0},{32,64},{64,32},{1,97},{97,1},{33,65},{65,33},{2,98}... | collective-permute-start | bytes 184328 | tf_op jit(solution)/shard_map/ppermute | solution.py:30
  30.6 1.9 %collective-permute-done.1 = bf16[120,256]{1,0:T(8,128)(2,1)S(1)} collective-permute-done((bf16[120,256]{1,0:T(8,128)(2,1)S(1)}, bf16[120,256]{1,0:T(8,128)(2,1)S(1)}, u32[]{:S(2)}, u32[]{:S(2)}) %collective-permute-start.1) | collective-permute-done | bytes 61472 | tf_op jit(solution)/shard_map/ppermute | solution.py:30
  32.6 1.3 broadcast_in_dim.14
  33.9 6.9 %all-to-all-start = ((bf16[16,160,256]{2,1,0:T(8,128)(2,1)}), bf16[16,160,256]{2,1,0:T(8,128)(2,1)}, u32[]{:S(2)}, u32[]{:S(2)}) async-start(bf16[16,160,256]{2,1,0:T(8,128)(2,1)} %broadcast_in_dim.14), calls=%async_computation | async-start | bytes 2621440 | tf_op jit(solution)/shard_map/all_to_all | solution.py:22
  40.9 5.9 %collective-permute-start.3 = (bf16[256,640]{1,0:T(8,128)(2,1)S(1)}, bf16[256,640]{1,0:T(8,128)(2,1)}, u32[]{:S(2)}, u32[]{:S(2)}) collective-permute-start(bf16[256,640]{1,0:T(8,128)(2,1)S(1)} %copy-done.5), channel_id=1, source_target_pairs={{0,4},{4,0},{1,5},{5,1},{2,6},{6,2},{3,7},{7,3},{8,12},{12,8},{9,1... | collective-permute-start | bytes 983048 | tf_op jit(solution)/shard_map/ppermute | solution.py:224
  46.9 1.3 collective-permute-done.3.xo_ref
  48.2 2.8 %shard_map.104 = (bf16[256,640]{1,0:T(8,128)(2,1)}, bf16[256,640]{1,0:T(8,128)(2,1)}) custom-call(bf16[640,640]{1,0:T(8,128)(2,1)} %constant.59.clone.order_ref, bf16[256,640]{1,0:T(8,128)(2,1)} %x_ref.3, bf16[256,640]{1,0:T(8,128)(2,1)} %collective-permute-done.3.xo_ref), custom_call_target="tpu_custom_call" | custom-call | flops 419430400 | bytes 2200000 | tf_op jit(solution)/shard_map/pallas_call | solution.py:112
  51.0 1.4 %copy-done.1 = bf16[640,1280]{1,0:T(8,128)(2,1)S(1)} copy-done((bf16[640,1280]{1,0:T(8,128)(2,1)S(1)}, bf16[640,1280]{1,0:T(8,128)(2,1)}, u32[]{:S(2)}) %copy-start.1) | copy-done | bytes 1638424
  52.5 3.7 %shard_map.103 = bf16[256,2560]{1,0:T(8,128)(2,1)} custom-call(s32[1]{0:T(128)} %bitcast.3.core_ref, bf16[256,640]{1,0:T(8,128)(2,1)S(1)} %copy-done.6, bf16[640,1280]{1,0:T(8,128)(2,1)S(1)} %copy-done.1, bf16[640,1280]{1,0:T(8,128)(2,1)} %collective-permute-done.2.other_ref), custom_call_target="tpu_custom_call" | custom-call | flops 838860800 | bytes 5000000 | tf_op jit(solution)/shard_map/pallas_call | solution.py:67
  56.2 1.1 all-to-all-done
  57.2 1.4 %copy.11 = bf16[4,4,4,40,256]{4,3,2,1,0:T(8,128)(2,1)S(1)} copy(bf16[4,4,4,40,256]{4,3,1,2,0:T(8,128)(2,1)} %bitcast.5) | data formatting | bytes 2621440 | tf_op jit(solution)/shard_map/transpose | solution.py:238
  58.7 0.9 constant_dynamic-slice_fusion
  59.7 1.4 all-gather.2.cloned.1.call-done.grad_ref
  61.0 5.9 %collective-permute-start.4 = (bf16[256,2560]{1,0:T(8,128)(2,1)}, bf16[256,2560]{1,0:T(8,128)(2,1)S(1)}, u32[]{:S(2)}, u32[]{:S(2)}) collective-permute-start(bf16[256,2560]{1,0:T(8,128)(2,1)} %all-gather.2.cloned.1.call-done.grad_ref), channel_id=1, source_target_pairs={{0,4},{4,0},{1,5},{5,1},{2,6},{6,2},{3,7},{7,3},{8,12},{12,8},{9,1... | collective-permute-start | bytes 3932168 | tf_op jit(solution)/shard_map/ppermute | solution.py:249
  67.0 1.9 %collective-permute-start.5 = (bf16[1280,256]{1,0:T(8,128)(2,1)S(1)}, bf16[1280,256]{1,0:T(8,128)(2,1)S(1)}, u32[]{:S(2)}, u32[]{:S(2)}) collective-permute-start(bf16[1280,256]{1,0:T(8,128)(2,1)S(1)} %get-tuple-element.28), channel_id=1, source_target_pairs={{0,4},{4,0},{1,5},{5,1},{2,6},{6,2},{3,7},{7,3},{8,12},{12,8},{9,1... | collective-permute-start | bytes 1966088 | tf_op jit(solution)/shard_map/ppermute | solution.py:247
  68.9 1.3 copy-done.3
  70.2 0.9 shard_map.105.refs_0_
  71.2 0.8 copy-done.10
  72.0 0.9 shard_map.106
  72.9 12.0 %all_to_all.15 = bf16[16,40,256]{2,1,0:T(8,128)(2,1)S(1)} all-to-all(bf16[16,40,256]{2,1,0:T(8,128)(2,1)S(1)} %bitcast.21), channel_id=1, replica_groups=mesh['y'=4,'zh'=4,'x'=4,'core'=2,'zl'=4] {'y','x'}, dimensions={0} | all-to-all | bytes 655360 | tf_op jit(solution)/shard_map/all_to_all | solution.py:254
  85.0 7.4 %collective-permute-start.6 = (bf16[40,256]{1,0:T(8,128)(2,1)S(1)}, bf16[40,256]{1,0:T(8,128)(2,1)S(1)}, u32[]{:S(2)}, u32[]{:S(2)}) collective-permute-start(bf16[40,256]{1,0:T(8,128)(2,1)S(1)} %reduce_sum.12), channel_id=1, source_target_pairs={{0,32},{32,0},{64,96},{96,64},{1,33},{33,1},{65,97},{97,65},{2,34}... | collective-permute-start | bytes 61448 | tf_op jit(solution)/shard_map/ppermute | solution.py:39
  92.3 1.3 collective-permute-done.6
  93.7 9.2 %collective-permute-start.7 = (bf16[40,256]{1,0:T(8,128)(2,1)S(1)}, bf16[40,256]{1,0:T(8,128)(2,1)S(1)}, u32[]{:S(2)}, u32[]{:S(2)}) collective-permute-start(bf16[40,256]{1,0:T(8,128)(2,1)S(1)} %add_convert_fusion), channel_id=1, source_target_pairs={{0,96},{96,0},{32,64},{64,32},{1,97},{97,1},{33,65},{65,33},{2,98}... | collective-permute-start | bytes 61448 | tf_op jit(solution)/shard_map/ppermute | solution.py:39
  102.8 1.8 %collective-permute-done.7 = bf16[40,256]{1,0:T(8,128)(2,1)S(1)} collective-permute-done((bf16[40,256]{1,0:T(8,128)(2,1)S(1)}, bf16[40,256]{1,0:T(8,128)(2,1)S(1)}, u32[]{:S(2)}, u32[]{:S(2)}) %collective-permute-start.7) | collective-permute-done | bytes 20512 | tf_op jit(solution)/shard_map/ppermute | solution.py:39
  105.4 3.5 %all-to-all-start.2 = ((bf16[16,40,256]{2,1,0:T(8,128)(2,1)}), bf16[16,40,256]{2,1,0:T(8,128)(2,1)S(1)}, u32[]{:S(2)}, u32[]{:S(2)}) async-start(bf16[16,40,256]{2,1,0:T(8,128)(2,1)} %broadcast_in_dim.15), calls=%async_computation.2 | async-start | bytes 655360 | tf_op jit(solution)/shard_map/all_to_all | solution.py:22
  109.0 3.4 %shard_map.107 = bf16[256,640]{1,0:T(8,128)(2,1)} custom-call(s32[1]{0:T(128)} %bitcast.3.core_ref, bf16[256,2560]{1,0:T(8,128)(2,1)S(1)} %copy-done.4, bf16[640,1280]{1,0:T(8,128)(2,1)S(1)} %copy-done.2, bf16[640,1280]{1,0:T(8,128)(2,1)} %collective-permute-done.2.other_ref), custom_call_target="tpu_custom_call" | custom-call | flops 838860800 | bytes 5000000 | tf_op jit(solution)/shard_map/pallas_call | solution.py:93
  112.3 4.6 %all-to-all-done.2 = bf16[16,40,256]{2,1,0:T(8,128)(2,1)S(1)} async-done(((bf16[16,40,256]{2,1,0:T(8,128)(2,1)}), bf16[16,40,256]{2,1,0:T(8,128)(2,1)S(1)}, u32[]{:S(2)}, u32[]{:S(2)}) %all-to-all-start.2) | async-done | bytes 327712 | tf_op jit(solution)/shard_map/all_to_all | solution.py:22
  116.9 6.4 %collective-permute-start.8 = (bf16[640,256]{1,0:T(8,128)(2,1)S(1)}, bf16[640,256]{1,0:T(8,128)(2,1)S(1)}, u32[]{:S(2)}, u32[]{:S(2)}) collective-permute-start(bf16[640,256]{1,0:T(8,128)(2,1)S(1)} %bitcast.22), channel_id=1, source_target_pairs={{0,4},{4,0},{1,5},{5,1},{2,6},{6,2},{3,7},{7,3},{8,12},{12,8},{9,1... | collective-permute-start | bytes 983048 | tf_op jit(solution)/shard_map/ppermute | solution.py:266
  123.3 1.2 collective-permute-done.8.other_hbm
  125.3 4.8 %shard_map.108 = bf16[640,1280]{1,0:T(8,128)(2,1)} custom-call(s32[1,640]{1,0:T(1,128)} %constant.60.clone.place_ref, bf16[640,256]{1,0:T(8,128)(2,1)} %bitcast.23, bf16[640,256]{1,0:T(8,128)(2,1)} %copy-done.11, bf16[1280,256]{1,0:T(8,128)(2,1)} %get-tuple-element.35.basis_hbm, bf16[1280,256]{1,0:T(8,128)(2,1)} %copy-done.10), custom_call_target="tpu_custom_call" | custom-call | flops 1258291200 | bytes 5000000 | tf_op jit(solution)/shard_map/pallas_call | solution.py:197
  (48 shorter events, 3.4 us)
Async XLA Ops:
  7.2 0.8 copy-start
  7.2 53.9 %all-gather.2.cloned.1.call-start = ((), (), s32[]{:S(2)}) async-start(), calls=%async_computation.4 | async-start | bytes 1638400 | tf_op jit(solution)/shard_map/all_gather | solution.py:222
  8.7 12.6 %collective-permute-start = (bf16[60,256]{1,0:T(8,128)(2,1)S(1)}, bf16[60,256]{1,0:T(8,128)(2,1)S(1)}, u32[]{:S(2)}, u32[]{:S(2)}) collective-permute-start(bf16[60,256]{1,0:T(8,128)(2,1)S(1)} %pad_maximum_fusion.2), channel_id=1, source_target_pairs={{0,32},{32,0},{64,96},{96,64},{1,33},{33,1},{65,97},{97,65},{2,34}... | collective-permute-start | bytes 92168 | tf_op jit(solution)/shard_map/ppermute | solution.py:27
  18.4 32.6 %collective-permute-start.2 = (bf16[640,1280]{1,0:T(8,128)(2,1)}, bf16[640,1280]{1,0:T(8,128)(2,1)}, u32[]{:S(2)}, u32[]{:S(2)}) collective-permute-start(bf16[640,1280]{1,0:T(8,128)(2,1)} %own_ref.3), channel_id=1, source_target_pairs={{0,4},{4,0},{1,5},{5,1},{2,6},{6,2},{3,7},{7,3},{8,12},{12,8},{9,1... | collective-permute-start | bytes 4915208 | tf_op jit(solution)/shard_map/ppermute | solution.py:223
  21.4 11.2 %collective-permute-start.1 = (bf16[120,256]{1,0:T(8,128)(2,1)S(1)}, bf16[120,256]{1,0:T(8,128)(2,1)S(1)}, u32[]{:S(2)}, u32[]{:S(2)}) collective-permute-start(bf16[120,256]{1,0:T(8,128)(2,1)S(1)} %pad_maximum_fusion.1), channel_id=1, source_target_pairs={{0,96},{96,0},{32,64},{64,32},{1,97},{97,1},{33,65},{65,33},{2,98}... | collective-permute-start | bytes 184328 | tf_op jit(solution)/shard_map/ppermute | solution.py:30
  33.9 7.0 %copy-start.5 = (bf16[256,640]{1,0:T(8,128)(2,1)S(1)}, bf16[256,640]{1,0:T(8,128)(2,1)}, u32[]{:S(2)}) copy-start(bf16[256,640]{1,0:T(8,128)(2,1)} %x_ref.3) | copy-start | bytes 983044
  33.9 23.3 %all-to-all-start = ((bf16[16,160,256]{2,1,0:T(8,128)(2,1)}), bf16[16,160,256]{2,1,0:T(8,128)(2,1)}, u32[]{:S(2)}, u32[]{:S(2)}) async-start(bf16[16,160,256]{2,1,0:T(8,128)(2,1)} %broadcast_in_dim.14), calls=%async_computation | async-start | bytes 2621440 | tf_op jit(solution)/shard_map/all_to_all | solution.py:22
  40.8 10.2 %copy-start.6 = (bf16[256,640]{1,0:T(8,128)(2,1)S(1)}, bf16[256,640]{1,0:T(8,128)(2,1)}, u32[]{:S(2)}) copy-start(bf16[256,640]{1,0:T(8,128)(2,1)} %x_ref.3) | copy-start | bytes 983044
  40.9 76.1 %reduce-scatter.2.cloned.1.call-start = ((), (), s32[]{:S(2)}) async-start(), calls=%async_computation.5 | async-start | bytes 1638400 | tf_op jit(solution)/shard_map/reduce_scatter | solution.py:240
  40.9 7.3 %collective-permute-start.3 = (bf16[256,640]{1,0:T(8,128)(2,1)S(1)}, bf16[256,640]{1,0:T(8,128)(2,1)}, u32[]{:S(2)}, u32[]{:S(2)}) collective-permute-start(bf16[256,640]{1,0:T(8,128)(2,1)S(1)} %copy-done.5), channel_id=1, source_target_pairs={{0,4},{4,0},{1,5},{5,1},{2,6},{6,2},{3,7},{7,3},{8,12},{12,8},{9,1... | collective-permute-start | bytes 983048 | tf_op jit(solution)/shard_map/ppermute | solution.py:224
  51.0 1.4 %copy-start.1 = (bf16[640,1280]{1,0:T(8,128)(2,1)S(1)}, bf16[640,1280]{1,0:T(8,128)(2,1)}, u32[]{:S(2)}) copy-start(bf16[640,1280]{1,0:T(8,128)(2,1)} %own_ref.3) | copy-start | bytes 4915204
  58.7 10.2 %copy-start.7 = (bf16[256,640]{1,0:T(8,128)(2,1)S(1)}, bf16[256,640]{1,0:T(8,128)(2,1)}, u32[]{:S(2)}) copy-start(bf16[256,640]{1,0:T(8,128)(2,1)} %get-tuple-element.27.x_ref) | copy-start | bytes 983044
  61.0 11.0 %collective-permute-start.4 = (bf16[256,2560]{1,0:T(8,128)(2,1)}, bf16[256,2560]{1,0:T(8,128)(2,1)S(1)}, u32[]{:S(2)}, u32[]{:S(2)}) collective-permute-start(bf16[256,2560]{1,0:T(8,128)(2,1)} %all-gather.2.cloned.1.call-done.grad_ref), channel_id=1, source_target_pairs={{0,4},{4,0},{1,5},{5,1},{2,6},{6,2},{3,7},{7,3},{8,12},{12,8},{9,1... | collective-permute-start | bytes 3932168 | tf_op jit(solution)/shard_map/ppermute | solution.py:249
  67.0 4.2 %collective-permute-start.5 = (bf16[1280,256]{1,0:T(8,128)(2,1)S(1)}, bf16[1280,256]{1,0:T(8,128)(2,1)S(1)}, u32[]{:S(2)}, u32[]{:S(2)}) collective-permute-start(bf16[1280,256]{1,0:T(8,128)(2,1)S(1)} %get-tuple-element.28), channel_id=1, source_target_pairs={{0,4},{4,0},{1,5},{5,1},{2,6},{6,2},{3,7},{7,3},{8,12},{12,8},{9,1... | collective-permute-start | bytes 1966088 | tf_op jit(solution)/shard_map/ppermute | solution.py:247
  68.9 1.3 copy-start.3
  70.2 1.8 %copy-start.8 = (bf16[256,640]{1,0:T(8,128)(2,1)S(1)}, bf16[256,640]{1,0:T(8,128)(2,1)}, u32[]{:S(2)}) copy-start(bf16[256,640]{1,0:T(8,128)(2,1)} %get-tuple-element.25.x_ref) | copy-start | bytes 983044
  71.1 0.8 copy-start.10
  72.0 37.0 %copy-start.4 = (bf16[256,2560]{1,0:T(8,128)(2,1)S(1)}, bf16[256,2560]{1,0:T(8,128)(2,1)}, u32[]{:S(2)}) copy-start(bf16[256,2560]{1,0:T(8,128)(2,1)} %all-gather.2.cloned.1.call-done.grad_ref) | copy-start | bytes 3932164
  72.9 36.1 %copy-start.2 = (bf16[640,1280]{1,0:T(8,128)(2,1)S(1)}, bf16[640,1280]{1,0:T(8,128)(2,1)}, u32[]{:S(2)}) copy-start(bf16[640,1280]{1,0:T(8,128)(2,1)} %own_ref.3) | copy-start | bytes 4915204
  85.0 8.7 %collective-permute-start.6 = (bf16[40,256]{1,0:T(8,128)(2,1)S(1)}, bf16[40,256]{1,0:T(8,128)(2,1)S(1)}, u32[]{:S(2)}, u32[]{:S(2)}) collective-permute-start(bf16[40,256]{1,0:T(8,128)(2,1)S(1)} %reduce_sum.12), channel_id=1, source_target_pairs={{0,32},{32,0},{64,96},{96,64},{1,33},{33,1},{65,97},{97,65},{2,34}... | collective-permute-start | bytes 61448 | tf_op jit(solution)/shard_map/ppermute | solution.py:39
  93.7 10.9 %collective-permute-start.7 = (bf16[40,256]{1,0:T(8,128)(2,1)S(1)}, bf16[40,256]{1,0:T(8,128)(2,1)S(1)}, u32[]{:S(2)}, u32[]{:S(2)}) collective-permute-start(bf16[40,256]{1,0:T(8,128)(2,1)S(1)} %add_convert_fusion), channel_id=1, source_target_pairs={{0,96},{96,0},{32,64},{64,32},{1,97},{97,1},{33,65},{65,33},{2,98}... | collective-permute-start | bytes 61448 | tf_op jit(solution)/shard_map/ppermute | solution.py:39
  105.4 11.5 %all-to-all-start.2 = ((bf16[16,40,256]{2,1,0:T(8,128)(2,1)}), bf16[16,40,256]{2,1,0:T(8,128)(2,1)S(1)}, u32[]{:S(2)}, u32[]{:S(2)}) async-start(bf16[16,40,256]{2,1,0:T(8,128)(2,1)} %broadcast_in_dim.15), calls=%async_computation.2 | async-start | bytes 655360 | tf_op jit(solution)/shard_map/all_to_all | solution.py:22
  116.9 7.7 %copy-start.9 = (bf16[16,40,256]{2,1,0:T(8,128)(2,1)}, bf16[16,40,256]{2,1,0:T(8,128)(2,1)S(1)}, u32[]{:S(2)}) copy-start(bf16[16,40,256]{2,1,0:T(8,128)(2,1)S(1)} %all-to-all-done.2) | copy-start | bytes 983044
  116.9 7.6 %collective-permute-start.8 = (bf16[640,256]{1,0:T(8,128)(2,1)S(1)}, bf16[640,256]{1,0:T(8,128)(2,1)S(1)}, u32[]{:S(2)}, u32[]{:S(2)}) collective-permute-start(bf16[640,256]{1,0:T(8,128)(2,1)S(1)} %bitcast.22), channel_id=1, source_target_pairs={{0,4},{4,0},{1,5},{5,1},{2,6},{6,2},{3,7},{7,3},{8,12},{12,8},{9,1... | collective-permute-start | bytes 983048 | tf_op jit(solution)/shard_map/ppermute | solution.py:266
  124.6 0.7 copy-start.11
Sparse Core Ops, SparseCore 0:
  18.5 42.4 all-gather.1
  64.4 42.4 reduce-scatter.1

commit v10 on v8

--- a/solution.py
+++ b/solution.py
@@ -139,10 +139,13 @@
     )(basis, rows, grads, *before)
 
 
-def update_kernel(own_ref, other_ref, order_ref, basis_ref, basis_other_ref, out_ref):
+def update_kernel(core_ref, rows_ref, order_ref, basis_ref, basis_other_ref, out_ref):
+    core = core_ref[0]
     total = None
-    for rows, basis in ((own_ref, basis_ref), (other_ref, basis_other_ref)):
-        direction = jnp.dot(order_ref[...], rows[...], preferred_element_type=F32).astype(BF16)
+    for which, basis in ((core, basis_ref), (1 - core, basis_other_ref)):
+        direction = jnp.dot(
+            order_ref[...], rows_ref[which], preferred_element_type=F32
+        ).astype(BF16)
         part = lax.dot_general(
             direction, basis[...], (((1,), (1,)), ((), ())), preferred_element_type=F32
         )
@@ -150,16 +153,16 @@
     out_ref[...] = total.astype(BF16)
 
 
-def update_matmul(rows, rows_other, order, basis, basis_other):
+def update_matmul(core, rows, order, basis, basis_other):
     half = basis.shape[0]
     return pl.pallas_call(
         update_kernel,
         out_shape=jax.ShapeDtypeStruct((640, half), BF16),
-        in_specs=[VMEM] * 5,
+        in_specs=[SMEM] + [VMEM] * 4,
         out_specs=VMEM,
         compiler_params=ROOM,
         cost_estimate=cost(2 * 640 * 512 * (640 + half), 5_000_000),
-    )(rows, rows_other, order, basis, basis_other)
+    )(core, rows, order, basis, basis_other)
 
 
 def shards(x_heads, proj_weight, out_grad, proj_basis, first_moment, second_moment):
@@ -211,12 +214,11 @@
     corr_two = 1.0 - 0.999**ADAM_STEP
     direction = (m_new / corr_one / (jnp.sqrt(v_new / corr_two) + 1e-08)).astype(BF16)
 
-    rows = spread(direction, ("y", "x"), 16).reshape(640, 256)
+    rows = spread(direction, ("core", "y", "x"), 32).reshape(2, 640, 256)
     head_rows = head_matmul(scalar, grad_block, proj_weight, weight_other)
     rows, head_rows, mixed_out = lax.optimization_barrier((rows, head_rows, mixed_out))
-    rows_other = lax.ppermute(rows, "core", CORE_SWAP)
-
-    update = update_matmul(rows, rows_other, order, basis_own, basis_other)
+
+    update = update_matmul(scalar, rows, order, basis_own, basis_other)
     return (mixed_out, head_rows, update)
 
 

time: 138 us -> 143 us (1.036)
  waiting for transfers between devices: 14.6 us -> 18.2 us
  starting transfers between devices: 69 us -> 67.3 us
  local copies, waits for them, and re-layouts: 12.1 us -> 13.8 us
    ppermute x1 -> x0, starting transfers between devices: 6.4 us -> none  [shards(): rows_other = lax.ppermute(rows, 'core', CORE_SWAP)]
    all_to_all x2, starting transfers between devices: 10.5 us -> 14.6 us  [spread(): return lax.all_to_all(copies, axes, 0, 0, tiled=True)]
    all_to_all x2, waiting for transfers between devices: 5.65 us -> 9.53 us  [spread(): return lax.all_to_all(copies, axes, 0, 0, tiled=True)]
    unnamed x28 -> x30, local copies, waits for them, and re-layouts: 6.85 us -> 8.16 us
  transfers between devices with their start and end apart: 13 -> 12, of which waited for: 8 -> 8; matrix products, arithmetic and copies ran while one was open for 3% -> 4% of each run, Pallas kernels for 9% -> 8%
where the time goes in v10:
time: 143 us; the launch traced here: 142 us
  starting transfers between devices  67.3 us (47%)
  waiting for transfers between devices  18.2 us (13%)
  Pallas kernels  16 us (11%)
  between operations  14.4 us (10%)
  local copies, waits for them, and re-layouts  13.8 us (10%)
  blocking collectives  12 us (8%)
    ppermute x2, starting transfers between devices, sum_zh(): values = sent.astype(F32) + lax.ppermute(sent, 'zh', partners).astype(F32)  16.6 us
    all_to_all x2, starting transfers between devices, spread(): return lax.all_to_all(copies, axes, 0, 0, tiled=True)  14.6 us
    all_to_all x1, blocking collectives, shards(): lax.all_to_all(low_chip.reshape(16, 40, 256), ('y', 'x'), 0, 0, tiled=True)  12 us
    ppermute x1, starting transfers between devices, gather_zh(): got = lax.ppermute(values, 'zh', PAIR)  9.65 us
    all_to_all x2, waiting for transfers between devices, spread(): return lax.all_to_all(copies, axes, 0, 0, tiled=True)  9.53 us
    ppermute x1, starting transfers between devices, gather_zh(): got = lax.ppermute(pair, 'zh', MIRROR)  9.28 us
    unnamed x30, local copies, waits for them, and re-layouts  8.16 us
    ppermute x1, starting transfers between devices, shards(): grad_other = lax.ppermute(grad_block, 'core', CORE_SWAP)  6.3 us
  transfers between devices with their start and end apart: 12, of which 8 were waited for; matrix products, arithmetic and copies ran while one was open for 4% of the time, Pallas kernels for 8%

profile of v10, /device:TPU:1, one launch (start us, length us, event | category | flops | bytes accessed | tf_op | source)
XLA Modules:
  0.0 141.9 jit_solution(1694606339006635624)
XLA Ops:
  8.7 9.6 %collective-permute-start = (bf16[60,256]{1,0:T(8,128)(2,1)S(1)}, bf16[60,256]{1,0:T(8,128)(2,1)S(1)}, u32[]{:S(2)}, u32[]{:S(2)}) collective-permute-start(bf16[60,256]{1,0:T(8,128)(2,1)S(1)} %pad_maximum_fusion.2), channel_id=1, source_target_pairs={{0,32},{32,0},{64,96},{96,64},{1,33},{33,1},{65,97},{97,65},{2,34}... | collective-permute-start | bytes 92168 | tf_op jit(solution)/shard_map/ppermute | solution.py:27
  18.4 2.9 %collective-permute-start.2 = (bf16[640,1280]{1,0:T(8,128)(2,1)}, bf16[640,1280]{1,0:T(8,128)(2,1)}, u32[]{:S(2)}, u32[]{:S(2)}) collective-permute-start(bf16[640,1280]{1,0:T(8,128)(2,1)} %own_ref.3), channel_id=1, source_target_pairs={{0,4},{4,0},{1,5},{5,1},{2,6},{6,2},{3,7},{7,3},{8,12},{12,8},{9,1... | collective-permute-start | bytes 4915208 | tf_op jit(solution)/shard_map/ppermute | solution.py:177
  21.4 9.3 %collective-permute-start.1 = (bf16[120,256]{1,0:T(8,128)(2,1)S(1)}, bf16[120,256]{1,0:T(8,128)(2,1)S(1)}, u32[]{:S(2)}, u32[]{:S(2)}) collective-permute-start(bf16[120,256]{1,0:T(8,128)(2,1)S(1)} %pad_maximum_fusion.1), channel_id=1, source_target_pairs={{0,96},{96,0},{32,64},{64,32},{1,97},{97,1},{33,65},{65,33},{2,98}... | collective-permute-start | bytes 184328 | tf_op jit(solution)/shard_map/ppermute | solution.py:30
  30.6 1.9 %collective-permute-done.1 = bf16[120,256]{1,0:T(8,128)(2,1)S(1)} collective-permute-done((bf16[120,256]{1,0:T(8,128)(2,1)S(1)}, bf16[120,256]{1,0:T(8,128)(2,1)S(1)}, u32[]{:S(2)}, u32[]{:S(2)}) %collective-permute-start.1) | collective-permute-done | bytes 61472 | tf_op jit(solution)/shard_map/ppermute | solution.py:30
  32.7 1.2 broadcast_in_dim.14
  33.9 6.9 %all-to-all-start = ((bf16[16,160,256]{2,1,0:T(8,128)(2,1)}), bf16[16,160,256]{2,1,0:T(8,128)(2,1)}, u32[]{:S(2)}, u32[]{:S(2)}) async-start(bf16[16,160,256]{2,1,0:T(8,128)(2,1)} %broadcast_in_dim.14), calls=%async_computation | async-start | bytes 2621440 | tf_op jit(solution)/shard_map/all_to_all | solution.py:22
  40.9 5.9 %collective-permute-start.3 = (bf16[256,640]{1,0:T(8,128)(2,1)S(1)}, bf16[256,640]{1,0:T(8,128)(2,1)S(1)}, u32[]{:S(2)}, u32[]{:S(2)}) collective-permute-start(bf16[256,640]{1,0:T(8,128)(2,1)S(1)} %copy-done.6), channel_id=1, source_target_pairs={{0,4},{4,0},{1,5},{5,1},{2,6},{6,2},{3,7},{7,3},{8,12},{12,8},{9,1... | collective-permute-start | bytes 983048 | tf_op jit(solution)/shard_map/ppermute | solution.py:178
  46.9 1.2 collective-permute-done.3.xo_ref
  48.8 2.8 %shard_map.95 = (bf16[256,640]{1,0:T(8,128)(2,1)}, bf16[256,640]{1,0:T(8,128)(2,1)}) custom-call(bf16[640,640]{1,0:T(8,128)(2,1)} %constant.57.clone.order_ref, bf16[256,640]{1,0:T(8,128)(2,1)} %x_ref.3, bf16[256,640]{1,0:T(8,128)(2,1)} %copy-done.13), custom_call_target="tpu_custom_call" | custom-call | flops 419430400 | bytes 2200000 | tf_op jit(solution)/shard_map/pallas_call | solution.py:110
  51.6 1.4 %copy-done.1 = bf16[640,1280]{1,0:T(8,128)(2,1)S(1)} copy-done((bf16[640,1280]{1,0:T(8,128)(2,1)S(1)}, bf16[640,1280]{1,0:T(8,128)(2,1)}, u32[]{:S(2)}) %copy-start.1) | copy-done | bytes 1638424
  53.1 2.6 %shard_map.94 = bf16[256,2560]{1,0:T(8,128)(2,1)S(1)} custom-call(s32[1]{0:T(128)} %bitcast.3.core_ref, bf16[256,640]{1,0:T(8,128)(2,1)S(1)} %copy-done.7, bf16[640,1280]{1,0:T(8,128)(2,1)S(1)} %copy-done.1, bf16[640,1280]{1,0:T(8,128)(2,1)} %collective-permute-done.2.other_ref), custom_call_target="tpu_custom_call" | custom-call | flops 838860800 | bytes 5000000 | tf_op jit(solution)/shard_map/pallas_call | solution.py:65
  55.7 1.0 copy-done.4
  57.2 1.4 %copy.10 = bf16[4,4,4,40,256]{4,3,2,1,0:T(8,128)(2,1)S(1)} copy(bf16[4,4,4,40,256]{4,3,1,2,0:T(8,128)(2,1)} %bitcast.5) | data formatting | bytes 2621440 | tf_op jit(solution)/shard_map/transpose | solution.py:192
  58.7 1.2 constant_dynamic-slice_fusion
  59.9 1.1 all-gather.2.cloned.1.call-done.grad_ref
  61.0 6.3 %collective-permute-start.4 = (bf16[256,2560]{1,0:T(8,128)(2,1)}, bf16[256,2560]{1,0:T(8,128)(2,1)}, u32[]{:S(2)}, u32[]{:S(2)}) collective-permute-start(bf16[256,2560]{1,0:T(8,128)(2,1)} %all-gather.2.cloned.1.call-done.grad_ref), channel_id=1, source_target_pairs={{0,4},{4,0},{1,5},{5,1},{2,6},{6,2},{3,7},{7,3},{8,12},{12,8},{9,1... | collective-permute-start | bytes 3932168 | tf_op jit(solution)/shard_map/ppermute | solution.py:203
  67.4 2.1 %collective-permute-start.5 = (bf16[1280,256]{1,0:T(8,128)(2,1)}, bf16[1280,256]{1,0:T(8,128)(2,1)S(1)}, u32[]{:S(2)}, u32[]{:S(2)}) collective-permute-start(bf16[1280,256]{1,0:T(8,128)(2,1)} %get-tuple-element.28), channel_id=1, source_target_pairs={{0,4},{4,0},{1,5},{5,1},{2,6},{6,2},{3,7},{7,3},{8,12},{12,8},{9,1... | collective-permute-start | bytes 1966088 | tf_op jit(solution)/shard_map/ppermute | solution.py:201
  69.5 0.9 shard_map.96.refs_0_
  70.4 1.3 collective-permute-done.5.basis_other_ref
  72.6 2.2 %shard_map.97 = bf16[640,256]{1,0:T(8,128)(2,1)S(1)} custom-call(bf16[2560,256]{1,0:T(8,128)(2,1)S(1)} %bitcast.20, bf16[256,640]{1,0:T(8,128)(2,1)S(1)} %copy-done.9, bf16[256,2560]{1,0:T(8,128)(2,1)} %collective-permute-done.4.grad_ref, f32[640,256]{1,0:T(8,128)S(1)} %shard_map.96.refs_0_), custom_call_target="tpu_custom_call" | custom-call | flops 419430400 | bytes 3500000 | tf_op jit(solution)/shard_map/pallas_call | solution.py:132
  74.8 12.0 %all_to_all.15 = bf16[16,40,256]{2,1,0:T(8,128)(2,1)S(1)} all-to-all(bf16[16,40,256]{2,1,0:T(8,128)(2,1)S(1)} %bitcast.21), channel_id=1, replica_groups=mesh['y'=4,'zh'=4,'x'=4,'core'=2,'zl'=4] {'y','x'}, dimensions={0} | all-to-all | bytes 655360 | tf_op jit(solution)/shard_map/all_to_all | solution.py:208
  86.9 7.5 %collective-permute-start.6 = (bf16[40,256]{1,0:T(8,128)(2,1)S(1)}, bf16[40,256]{1,0:T(8,128)(2,1)S(1)}, u32[]{:S(2)}, u32[]{:S(2)}) collective-permute-start(bf16[40,256]{1,0:T(8,128)(2,1)S(1)} %reduce_sum.12), channel_id=1, source_target_pairs={{0,32},{32,0},{64,96},{96,64},{1,33},{33,1},{65,97},{97,65},{2,34}... | collective-permute-start | bytes 61448 | tf_op jit(solution)/shard_map/ppermute | solution.py:39
  94.4 1.3 collective-permute-done.6
  95.7 9.1 %collective-permute-start.7 = (bf16[40,256]{1,0:T(8,128)(2,1)S(1)}, bf16[40,256]{1,0:T(8,128)(2,1)S(1)}, u32[]{:S(2)}, u32[]{:S(2)}) collective-permute-start(bf16[40,256]{1,0:T(8,128)(2,1)S(1)} %add_convert_fusion), channel_id=1, source_target_pairs={{0,96},{96,0},{32,64},{64,32},{1,97},{97,1},{33,65},{65,33},{2,98}... | collective-permute-start | bytes 61448 | tf_op jit(solution)/shard_map/ppermute | solution.py:39
  104.8 1.8 %collective-permute-done.7 = bf16[40,256]{1,0:T(8,128)(2,1)S(1)} collective-permute-done((bf16[40,256]{1,0:T(8,128)(2,1)S(1)}, bf16[40,256]{1,0:T(8,128)(2,1)S(1)}, u32[]{:S(2)}, u32[]{:S(2)}) %collective-permute-start.7) | collective-permute-done | bytes 20512 | tf_op jit(solution)/shard_map/ppermute | solution.py:39
  107.5 7.7 %all-to-all-start.2 = ((bf16[32,40,256]{2,1,0:T(8,128)(2,1)}), bf16[32,40,256]{2,1,0:T(8,128)(2,1)}, u32[]{:S(2)}, u32[]{:S(2)}) async-start(bf16[32,40,256]{2,1,0:T(8,128)(2,1)} %broadcast_in_dim.15), calls=%async_computation.2 | async-start | bytes 1310720 | tf_op jit(solution)/shard_map/all_to_all | solution.py:22
  115.2 3.4 %shard_map.98 = bf16[256,640]{1,0:T(8,128)(2,1)} custom-call(s32[1]{0:T(128)} %bitcast.3.core_ref, bf16[256,2560]{1,0:T(8,128)(2,1)S(1)} %copy-done.3, bf16[640,1280]{1,0:T(8,128)(2,1)S(1)} %copy-done.2, bf16[640,1280]{1,0:T(8,128)(2,1)} %collective-permute-done.2.other_ref), custom_call_target="tpu_custom_call" | custom-call | flops 838860800 | bytes 5000000 | tf_op jit(solution)/shard_map/pallas_call | solution.py:91
  118.6 9.1 %all-to-all-done.2 = bf16[32,40,256]{2,1,0:T(8,128)(2,1)} async-done(((bf16[32,40,256]{2,1,0:T(8,128)(2,1)}), bf16[32,40,256]{2,1,0:T(8,128)(2,1)}, u32[]{:S(2)}, u32[]{:S(2)}) %all-to-all-start.2) | async-done | bytes 655392 | tf_op jit(solution)/shard_map/all_to_all | solution.py:22
  127.6 1.1 copy-done.5
  128.7 1.1 copy-done.11
  129.8 1.1 copy-done.12
  130.9 4.1 %shard_map.99 = bf16[640,1280]{1,0:T(8,128)(2,1)} custom-call(s32[1]{0:T(128)} %bitcast.3.core_ref, bf16[2,640,256]{2,1,0:T(8,128)(2,1)} %bitcast.8.rows_ref, bf16[640,640]{1,0:T(8,128)(2,1)S(1)} %copy-done.12, bf16[1280,256]{1,0:T(8,128)(2,1)S(1)} %copy-done.5, bf16[1280,256]{1,0:T(8,128)(2,1)S(1)} %copy-done.11), custom_call_target="tpu_custom_call" | custom-call | flops 1258291200 | bytes 5000000 | tf_op jit(solution)/shard_map/pallas_call | solution.py:158
  (50 shorter events, 4.9 us)
Async XLA Ops:
  7.2 0.8 copy-start
  7.2 53.9 %all-gather.2.cloned.1.call-start = ((), (), s32[]{:S(2)}) async-start(), calls=%async_computation.4 | async-start | bytes 1638400 | tf_op jit(solution)/shard_map/all_gather | solution.py:176
  8.7 12.6 %collective-permute-start = (bf16[60,256]{1,0:T(8,128)(2,1)S(1)}, bf16[60,256]{1,0:T(8,128)(2,1)S(1)}, u32[]{:S(2)}, u32[]{:S(2)}) collective-permute-start(bf16[60,256]{1,0:T(8,128)(2,1)S(1)} %pad_maximum_fusion.2), channel_id=1, source_target_pairs={{0,32},{32,0},{64,96},{96,64},{1,33},{33,1},{65,97},{97,65},{2,34}... | collective-permute-start | bytes 92168 | tf_op jit(solution)/shard_map/ppermute | solution.py:27
  18.4 33.2 %collective-permute-start.2 = (bf16[640,1280]{1,0:T(8,128)(2,1)}, bf16[640,1280]{1,0:T(8,128)(2,1)}, u32[]{:S(2)}, u32[]{:S(2)}) collective-permute-start(bf16[640,1280]{1,0:T(8,128)(2,1)} %own_ref.3), channel_id=1, source_target_pairs={{0,4},{4,0},{1,5},{5,1},{2,6},{6,2},{3,7},{7,3},{8,12},{12,8},{9,1... | collective-permute-start | bytes 4915208 | tf_op jit(solution)/shard_map/ppermute | solution.py:177
  21.4 11.2 %collective-permute-start.1 = (bf16[120,256]{1,0:T(8,128)(2,1)S(1)}, bf16[120,256]{1,0:T(8,128)(2,1)S(1)}, u32[]{:S(2)}, u32[]{:S(2)}) collective-permute-start(bf16[120,256]{1,0:T(8,128)(2,1)S(1)} %pad_maximum_fusion.1), channel_id=1, source_target_pairs={{0,96},{96,0},{32,64},{64,32},{1,97},{97,1},{33,65},{65,33},{2,98}... | collective-permute-start | bytes 184328 | tf_op jit(solution)/shard_map/ppermute | solution.py:30
  33.9 7.0 %copy-start.6 = (bf16[256,640]{1,0:T(8,128)(2,1)S(1)}, bf16[256,640]{1,0:T(8,128)(2,1)}, u32[]{:S(2)}) copy-start(bf16[256,640]{1,0:T(8,128)(2,1)} %x_ref.3) | copy-start | bytes 983044
  33.9 23.3 %all-to-all-start = ((bf16[16,160,256]{2,1,0:T(8,128)(2,1)}), bf16[16,160,256]{2,1,0:T(8,128)(2,1)}, u32[]{:S(2)}, u32[]{:S(2)}) async-start(bf16[16,160,256]{2,1,0:T(8,128)(2,1)} %broadcast_in_dim.14), calls=%async_computation | async-start | bytes 2621440 | tf_op jit(solution)/shard_map/all_to_all | solution.py:22
  40.8 10.8 %copy-start.7 = (bf16[256,640]{1,0:T(8,128)(2,1)S(1)}, bf16[256,640]{1,0:T(8,128)(2,1)}, u32[]{:S(2)}) copy-start(bf16[256,640]{1,0:T(8,128)(2,1)} %x_ref.3) | copy-start | bytes 983044
  40.9 86.8 %reduce-scatter.2.cloned.1.call-start = ((), (), s32[]{:S(2)}) async-start(), calls=%async_computation.5 | async-start | bytes 1638400 | tf_op jit(solution)/shard_map/reduce_scatter | solution.py:194
  40.9 7.2 %collective-permute-start.3 = (bf16[256,640]{1,0:T(8,128)(2,1)S(1)}, bf16[256,640]{1,0:T(8,128)(2,1)S(1)}, u32[]{:S(2)}, u32[]{:S(2)}) collective-permute-start(bf16[256,640]{1,0:T(8,128)(2,1)S(1)} %copy-done.6), channel_id=1, source_target_pairs={{0,4},{4,0},{1,5},{5,1},{2,6},{6,2},{3,7},{7,3},{8,12},{12,8},{9,1... | collective-permute-start | bytes 983048 | tf_op jit(solution)/shard_map/ppermute | solution.py:178
  48.1 0.7 copy-start.13
  51.6 1.4 %copy-start.1 = (bf16[640,1280]{1,0:T(8,128)(2,1)S(1)}, bf16[640,1280]{1,0:T(8,128)(2,1)}, u32[]{:S(2)}) copy-start(bf16[640,1280]{1,0:T(8,128)(2,1)} %own_ref.3) | copy-start | bytes 4915204
  55.7 1.1 copy-start.4
  58.7 10.7 %copy-start.8 = (bf16[256,640]{1,0:T(8,128)(2,1)S(1)}, bf16[256,640]{1,0:T(8,128)(2,1)}, u32[]{:S(2)}) copy-start(bf16[256,640]{1,0:T(8,128)(2,1)} %get-tuple-element.27.x_ref) | copy-start | bytes 983044
  61.0 8.4 %copy-start.3 = (bf16[256,2560]{1,0:T(8,128)(2,1)S(1)}, bf16[256,2560]{1,0:T(8,128)(2,1)}, u32[]{:S(2)}) copy-start(bf16[256,2560]{1,0:T(8,128)(2,1)} %all-gather.2.cloned.1.call-done.grad_ref) | copy-start | bytes 3932164
  61.0 11.6 %collective-permute-start.4 = (bf16[256,2560]{1,0:T(8,128)(2,1)}, bf16[256,2560]{1,0:T(8,128)(2,1)}, u32[]{:S(2)}, u32[]{:S(2)}) collective-permute-start(bf16[256,2560]{1,0:T(8,128)(2,1)} %all-gather.2.cloned.1.call-done.grad_ref), channel_id=1, source_target_pairs={{0,4},{4,0},{1,5},{5,1},{2,6},{6,2},{3,7},{7,3},{8,12},{12,8},{9,1... | collective-permute-start | bytes 3932168 | tf_op jit(solution)/shard_map/ppermute | solution.py:203
  67.4 5.2 %copy-start.9 = (bf16[256,640]{1,0:T(8,128)(2,1)S(1)}, bf16[256,640]{1,0:T(8,128)(2,1)}, u32[]{:S(2)}) copy-start(bf16[256,640]{1,0:T(8,128)(2,1)} %get-tuple-element.25.x_ref) | copy-start | bytes 983044
  67.4 4.3 %collective-permute-start.5 = (bf16[1280,256]{1,0:T(8,128)(2,1)}, bf16[1280,256]{1,0:T(8,128)(2,1)S(1)}, u32[]{:S(2)}, u32[]{:S(2)}) collective-permute-start(bf16[1280,256]{1,0:T(8,128)(2,1)} %get-tuple-element.28), channel_id=1, source_target_pairs={{0,4},{4,0},{1,5},{5,1},{2,6},{6,2},{3,7},{7,3},{8,12},{12,8},{9,1... | collective-permute-start | bytes 1966088 | tf_op jit(solution)/shard_map/ppermute | solution.py:201
  71.7 0.9 copy-start.10
  86.8 28.3 %copy-start.2 = (bf16[640,1280]{1,0:T(8,128)(2,1)S(1)}, bf16[640,1280]{1,0:T(8,128)(2,1)}, u32[]{:S(2)}) copy-start(bf16[640,1280]{1,0:T(8,128)(2,1)} %own_ref.3) | copy-start | bytes 4915204
  86.9 8.8 %collective-permute-start.6 = (bf16[40,256]{1,0:T(8,128)(2,1)S(1)}, bf16[40,256]{1,0:T(8,128)(2,1)S(1)}, u32[]{:S(2)}, u32[]{:S(2)}) collective-permute-start(bf16[40,256]{1,0:T(8,128)(2,1)S(1)} %reduce_sum.12), channel_id=1, source_target_pairs={{0,32},{32,0},{64,96},{96,64},{1,33},{33,1},{65,97},{97,65},{2,34}... | collective-permute-start | bytes 61448 | tf_op jit(solution)/shard_map/ppermute | solution.py:39
  95.7 10.9 %collective-permute-start.7 = (bf16[40,256]{1,0:T(8,128)(2,1)S(1)}, bf16[40,256]{1,0:T(8,128)(2,1)S(1)}, u32[]{:S(2)}, u32[]{:S(2)}) collective-permute-start(bf16[40,256]{1,0:T(8,128)(2,1)S(1)} %add_convert_fusion), channel_id=1, source_target_pairs={{0,96},{96,0},{32,64},{64,32},{1,97},{97,1},{33,65},{65,33},{2,98}... | collective-permute-start | bytes 61448 | tf_op jit(solution)/shard_map/ppermute | solution.py:39
  107.5 20.1 %all-to-all-start.2 = ((bf16[32,40,256]{2,1,0:T(8,128)(2,1)}), bf16[32,40,256]{2,1,0:T(8,128)(2,1)}, u32[]{:S(2)}, u32[]{:S(2)}) async-start(bf16[32,40,256]{2,1,0:T(8,128)(2,1)} %broadcast_in_dim.15), calls=%async_computation.2 | async-start | bytes 1310720 | tf_op jit(solution)/shard_map/all_to_all | solution.py:22
  127.6 1.1 copy-start.5
  128.7 1.1 copy-start.11
  129.8 1.1 copy-start.12
Sparse Core Ops, SparseCore 0:
  18.5 42.4 all-gather.1
  67.5 39.2 reduce-scatter.1

commit v11 on v9

--- a/solution.py
+++ b/solution.py
@@ -151,11 +151,12 @@
 
 
 def update_kernel(
-    place_ref, own_hbm, other_hbm, basis_hbm, basis_other_hbm, out_hbm,
-    rows_ref, basis_ref, out_ref, sems, out_sems,
+    own_hbm, other_hbm, order_hbm, basis_hbm, basis_other_hbm, out_hbm,
+    rows_ref, order_ref, basis_ref, out_ref, sems, out_sems,
 ):
     copies = fetch(
         [
+            (order_hbm, order_ref),
             (own_hbm, rows_ref.at[0]),
             (other_hbm, rows_ref.at[1]),
             (basis_hbm, basis_ref.at[0]),
@@ -163,15 +164,14 @@
         ],
         sems,
     )
-    natural = lax.broadcasted_iota(jnp.int32, (640, 640), 0)
-    order = jnp.where(natural == place_ref[...], 1.0, 0.0).astype(BF16)
+    copies[0].wait()
     directions = []
     for which in range(2):
-        copies[which].wait()
-        moved = jnp.dot(order, rows_ref[which], preferred_element_type=F32)
+        copies[1 + which].wait()
+        moved = jnp.dot(order_ref[...], rows_ref[which], preferred_element_type=F32)
         directions.append(moved.astype(BF16))
-    copies[2].wait()
     copies[3].wait()
+    copies[4].wait()
     leaving = []
     for block in range(out_ref.shape[0]):
         cols = slice(256 * block, 256 * (block + 1))
@@ -192,23 +192,24 @@
         copy.wait()
 
 
-def update_matmul(place, rows, rows_other, basis, basis_other):
+def update_matmul(rows, rows_other, order, basis, basis_other):
     half = basis.shape[0]
     return pl.pallas_call(
         update_kernel,
         out_shape=jax.ShapeDtypeStruct((640, half), BF16),
-        in_specs=[pl.BlockSpec()] + [FAR] * 4,
+        in_specs=[FAR] * 5,
         out_specs=FAR,
         scratch_shapes=[
             pltpu.VMEM((2, 640, 256), BF16),
+            pltpu.VMEM((640, 640), BF16),
             pltpu.VMEM((2, half, 256), BF16),
             pltpu.VMEM((half // 256, 640, 256), BF16),
-            pltpu.SemaphoreType.DMA((4,)),
+            pltpu.SemaphoreType.DMA((5,)),
             pltpu.SemaphoreType.DMA((half // 256,)),
         ],
         compiler_params=ALL,
         cost_estimate=cost(2 * 640 * 512 * (640 + half), 5_000_000),
-    )(place, rows, rows_other, basis, basis_other)
+    )(rows, rows_other, order, basis, basis_other)
 
 
 def shards(x_heads, proj_weight, out_grad, proj_basis, first_moment, second_moment):
@@ -265,8 +266,7 @@
     rows, head_rows, mixed_out = lax.optimization_barrier((rows, head_rows, mixed_out))
     rows_other = lax.ppermute(rows, "core", CORE_SWAP)
 
-    place = jnp.asarray(ORDER.argmax(0).reshape(1, 640), jnp.int32)
-    update = update_matmul(place, rows, rows_other, basis_own, basis_other)
+    update = update_matmul(rows, rows_other, order, basis_own, basis_other)
     return (mixed_out, head_rows, update)
 
 

time: 138 us -> 137 us (level)
  no operation moved by 1% of the time
where the time goes in v11:
time: 137 us
  starting transfers between devices  69.1 us (50%)
  Pallas kernels  16.1 us (12%)
  waiting for transfers between devices  14.5 us (11%)
  between operations  14.4 us (11%)
  blocking collectives  12 us (9%)
  local copies, waits for them, and re-layouts  10.3 us (8%)
    ppermute x2, starting transfers between devices, sum_zh(): values = sent.astype(F32) + lax.ppermute(sent, 'zh', partners).astype(F32)  16.5 us
    all_to_all x1, blocking collectives, shards(): lax.all_to_all(low_chip.reshape(16, 40, 256), ('y', 'x'), 0, 0, tiled=True)  12 us
    all_to_all x2, starting transfers between devices, spread(): return lax.all_to_all(copies, axes, 0, 0, tiled=True)  10.5 us
    ppermute x1, starting transfers between devices, gather_zh(): got = lax.ppermute(values, 'zh', PAIR)  9.65 us
    ppermute x1, starting transfers between devices, gather_zh(): got = lax.ppermute(pair, 'zh', MIRROR)  9.28 us
    ppermute x1, starting transfers between devices, shards(): rows_other = lax.ppermute(rows, 'core', CORE_SWAP)  6.4 us
    ppermute x1, starting transfers between devices, shards(): x_other = lax.ppermute(x_heads, 'core', CORE_SWAP)  5.94 us
    ppermute x1, starting transfers between devices, shards(): grad_other = lax.ppermute(grad_block, 'core', CORE_SWAP)  5.93 us
  transfers between devices with their start and end apart: 13, of which 8 were waited for; matrix products, arithmetic and copies ran while one was open for 3% of the time, Pallas kernels for 9%

profile of v11, /device:TPU:1, one launch (start us, length us, event | category | flops | bytes accessed | tf_op | source)
XLA Modules:
  0.0 136.5 jit_solution(15996432804051703492)
XLA Ops:
  8.7 9.6 %collective-permute-start = (bf16[60,256]{1,0:T(8,128)(2,1)S(1)}, bf16[60,256]{1,0:T(8,128)(2,1)S(1)}, u32[]{:S(2)}, u32[]{:S(2)}) collective-permute-start(bf16[60,256]{1,0:T(8,128)(2,1)S(1)} %pad_maximum_fusion.2), channel_id=1, source_target_pairs={{0,32},{32,0},{64,96},{96,64},{1,33},{33,1},{65,97},{97,65},{2,34}... | collective-permute-start | bytes 92168 | tf_op jit(solution)/shard_map/ppermute | solution.py:27
  18.4 2.9 %collective-permute-start.2 = (bf16[640,1280]{1,0:T(8,128)(2,1)}, bf16[640,1280]{1,0:T(8,128)(2,1)}, u32[]{:S(2)}, u32[]{:S(2)}) collective-permute-start(bf16[640,1280]{1,0:T(8,128)(2,1)} %own_ref.3), channel_id=1, source_target_pairs={{0,4},{4,0},{1,5},{5,1},{2,6},{6,2},{3,7},{7,3},{8,12},{12,8},{9,1... | collective-permute-start | bytes 4915208 | tf_op jit(solution)/shard_map/ppermute | solution.py:224
  21.4 9.3 %collective-permute-start.1 = (bf16[120,256]{1,0:T(8,128)(2,1)S(1)}, bf16[120,256]{1,0:T(8,128)(2,1)S(1)}, u32[]{:S(2)}, u32[]{:S(2)}) collective-permute-start(bf16[120,256]{1,0:T(8,128)(2,1)S(1)} %pad_maximum_fusion.1), channel_id=1, source_target_pairs={{0,96},{96,0},{32,64},{64,32},{1,97},{97,1},{33,65},{65,33},{2,98}... | collective-permute-start | bytes 184328 | tf_op jit(solution)/shard_map/ppermute | solution.py:30
  30.6 1.9 %collective-permute-done.1 = bf16[120,256]{1,0:T(8,128)(2,1)S(1)} collective-permute-done((bf16[120,256]{1,0:T(8,128)(2,1)S(1)}, bf16[120,256]{1,0:T(8,128)(2,1)S(1)}, u32[]{:S(2)}, u32[]{:S(2)}) %collective-permute-start.1) | collective-permute-done | bytes 61472 | tf_op jit(solution)/shard_map/ppermute | solution.py:30
  32.6 1.3 broadcast_in_dim.14
  33.9 6.9 %all-to-all-start = ((bf16[16,160,256]{2,1,0:T(8,128)(2,1)}), bf16[16,160,256]{2,1,0:T(8,128)(2,1)}, u32[]{:S(2)}, u32[]{:S(2)}) async-start(bf16[16,160,256]{2,1,0:T(8,128)(2,1)} %broadcast_in_dim.14), calls=%async_computation | async-start | bytes 2621440 | tf_op jit(solution)/shard_map/all_to_all | solution.py:22
  40.9 5.9 %collective-permute-start.3 = (bf16[256,640]{1,0:T(8,128)(2,1)S(1)}, bf16[256,640]{1,0:T(8,128)(2,1)}, u32[]{:S(2)}, u32[]{:S(2)}) collective-permute-start(bf16[256,640]{1,0:T(8,128)(2,1)S(1)} %copy-done.5), channel_id=1, source_target_pairs={{0,4},{4,0},{1,5},{5,1},{2,6},{6,2},{3,7},{7,3},{8,12},{12,8},{9,1... | collective-permute-start | bytes 983048 | tf_op jit(solution)/shard_map/ppermute | solution.py:225
  46.9 1.3 collective-permute-done.3.xo_ref
  48.2 2.8 %shard_map.95 = (bf16[256,640]{1,0:T(8,128)(2,1)}, bf16[256,640]{1,0:T(8,128)(2,1)}) custom-call(bf16[640,640]{1,0:T(8,128)(2,1)} %constant.57.clone.order_ref.order_hbm, bf16[256,640]{1,0:T(8,128)(2,1)} %x_ref.3, bf16[256,640]{1,0:T(8,128)(2,1)} %collective-permute-done.3.xo_ref), custom_call_target="tpu_custom_call" | custom-call | flops 419430400 | bytes 2200000 | tf_op jit(solution)/shard_map/pallas_call | solution.py:112
  51.0 1.4 %copy-done.1 = bf16[640,1280]{1,0:T(8,128)(2,1)S(1)} copy-done((bf16[640,1280]{1,0:T(8,128)(2,1)S(1)}, bf16[640,1280]{1,0:T(8,128)(2,1)}, u32[]{:S(2)}) %copy-start.1) | copy-done | bytes 1638424
  52.5 3.7 %shard_map.94 = bf16[256,2560]{1,0:T(8,128)(2,1)} custom-call(s32[1]{0:T(128)} %bitcast.3.core_ref, bf16[256,640]{1,0:T(8,128)(2,1)S(1)} %copy-done.6, bf16[640,1280]{1,0:T(8,128)(2,1)S(1)} %copy-done.1, bf16[640,1280]{1,0:T(8,128)(2,1)} %collective-permute-done.2.other_ref), custom_call_target="tpu_custom_call" | custom-call | flops 838860800 | bytes 5000000 | tf_op jit(solution)/shard_map/pallas_call | solution.py:67
  56.2 1.1 all-to-all-done
  57.2 1.4 %copy.10 = bf16[4,4,4,40,256]{4,3,2,1,0:T(8,128)(2,1)S(1)} copy(bf16[4,4,4,40,256]{4,3,1,2,0:T(8,128)(2,1)} %bitcast.5) | data formatting | bytes 2621440 | tf_op jit(solution)/shard_map/transpose | solution.py:239
  58.7 0.9 constant_dynamic-slice_fusion
  59.7 1.4 all-gather.2.cloned.1.call-done.grad_ref
  61.0 5.9 %collective-permute-start.4 = (bf16[256,2560]{1,0:T(8,128)(2,1)}, bf16[256,2560]{1,0:T(8,128)(2,1)S(1)}, u32[]{:S(2)}, u32[]{:S(2)}) collective-permute-start(bf16[256,2560]{1,0:T(8,128)(2,1)} %all-gather.2.cloned.1.call-done.grad_ref), channel_id=1, source_target_pairs={{0,4},{4,0},{1,5},{5,1},{2,6},{6,2},{3,7},{7,3},{8,12},{12,8},{9,1... | collective-permute-start | bytes 3932168 | tf_op jit(solution)/shard_map/ppermute | solution.py:250
  67.0 1.9 %collective-permute-start.5 = (bf16[1280,256]{1,0:T(8,128)(2,1)S(1)}, bf16[1280,256]{1,0:T(8,128)(2,1)S(1)}, u32[]{:S(2)}, u32[]{:S(2)}) collective-permute-start(bf16[1280,256]{1,0:T(8,128)(2,1)S(1)} %get-tuple-element.28), channel_id=1, source_target_pairs={{0,4},{4,0},{1,5},{5,1},{2,6},{6,2},{3,7},{7,3},{8,12},{12,8},{9,1... | collective-permute-start | bytes 1966088 | tf_op jit(solution)/shard_map/ppermute | solution.py:248
  68.9 1.3 copy-done.3
  70.2 0.9 shard_map.96.refs_0_
  71.2 0.8 copy-done.10
  72.0 0.9 shard_map.97
  72.9 12.0 %all_to_all.15 = bf16[16,40,256]{2,1,0:T(8,128)(2,1)S(1)} all-to-all(bf16[16,40,256]{2,1,0:T(8,128)(2,1)S(1)} %bitcast.21), channel_id=1, replica_groups=mesh['y'=4,'zh'=4,'x'=4,'core'=2,'zl'=4] {'y','x'}, dimensions={0} | all-to-all | bytes 655360 | tf_op jit(solution)/shard_map/all_to_all | solution.py:255
  85.0 7.4 %collective-permute-start.6 = (bf16[40,256]{1,0:T(8,128)(2,1)S(1)}, bf16[40,256]{1,0:T(8,128)(2,1)S(1)}, u32[]{:S(2)}, u32[]{:S(2)}) collective-permute-start(bf16[40,256]{1,0:T(8,128)(2,1)S(1)} %reduce_sum.12), channel_id=1, source_target_pairs={{0,32},{32,0},{64,96},{96,64},{1,33},{33,1},{65,97},{97,65},{2,34}... | collective-permute-start | bytes 61448 | tf_op jit(solution)/shard_map/ppermute | solution.py:39
  92.3 1.3 collective-permute-done.6
  93.7 9.2 %collective-permute-start.7 = (bf16[40,256]{1,0:T(8,128)(2,1)S(1)}, bf16[40,256]{1,0:T(8,128)(2,1)S(1)}, u32[]{:S(2)}, u32[]{:S(2)}) collective-permute-start(bf16[40,256]{1,0:T(8,128)(2,1)S(1)} %add_convert_fusion), channel_id=1, source_target_pairs={{0,96},{96,0},{32,64},{64,32},{1,97},{97,1},{33,65},{65,33},{2,98}... | collective-permute-start | bytes 61448 | tf_op jit(solution)/shard_map/ppermute | solution.py:39
  102.8 1.8 %collective-permute-done.7 = bf16[40,256]{1,0:T(8,128)(2,1)S(1)} collective-permute-done((bf16[40,256]{1,0:T(8,128)(2,1)S(1)}, bf16[40,256]{1,0:T(8,128)(2,1)S(1)}, u32[]{:S(2)}, u32[]{:S(2)}) %collective-permute-start.7) | collective-permute-done | bytes 20512 | tf_op jit(solution)/shard_map/ppermute | solution.py:39
  105.4 3.5 %all-to-all-start.2 = ((bf16[16,40,256]{2,1,0:T(8,128)(2,1)}), bf16[16,40,256]{2,1,0:T(8,128)(2,1)S(1)}, u32[]{:S(2)}, u32[]{:S(2)}) async-start(bf16[16,40,256]{2,1,0:T(8,128)(2,1)} %broadcast_in_dim.15), calls=%async_computation.2 | async-start | bytes 655360 | tf_op jit(solution)/shard_map/all_to_all | solution.py:22
  109.0 3.4 %shard_map.98 = bf16[256,640]{1,0:T(8,128)(2,1)} custom-call(s32[1]{0:T(128)} %bitcast.3.core_ref, bf16[256,2560]{1,0:T(8,128)(2,1)S(1)} %copy-done.4, bf16[640,1280]{1,0:T(8,128)(2,1)S(1)} %copy-done.2, bf16[640,1280]{1,0:T(8,128)(2,1)} %collective-permute-done.2.other_ref), custom_call_target="tpu_custom_call" | custom-call | flops 838860800 | bytes 5000000 | tf_op jit(solution)/shard_map/pallas_call | solution.py:93
  112.3 4.6 %all-to-all-done.2 = bf16[16,40,256]{2,1,0:T(8,128)(2,1)S(1)} async-done(((bf16[16,40,256]{2,1,0:T(8,128)(2,1)}), bf16[16,40,256]{2,1,0:T(8,128)(2,1)S(1)}, u32[]{:S(2)}, u32[]{:S(2)}) %all-to-all-start.2) | async-done | bytes 327712 | tf_op jit(solution)/shard_map/all_to_all | solution.py:22
  116.9 6.4 %collective-permute-start.8 = (bf16[640,256]{1,0:T(8,128)(2,1)S(1)}, bf16[640,256]{1,0:T(8,128)(2,1)S(1)}, u32[]{:S(2)}, u32[]{:S(2)}) collective-permute-start(bf16[640,256]{1,0:T(8,128)(2,1)S(1)} %bitcast.22), channel_id=1, source_target_pairs={{0,4},{4,0},{1,5},{5,1},{2,6},{6,2},{3,7},{7,3},{8,12},{12,8},{9,1... | collective-permute-start | bytes 983048 | tf_op jit(solution)/shard_map/ppermute | solution.py:267
  123.3 1.2 collective-permute-done.8.other_hbm
  125.3 4.4 %shard_map.99 = bf16[640,1280]{1,0:T(8,128)(2,1)} custom-call(bf16[640,256]{1,0:T(8,128)(2,1)} %bitcast.23, bf16[640,256]{1,0:T(8,128)(2,1)} %copy-done.11, bf16[640,640]{1,0:T(8,128)(2,1)} %constant.57.clone.order_ref.order_hbm, bf16[1280,256]{1,0:T(8,128)(2,1)} %get-tuple-element.35.basis_hbm, bf16[1280,256]{1,0:T(8,128)(2,1)} %copy-done.10), custom_call_target="tpu_custom_call" | custom-call | flops 1258291200 | bytes 5000000 | tf_op jit(solution)/shard_map/pallas_call | solution.py:197
  (48 shorter events, 3.4 us)
Async XLA Ops:
  7.2 0.8 copy-start
  7.2 53.9 %all-gather.2.cloned.1.call-start = ((), (), s32[]{:S(2)}) async-start(), calls=%async_computation.4 | async-start | bytes 1638400 | tf_op jit(solution)/shard_map/all_gather | solution.py:223
  8.7 12.6 %collective-permute-start = (bf16[60,256]{1,0:T(8,128)(2,1)S(1)}, bf16[60,256]{1,0:T(8,128)(2,1)S(1)}, u32[]{:S(2)}, u32[]{:S(2)}) collective-permute-start(bf16[60,256]{1,0:T(8,128)(2,1)S(1)} %pad_maximum_fusion.2), channel_id=1, source_target_pairs={{0,32},{32,0},{64,96},{96,64},{1,33},{33,1},{65,97},{97,65},{2,34}... | collective-permute-start | bytes 92168 | tf_op jit(solution)/shard_map/ppermute | solution.py:27
  18.4 32.6 %collective-permute-start.2 = (bf16[640,1280]{1,0:T(8,128)(2,1)}, bf16[640,1280]{1,0:T(8,128)(2,1)}, u32[]{:S(2)}, u32[]{:S(2)}) collective-permute-start(bf16[640,1280]{1,0:T(8,128)(2,1)} %own_ref.3), channel_id=1, source_target_pairs={{0,4},{4,0},{1,5},{5,1},{2,6},{6,2},{3,7},{7,3},{8,12},{12,8},{9,1... | collective-permute-start | bytes 4915208 | tf_op jit(solution)/shard_map/ppermute | solution.py:224
  21.4 11.2 %collective-permute-start.1 = (bf16[120,256]{1,0:T(8,128)(2,1)S(1)}, bf16[120,256]{1,0:T(8,128)(2,1)S(1)}, u32[]{:S(2)}, u32[]{:S(2)}) collective-permute-start(bf16[120,256]{1,0:T(8,128)(2,1)S(1)} %pad_maximum_fusion.1), channel_id=1, source_target_pairs={{0,96},{96,0},{32,64},{64,32},{1,97},{97,1},{33,65},{65,33},{2,98}... | collective-permute-start | bytes 184328 | tf_op jit(solution)/shard_map/ppermute | solution.py:30
  33.9 7.0 %copy-start.5 = (bf16[256,640]{1,0:T(8,128)(2,1)S(1)}, bf16[256,640]{1,0:T(8,128)(2,1)}, u32[]{:S(2)}) copy-start(bf16[256,640]{1,0:T(8,128)(2,1)} %x_ref.3) | copy-start | bytes 983044
  33.9 23.3 %all-to-all-start = ((bf16[16,160,256]{2,1,0:T(8,128)(2,1)}), bf16[16,160,256]{2,1,0:T(8,128)(2,1)}, u32[]{:S(2)}, u32[]{:S(2)}) async-start(bf16[16,160,256]{2,1,0:T(8,128)(2,1)} %broadcast_in_dim.14), calls=%async_computation | async-start | bytes 2621440 | tf_op jit(solution)/shard_map/all_to_all | solution.py:22
  40.8 10.2 %copy-start.6 = (bf16[256,640]{1,0:T(8,128)(2,1)S(1)}, bf16[256,640]{1,0:T(8,128)(2,1)}, u32[]{:S(2)}) copy-start(bf16[256,640]{1,0:T(8,128)(2,1)} %x_ref.3) | copy-start | bytes 983044
  40.9 76.1 %reduce-scatter.2.cloned.1.call-start = ((), (), s32[]{:S(2)}) async-start(), calls=%async_computation.5 | async-start | bytes 1638400 | tf_op jit(solution)/shard_map/reduce_scatter | solution.py:241
  40.9 7.3 %collective-permute-start.3 = (bf16[256,640]{1,0:T(8,128)(2,1)S(1)}, bf16[256,640]{1,0:T(8,128)(2,1)}, u32[]{:S(2)}, u32[]{:S(2)}) collective-permute-start(bf16[256,640]{1,0:T(8,128)(2,1)S(1)} %copy-done.5), channel_id=1, source_target_pairs={{0,4},{4,0},{1,5},{5,1},{2,6},{6,2},{3,7},{7,3},{8,12},{12,8},{9,1... | collective-permute-start | bytes 983048 | tf_op jit(solution)/shard_map/ppermute | solution.py:225
  51.0 1.4 %copy-start.1 = (bf16[640,1280]{1,0:T(8,128)(2,1)S(1)}, bf16[640,1280]{1,0:T(8,128)(2,1)}, u32[]{:S(2)}) copy-start(bf16[640,1280]{1,0:T(8,128)(2,1)} %own_ref.3) | copy-start | bytes 4915204
  58.7 10.2 %copy-start.7 = (bf16[256,640]{1,0:T(8,128)(2,1)S(1)}, bf16[256,640]{1,0:T(8,128)(2,1)}, u32[]{:S(2)}) copy-start(bf16[256,640]{1,0:T(8,128)(2,1)} %get-tuple-element.27.x_ref) | copy-start | bytes 983044
  61.0 11.0 %collective-permute-start.4 = (bf16[256,2560]{1,0:T(8,128)(2,1)}, bf16[256,2560]{1,0:T(8,128)(2,1)S(1)}, u32[]{:S(2)}, u32[]{:S(2)}) collective-permute-start(bf16[256,2560]{1,0:T(8,128)(2,1)} %all-gather.2.cloned.1.call-done.grad_ref), channel_id=1, source_target_pairs={{0,4},{4,0},{1,5},{5,1},{2,6},{6,2},{3,7},{7,3},{8,12},{12,8},{9,1... | collective-permute-start | bytes 3932168 | tf_op jit(solution)/shard_map/ppermute | solution.py:250
  67.0 4.2 %collective-permute-start.5 = (bf16[1280,256]{1,0:T(8,128)(2,1)S(1)}, bf16[1280,256]{1,0:T(8,128)(2,1)S(1)}, u32[]{:S(2)}, u32[]{:S(2)}) collective-permute-start(bf16[1280,256]{1,0:T(8,128)(2,1)S(1)} %get-tuple-element.28), channel_id=1, source_target_pairs={{0,4},{4,0},{1,5},{5,1},{2,6},{6,2},{3,7},{7,3},{8,12},{12,8},{9,1... | collective-permute-start | bytes 1966088 | tf_op jit(solution)/shard_map/ppermute | solution.py:248
  68.9 1.3 copy-start.3
  70.2 1.8 %copy-start.8 = (bf16[256,640]{1,0:T(8,128)(2,1)S(1)}, bf16[256,640]{1,0:T(8,128)(2,1)}, u32[]{:S(2)}) copy-start(bf16[256,640]{1,0:T(8,128)(2,1)} %get-tuple-element.25.x_ref) | copy-start | bytes 983044
  71.1 0.8 copy-start.10
  72.0 37.0 %copy-start.4 = (bf16[256,2560]{1,0:T(8,128)(2,1)S(1)}, bf16[256,2560]{1,0:T(8,128)(2,1)}, u32[]{:S(2)}) copy-start(bf16[256,2560]{1,0:T(8,128)(2,1)} %all-gather.2.cloned.1.call-done.grad_ref) | copy-start | bytes 3932164
  72.9 36.1 %copy-start.2 = (bf16[640,1280]{1,0:T(8,128)(2,1)S(1)}, bf16[640,1280]{1,0:T(8,128)(2,1)}, u32[]{:S(2)}) copy-start(bf16[640,1280]{1,0:T(8,128)(2,1)} %own_ref.3) | copy-start | bytes 4915204
  85.0 8.7 %collective-permute-start.6 = (bf16[40,256]{1,0:T(8,128)(2,1)S(1)}, bf16[40,256]{1,0:T(8,128)(2,1)S(1)}, u32[]{:S(2)}, u32[]{:S(2)}) collective-permute-start(bf16[40,256]{1,0:T(8,128)(2,1)S(1)} %reduce_sum.12), channel_id=1, source_target_pairs={{0,32},{32,0},{64,96},{96,64},{1,33},{33,1},{65,97},{97,65},{2,34}... | collective-permute-start | bytes 61448 | tf_op jit(solution)/shard_map/ppermute | solution.py:39
  93.7 10.9 %collective-permute-start.7 = (bf16[40,256]{1,0:T(8,128)(2,1)S(1)}, bf16[40,256]{1,0:T(8,128)(2,1)S(1)}, u32[]{:S(2)}, u32[]{:S(2)}) collective-permute-start(bf16[40,256]{1,0:T(8,128)(2,1)S(1)} %add_convert_fusion), channel_id=1, source_target_pairs={{0,96},{96,0},{32,64},{64,32},{1,97},{97,1},{33,65},{65,33},{2,98}... | collective-permute-start | bytes 61448 | tf_op jit(solution)/shard_map/ppermute | solution.py:39
  105.4 11.5 %all-to-all-start.2 = ((bf16[16,40,256]{2,1,0:T(8,128)(2,1)}), bf16[16,40,256]{2,1,0:T(8,128)(2,1)S(1)}, u32[]{:S(2)}, u32[]{:S(2)}) async-start(bf16[16,40,256]{2,1,0:T(8,128)(2,1)} %broadcast_in_dim.15), calls=%async_computation.2 | async-start | bytes 655360 | tf_op jit(solution)/shard_map/all_to_all | solution.py:22
  116.9 7.7 %copy-start.9 = (bf16[16,40,256]{2,1,0:T(8,128)(2,1)}, bf16[16,40,256]{2,1,0:T(8,128)(2,1)S(1)}, u32[]{:S(2)}) copy-start(bf16[16,40,256]{2,1,0:T(8,128)(2,1)S(1)} %all-to-all-done.2) | copy-start | bytes 983044
  116.9 7.6 %collective-permute-start.8 = (bf16[640,256]{1,0:T(8,128)(2,1)S(1)}, bf16[640,256]{1,0:T(8,128)(2,1)S(1)}, u32[]{:S(2)}, u32[]{:S(2)}) collective-permute-start(bf16[640,256]{1,0:T(8,128)(2,1)S(1)} %bitcast.22), channel_id=1, source_target_pairs={{0,4},{4,0},{1,5},{5,1},{2,6},{6,2},{3,7},{7,3},{8,12},{12,8},{9,1... | collective-permute-start | bytes 983048 | tf_op jit(solution)/shard_map/ppermute | solution.py:267
  124.6 0.7 copy-start.11
Sparse Core Ops, SparseCore 0:
  18.5 42.4 all-gather.1
  64.4 42.4 reduce-scatter.1
